TPU v7x, 32 devices: a whole 2x2x4 slice. The times are simulated.
32 devices in a mesh: groups: 2 (over y), px: 8 (over z, x), py: 2 (over core).
Axes of the slice: x: 2, y: 2, z: 4, core: 2. Of those that a mesh axis runs over, the one named last changes fastest.
Arguments:
- velocity: float32 [3, 16, 128, 128], P(None, ('groups', 'px'), 'py'), parts along dimension 1, may hold values from -6 to 6
- cotangent: float32 [3, 16, 128, 128], P(None, ('groups', 'px'), 'py'), parts along dimension 1, may hold values from -6 to 6
- first_kernel: float32 [16, 3, 3, 3, 3], replicated, may hold values from -0.625 to 0.625
- first_bias: float32 [16], replicated, may hold values from -3 to 3
- second_kernel: float32 [6, 16, 3, 3, 3], replicated, may hold values from -0.3125 to 0.3125
- second_bias: float32 [6], replicated, may hold values from -4 to 4
Outputs:
- grad_velocity: float32 [3, 16, 128, 128], P(None, ('groups', 'px'), 'py'), parts along dimension 1
- grad_first_kernel: float32 [32, 3, 3, 3, 3], P('groups'), parts along dimension 0
- grad_first_bias: float32 [32], P('groups'), parts along dimension 0
- grad_second_kernel: float32 [12, 16, 3, 3, 3], P('groups'), parts along dimension 0
- grad_second_bias: float32 [12], P('groups'), parts along dimension 0
There are 2 independent parts, one for each index of `groups`. A program takes and returns all parts, laid end to end along the dimension named above; an argument that names none is the same for every part. Nothing has to cross between parts.
All inputs are finite; a program needn't handle non-finite values.
Results may differ from a plain program's by a relative error of at most 0.0003.
Values sent between devices are 32-bit elements; how exact they have to be, the bound alone decides.
No kernel may reach another device: no remote copies, remote signals or barrier semaphores. Data moves between devices by JAX's collectives and lax.ppermute only.
A program may use at most 128 MiB of HBM per device.

v0:
```python
import math

import jax
import jax.numpy as jnp
from jax import lax
from jax.sharding import PartitionSpec as P

ITERS = 2


KAPPA = 0.25


def padded_2(value, sides, width):
    for axis, dim in sides:
        size, length = (lax.axis_size(axis), value.shape[dim])
        up = [(i, (i + 1) % size) for i in range(size)]
        down = [(j, i) for i, j in up]
        last = lax.slice_in_dim(value, length - width, length, axis=dim)
        initial = lax.slice_in_dim(value, 0, width, axis=dim)
        before = lax.ppermute(last, axis, up)
        after = lax.ppermute(initial, axis, down)
        value = jnp.concatenate([before, value, after], axis=dim)
    return value


def extend(field):
    rimmed = padded_2(field, (("px", 1), ("py", 2)), 1)
    return jnp.concatenate([rimmed[..., -1:], rimmed, rimmed[..., :1]], axis=3)


def across_columns(spectrum):
    return lax.all_to_all(spectrum, "px", split_axis=2, concat_axis=4, tiled=True)


def across_pairs(spectrum):
    return lax.all_to_all(spectrum, "py", split_axis=3, concat_axis=4, tiled=True)


def summed(grads):
    return lax.psum((grads[0], grads[1], grads[2], grads[3]), ("px", "py"))


def all_taps():
    return [
        (shift_x, shift_y, shift_z)
        for shift_x in range(3)
        for shift_y in range(3)
        for shift_z in range(3)
    ]


def gather_conv(padded, kernel):
    size_x = padded.shape[1] - 2
    size_y = padded.shape[2] - 2
    size_z = padded.shape[3] - 2
    stacked = jnp.concatenate(
        [
            padded[:, sx_one : sx_one + size_x, sy_one : sy_one + size_y, sz_one : sz_one + size_z]
            for sx_one, sy_one, sz_one in all_taps()
        ],
        axis=0,
    )
    matrix = jnp.transpose(kernel, (0, 2, 3, 4, 1)).reshape(kernel.shape[0], -1)
    result = jnp.einsum("ok,kxyz->oxyz", matrix, stacked, precision=lax.Precision.HIGHEST)
    return (result, stacked)


def scatter_conv(padded, kernel):
    outputs = kernel.shape[0]
    inputs = kernel.shape[1]
    size_x = padded.shape[1] - 2
    size_y = padded.shape[2] - 2
    size_z = padded.shape[3] - 2
    total = jnp.zeros((outputs, size_x, size_y, size_z), jnp.float32)
    for shift_x in range(3):
        matrix = jnp.transpose(kernel[:, :, shift_x], (0, 2, 3, 1)).reshape(outputs * 9, inputs)
        layer = jnp.einsum(
            "km,mxyz->kxyz",
            matrix,
            padded[:, shift_x : shift_x + size_x],
            precision=lax.Precision.HIGHEST,
        )
        layer = layer.reshape(outputs, 3, 3, size_x, size_y + 2, size_z + 2)
        for shift_y in range(3):
            for shift_z in range(3):
                total = (
                    total
                    + layer[
                        :,
                        shift_y,
                        shift_z,
                        :,
                        shift_y : shift_y + size_y,
                        shift_z : shift_z + size_z,
                    ]
                )
    return total


def flipped(kernel):
    return jnp.transpose(kernel[:, :, ::-1, ::-1, ::-1], (1, 0, 2, 3, 4))


def moved(padded, axis_dim, offset_cells):
    index = [slice(None), slice(1, -1), slice(1, -1), slice(1, -1)]
    index[axis_dim] = slice(1 + offset_cells, padded.shape[axis_dim] - 1 + offset_cells)
    return padded[tuple(index)]


def advect(padded, weights):
    center = moved(padded, 1, 0)
    total = jnp.zeros_like(center)
    for direction in range(3):
        ahead = moved(padded, direction + 1, 1)
        behind = moved(padded, direction + 1, -1)
        vplus = 0.5 * (center[direction] + ahead[direction])
        vminus = 0.5 * (behind[direction] + center[direction])
        upper = center + weights[2 * direction] * (ahead - center)
        lower = center + weights[2 * direction + 1] * (behind - center)
        total = total + vplus * upper - vminus * lower
    return total


def advect_back(padded, weights_pad, source_pad):
    center = moved(padded, 1, 0)
    source = moved(source_pad, 1, 0)
    weights = moved(weights_pad, 1, 0)
    grad_field = jnp.zeros_like(center)
    fluxes = []
    parts = []
    for direction in range(3):
        ahead = moved(padded, direction + 1, 1)
        behind = moved(padded, direction + 1, -1)
        vplus = 0.5 * (center[direction] + ahead[direction])
        vminus = 0.5 * (behind[direction] + center[direction])
        rate_up = weights[2 * direction]
        rate_low = weights[2 * direction + 1]
        rate_before = moved(weights_pad[2 * direction : 2 * direction + 1], direction + 1, -1)[0]
        rate_after = moved(weights_pad[2 * direction + 1 : 2 * direction + 2], direction + 1, 1)[0]
        source_before = moved(source_pad, direction + 1, -1)
        source_after = moved(source_pad, direction + 1, 1)
        upper = center + rate_up * (ahead - center)
        lower = center + rate_low * (behind - center)
        upper_before = behind + rate_before * (center - behind)
        lower_after = ahead + rate_after * (center - ahead)
        grad_field = grad_field + source * (vplus * (1.0 - rate_up) - vminus * (1.0 - rate_low))
        grad_field = (
            grad_field + vminus * rate_before * source_before - vplus * rate_after * source_after
        )
        fluxes.append(
            0.5
            * (
                jnp.sum(source * upper, 0)
                - jnp.sum(source * lower, 0)
                + jnp.sum(source_before * upper_before, 0)
                - jnp.sum(source_after * lower_after, 0)
            )
        )
        parts.append(jnp.sum(source * vplus * (ahead - center), 0))
        parts.append(-jnp.sum(source * vminus * (behind - center), 0))
    return (grad_field + jnp.stack(fluxes), jnp.stack(parts))


def tables(count):
    index = jnp.arange(count, dtype=jnp.int32)
    phase = index[:, None] * index[None, :] % count
    angle = phase.astype(jnp.float32) * (2.0 * math.pi / count)
    return (jnp.cos(angle), jnp.sin(angle))


def mix(form, data, table):
    return jnp.einsum(form, data, table, precision=lax.Precision.HIGHEST)


def waves(start, count, total):
    index = start + jnp.arange(count, dtype=jnp.int32)
    return jnp.where(index < total // 2, index, index - total).astype(jnp.float32)


def project(field):
    depth = field.shape[3]
    cos_z, sin_z = tables(depth)
    real_z = mix("cxyz,zk->cxky", field, cos_z)
    imag_z = -mix("cxyz,zk->cxky", field, sin_z)
    spectrum = across_pairs(jnp.stack([real_z, imag_z]))
    span_y = spectrum.shape[4]
    cos_y, sin_y = tables(span_y)
    real_y = mix("cxky,yq->cqkx", spectrum[0], cos_y) + mix("cxky,yq->cqkx", spectrum[1], sin_y)
    imag_y = mix("cxky,yq->cqkx", spectrum[1], cos_y) - mix("cxky,yq->cqkx", spectrum[0], sin_y)
    spectrum = across_columns(jnp.stack([real_y, imag_y]))
    span_x = spectrum.shape[4]
    cos_x, sin_x = tables(span_x)
    real_x = mix("cqkx,xp->cqkp", spectrum[0], cos_x) + mix("cqkx,xp->cqkp", spectrum[1], sin_x)
    imag_x = mix("cqkx,xp->cqkp", spectrum[1], cos_x) - mix("cqkx,xp->cqkp", spectrum[0], sin_x)
    rows_y = spectrum.shape[2]
    rows_z = spectrum.shape[3]
    wave_y = waves(lax.axis_index("px") * rows_y, rows_y, span_y)[:, None, None]
    wave_z = waves(lax.axis_index("py") * rows_z, rows_z, depth)[None, :, None]
    wave_x = waves(0, span_x, span_x)[None, None, :]
    size = jnp.maximum(wave_x * wave_x + wave_y * wave_y + wave_z * wave_z, 1.0)
    vectors = jnp.stack(jnp.broadcast_arrays(wave_x, wave_y, wave_z))
    real_x = real_x - vectors * (
        (wave_x * real_x[0] + wave_y * real_x[1] + wave_z * real_x[2]) / size
    )
    imag_x = imag_x - vectors * (
        (wave_x * imag_x[0] + wave_y * imag_x[1] + wave_z * imag_x[2]) / size
    )
    back_real = (mix("cqkp,px->cxkq", real_x, cos_x) - mix("cqkp,px->cxkq", imag_x, sin_x)) / span_x
    back_imag = (mix("cqkp,px->cxkq", imag_x, cos_x) + mix("cqkp,px->cxkq", real_x, sin_x)) / span_x
    spectrum = across_columns(jnp.stack([back_real, back_imag]))
    rows_real = (
        mix("cxkq,qy->cxyk", spectrum[0], cos_y) - mix("cxkq,qy->cxyk", spectrum[1], sin_y)
    ) / span_y
    rows_imag = (
        mix("cxkq,qy->cxyk", spectrum[1], cos_y) + mix("cxkq,qy->cxyk", spectrum[0], sin_y)
    ) / span_y
    spectrum = across_pairs(jnp.stack([rows_real, rows_imag]))
    return (
        mix("cxyk,kz->cxyz", spectrum[0], cos_z) - mix("cxyk,kz->cxyz", spectrum[1], sin_z)
    ) / depth


def forward_state(field, first_kernel, first_bias, second_kernel, second_bias):
    padded = extend(field)
    first_out, field_taps = gather_conv(padded, first_kernel)
    hidden = jnp.tanh(first_out + first_bias[:, None, None, None])
    weights = jax.nn.sigmoid(
        scatter_conv(extend(hidden), second_kernel) + second_bias[:, None, None, None]
    )
    return (padded, hidden, weights, field_taps)


def backward_step(state, upstream, first_kernel, second_kernel):
    padded, hidden, weights, field_taps = state
    moved_grad = project(upstream)
    source = -KAPPA * moved_grad
    stacked = extend(jnp.concatenate([source, weights], axis=0))
    grad_field, grad_weights = advect_back(padded, stacked[3:], stacked[:3])
    grad_field = grad_field + moved_grad
    grad_logits = grad_weights * weights * (1.0 - weights)
    logits_pad = extend(grad_logits)
    grad_hidden, logit_taps = gather_conv(logits_pad, flipped(second_kernel))
    product = jnp.einsum("kxyz,mxyz->km", logit_taps, hidden, precision=lax.Precision.HIGHEST)
    product = product.reshape(3, 3, 3, second_kernel.shape[0], second_kernel.shape[1])
    grad_second = jnp.transpose(product[::-1, ::-1, ::-1], (3, 4, 0, 1, 2))
    grad_second_bias = jnp.sum(grad_logits, axis=(1, 2, 3))
    grad_pre = grad_hidden * (1.0 - hidden * hidden)
    pre_pad = extend(grad_pre)
    grad_field = grad_field + scatter_conv(pre_pad, flipped(first_kernel))
    first_product = jnp.einsum(
        "oxyz,kxyz->ok", grad_pre, field_taps, precision=lax.Precision.HIGHEST
    )
    first_product = first_product.reshape(first_kernel.shape[0], 3, 3, 3, first_kernel.shape[1])
    grad_first = jnp.transpose(first_product, (0, 4, 1, 2, 3))
    grad_first_bias = jnp.sum(grad_pre, axis=(1, 2, 3))
    return (grad_field, (grad_first, grad_first_bias, grad_second, grad_second_bias))


def on_device(velocity, cotangent, first_kernel, first_bias, second_kernel, second_bias):
    field = velocity
    fields = [velocity]
    saved = []
    for section in range(ITERS):
        state = forward_state(field, first_kernel, first_bias, second_kernel, second_bias)
        saved.append(state)
        field = project(field - KAPPA * advect(state[0], state[2]))
        fields.append(field)
    upstream = cotangent
    totals = None
    for section in reversed(range(ITERS)):
        state = saved[section]
        upstream, grads = backward_step(state, upstream, first_kernel, second_kernel)
        grads = summed(grads)
        if totals is None:
            totals = grads
        else:
            totals = tuple((older + newer for older, newer in zip(totals, grads)))
    return (upstream, totals[0], totals[1], totals[2], totals[3])


def solution(mesh):
    return jax.shard_map(
        on_device,
        mesh=mesh,
        in_specs=(
            P(None, ("groups", "px"), "py", None),
            P(None, ("groups", "px"), "py", None),
            P(),
            P(),
            P(),
            P(),
        ),
        out_specs=(
            P(None, ("groups", "px"), "py", None),
            P("groups", None, None, None, None),
            P("groups"),
            P("groups", None, None, None, None),
            P("groups"),
        ),
        check_vma=False,
    )
```

profile of v0, /device:TPU:0, one launch (start us, length us, event | category | flops | bytes accessed | tf_op | source)
XLA Modules:
  0.0 712.6 jit_solution(291719841912391532)
XLA Ops:
  30.7 4.7 collective-permute-start.5
  38.3 18.0 %collective-permute-done.5 = f32[16,1,64,128]{3,0,2,1:T(8,128)S(1)} collective-permute-done((f32[16,1,64,128]{3,0,2,1:T(8,128)S(1)}, f32[16,1,64,128]{3,0,2,1:T(8,128)S(1)}, u32[]{:S(2)}, u32[]{:S(2)}) %collective-permute-start.5) | collective-permute-done | bytes 524320 | tf_op jit(solution)/shard_map/ppermute | solution.py:22
  140.4 6.2 all-to-all-start.5
  147.4 7.5 %all-to-all-done.5 = f32[8,1,6144]{2,1,0:T(1,128)S(1)} async-done(((f32[8,1,6144]{2,1,0:T(1,128)}), f32[8,1,6144]{2,1,0:T(1,128)S(1)}, u32[]{:S(2)}, u32[]{:S(2)}) %all-to-all-start.5) | async-done | bytes 196640 | tf_op jit(solution)/shard_map/all_to_all | solution.py:33
  167.2 5.2 all-to-all-done.6
  215.7 20.9 %collective-permute-done.13 = f32[16,1,64,128]{3,0,2,1:T(8,128)S(1)} collective-permute-done((f32[16,1,64,128]{3,0,2,1:T(8,128)S(1)}, f32[16,1,64,128]{3,0,2,1:T(8,128)S(1)}, u32[]{:S(2)}, u32[]{:S(2)}) %collective-permute-start.13) | collective-permute-done | bytes 524320 | tf_op jit(solution)/shard_map/ppermute | solution.py:22
  271.6 4.7 convolution_bitcast_fusion
  293.7 4.3 convolution_bitcast_fusion.2
  322.0 12.0 %collective-permute-done.17 = f32[9,1,64,128]{3,2,1,0:T(8,128)S(1)} collective-permute-done((f32[9,1,64,128]{3,2,1,0:T(8,128)S(1)}, f32[9,1,64,128]{3,2,1,0:T(8,128)S(1)}, u32[]{:S(2)}, u32[]{:S(2)}) %collective-permute-start.17) | collective-permute-done | bytes 294944 | tf_op jit(solution)/shard_map/ppermute | solution.py:22
  346.4 9.6 %collective-permute-done.21 = f32[6,1,64,128]{3,2,0,1:T(8,128)S(1)} collective-permute-done((f32[6,1,64,128]{3,2,0,1:T(8,128)S(1)}, f32[6,1,64,128]{3,2,0,1:T(8,128)S(1)}, u32[]{:S(2)}, u32[]{:S(2)}) %collective-permute-start.21) | collective-permute-done | bytes 196640 | tf_op jit(solution)/shard_map/ppermute | solution.py:22
  359.8 6.7 fusion.701
  376.6 15.4 %collective-permute-done.25 = f32[16,1,64,128]{3,0,2,1:T(8,128)S(1)} collective-permute-done((f32[16,1,64,128]{3,0,2,1:T(8,128)S(1)}, f32[16,1,64,128]{3,0,2,1:T(8,128)S(1)}, u32[]{:S(2)}, u32[]{:S(2)}) %collective-permute-start.25) | collective-permute-done | bytes 524320 | tf_op jit(solution)/shard_map/ppermute | solution.py:22
  479.9 4.4 all-to-all-start.9
  485.6 7.0 all-to-all-done.9
  503.0 6.4 all-to-all-done.10
  523.3 14.9 %fusion.52 = f32[3,3,3,6,16]{4,3,2,1,0:T(8,128)S(1)} fusion(f32[3,3,3,6,64,128]{5,4,3,2,1,0:T(8,128)} %bitcast.1477, f32[64,128,16]{1,2,0:T(8,128)S(1)} %fusion.25), kind=kOutput, calls=%fused_computation.72 | convolution fusion | flops 254803968 | bytes 5843072 | tf_op jit(solution)/shard_map/kxyz,mxyz->km/dot_general | solution.py:244
  538.8 6.3 fusion.80
  552.5 4.4 collective-permute-start.33
  561.3 5.3 collective-permute-done.32
  570.6 6.1 fusion.702
  579.0 6.4 fusion.89
  585.4 11.4 %fusion.55 = f32[3,3,3,6,16]{4,3,2,1,0:T(8,128)S(1)} fusion(f32[3,3,3,6,64,128]{5,4,3,2,1,0:T(8,128)S(1)} %bitcast.1479, f32[64,128,16]{1,2,0:T(8,128)S(1)} %fusion.19), kind=kOutput, calls=%fused_computation.73 | convolution fusion | flops 254803968 | bytes 5843072 | tf_op jit(solution)/shard_map/kxyz,mxyz->km/dot_general | solution.py:244
  596.8 5.4 collective-permute-done.37
  602.9 61.0 %all-reduce = (f32[16,3,3,3,3]{0,1,4,3,2:T(4,128)S(1)}, f32[16]{0:T(128)}, f32[6,16,3,3,3]{1,0,4,3,2:T(8,128)S(1)}, f32[6]{0:T(128)}) all-reduce(f32[16,3,3,3,3]{0,1,4,3,2:T(4,128)S(1)} %fusion.89, f32[16]{0:T(128)S(1)} %add.2437, ...), channel_id=1, replica_groups=mesh['groups'=2,'px'=8,'py'=2] {'px','py'}, use_global_device_ids=true, to_apply=%region_36.37 | all-reduce | flops 3910 | bytes 31280 | tf_op jit(solution)/shard_map/psum | solution.py:41
  (841 shorter events, 453.4 us)
Async XLA Ops:
  0.6 23.0 %collective-permute-start.1 = (f32[3,1,64,128]{3,2,0,1:T(8,128)}, f32[3,1,64,128]{3,2,0,1:T(8,128)S(1)}, u32[]{:S(2)}, u32[]{:S(2)}) collective-permute-start(f32[3,1,64,128]{3,2,0,1:T(8,128)} %bitcast.1509), channel_id=1, source_target_pairs={{0,2},{2,4},{4,6},{6,8},{8,10},{10,12},{12,14},{14,0},{1,3},{3,5},... | collective-permute-start | bytes 294920 | tf_op jit(solution)/shard_map/ppermute | solution.py:21
  3.6 20.0 %collective-permute-start = (f32[3,1,64,128]{3,2,0,1:T(8,128)}, f32[3,1,64,128]{3,2,0,1:T(8,128)S(1)}, u32[]{:S(2)}, u32[]{:S(2)}) collective-permute-start(f32[3,1,64,128]{3,2,0,1:T(8,128)} %bitcast.1510), channel_id=1, source_target_pairs={{2,0},{4,2},{6,4},{8,6},{10,8},{12,10},{14,12},{0,14},{3,1},{5,3},... | collective-permute-start | bytes 294920 | tf_op jit(solution)/shard_map/ppermute | solution.py:22
  18.6 17.7 %all-to-all-start.1 = ((f32[8,1,6144]{2,1,0:T(1,128)}), f32[8,1,6144]{2,1,0:T(1,128)S(1)}, u32[]{:S(2)}, u32[]{:S(2)}) async-start(f32[8,1,6144]{2,1,0:T(1,128)} %reshape.3150), calls=%async_computation.1 | async-start | bytes 393216 | tf_op jit(solution)/shard_map/all_to_all | solution.py:33
  30.7 25.6 %collective-permute-start.5 = (f32[16,1,64,128]{3,0,2,1:T(8,128)S(1)}, f32[16,1,64,128]{3,0,2,1:T(8,128)S(1)}, u32[]{:S(2)}, u32[]{:S(2)}) collective-permute-start(f32[16,1,64,128]{3,0,2,1:T(8,128)S(1)} %bitcast.1489), channel_id=1, source_target_pairs={{2,0},{4,2},{6,4},{8,6},{10,8},{12,10},{14,12},{0,14},{3,1},{5,3},... | collective-permute-start | bytes 1572872 | tf_op jit(solution)/shard_map/ppermute | solution.py:22
  35.4 21.1 %collective-permute-start.4 = (f32[16,1,64,128]{3,0,2,1:T(8,128)S(1)}, f32[16,1,64,128]{3,0,2,1:T(8,128)S(1)}, u32[]{:S(2)}, u32[]{:S(2)}) collective-permute-start(f32[16,1,64,128]{3,0,2,1:T(8,128)S(1)} %bitcast.1490), channel_id=1, source_target_pairs={{0,2},{2,4},{4,6},{6,8},{8,10},{10,12},{12,14},{14,0},{1,3},{3,5},... | collective-permute-start | bytes 1572872 | tf_op jit(solution)/shard_map/ppermute | solution.py:21
  140.4 14.4 %all-to-all-start.5 = ((f32[8,1,6144]{2,1,0:T(1,128)}), f32[8,1,6144]{2,1,0:T(1,128)S(1)}, u32[]{:S(2)}, u32[]{:S(2)}) async-start(f32[8,1,6144]{2,1,0:T(1,128)} %reshape.3158), calls=%async_computation.5 | async-start | bytes 393216 | tf_op jit(solution)/shard_map/all_to_all | solution.py:33
  160.9 11.5 %all-to-all-start.6 = ((f32[8,1,6144]{2,1,0:T(1,128)}), f32[8,1,6144]{2,1,0:T(1,128)S(1)}, u32[]{:S(2)}, u32[]{:S(2)}) async-start(f32[8,1,6144]{2,1,0:T(1,128)} %reshape.3160), calls=%async_computation.6 | async-start | bytes 393216 | tf_op jit(solution)/shard_map/all_to_all | solution.py:33
  180.6 12.0 %all-to-all-start.2 = ((f32[8,1,6144]{2,1,0:T(1,128)}), f32[8,1,6144]{2,1,0:T(1,128)S(1)}, u32[]{:S(2)}, u32[]{:S(2)}) async-start(f32[8,1,6144]{2,1,0:T(1,128)} %reshape.3152), calls=%async_computation.2 | async-start | bytes 393216 | tf_op jit(solution)/shard_map/all_to_all | solution.py:33
  187.3 15.7 %collective-permute-start.9 = (f32[3,1,64,128]{3,2,1,0:T(8,128)S(1)}, f32[3,1,64,128]{3,2,1,0:T(8,128)S(1)}, u32[]{:S(2)}, u32[]{:S(2)}) collective-permute-start(f32[3,1,64,128]{3,2,1,0:T(8,128)S(1)} %bitcast.1517), channel_id=1, source_target_pairs={{0,2},{2,4},{4,6},{6,8},{8,10},{10,12},{12,14},{14,0},{1,3},{3,5},... | collective-permute-start | bytes 294920 | tf_op jit(solution)/shard_map/ppermute | solution.py:21
  189.2 13.7 %collective-permute-start.8 = (f32[3,1,64,128]{3,2,1,0:T(8,128)S(1)}, f32[3,1,64,128]{3,2,1,0:T(8,128)S(1)}, u32[]{:S(2)}, u32[]{:S(2)}) collective-permute-start(f32[3,1,64,128]{3,2,1,0:T(8,128)S(1)} %bitcast.1518), channel_id=1, source_target_pairs={{2,0},{4,2},{6,4},{8,6},{10,8},{12,10},{14,12},{0,14},{3,1},{5,3},... | collective-permute-start | bytes 294920 | tf_op jit(solution)/shard_map/ppermute | solution.py:22
  209.9 26.7 %collective-permute-start.13 = (f32[16,1,64,128]{3,0,2,1:T(8,128)S(1)}, f32[16,1,64,128]{3,0,2,1:T(8,128)S(1)}, u32[]{:S(2)}, u32[]{:S(2)}) collective-permute-start(f32[16,1,64,128]{3,0,2,1:T(8,128)S(1)} %bitcast.1494), channel_id=1, source_target_pairs={{2,0},{4,2},{6,4},{8,6},{10,8},{12,10},{14,12},{0,14},{3,1},{5,3},... | collective-permute-start | bytes 1572872 | tf_op jit(solution)/shard_map/ppermute | solution.py:22
  211.7 24.9 %collective-permute-start.12 = (f32[16,1,64,128]{3,0,2,1:T(8,128)S(1)}, f32[16,1,64,128]{3,0,2,1:T(8,128)S(1)}, u32[]{:S(2)}, u32[]{:S(2)}) collective-permute-start(f32[16,1,64,128]{3,0,2,1:T(8,128)S(1)} %bitcast.1495), channel_id=1, source_target_pairs={{0,2},{2,4},{4,6},{6,8},{8,10},{10,12},{12,14},{14,0},{1,3},{3,5},... | collective-permute-start | bytes 1572872 | tf_op jit(solution)/shard_map/ppermute | solution.py:21
  318.4 15.6 %collective-permute-start.17 = (f32[9,1,64,128]{3,2,1,0:T(8,128)S(1)}, f32[9,1,64,128]{3,2,1,0:T(8,128)S(1)}, u32[]{:S(2)}, u32[]{:S(2)}) collective-permute-start(f32[9,1,64,128]{3,2,1,0:T(8,128)S(1)} %pad_maximum_fusion.23), channel_id=1, source_target_pairs={{2,0},{4,2},{6,4},{8,6},{10,8},{12,10},{14,12},{0,14},{3,1},{5,3},... | collective-permute-start | bytes 884744 | tf_op jit(solution)/shard_map/ppermute | solution.py:22
  319.7 14.3 %collective-permute-start.16 = (f32[9,1,64,128]{3,2,1,0:T(8,128)S(1)}, f32[9,1,64,128]{3,2,1,0:T(8,128)S(1)}, u32[]{:S(2)}, u32[]{:S(2)}) collective-permute-start(f32[9,1,64,128]{3,2,1,0:T(8,128)S(1)} %pad_maximum_fusion.23), channel_id=1, source_target_pairs={{0,2},{2,4},{4,6},{6,8},{8,10},{10,12},{12,14},{14,0},{1,3},{3,5},... | collective-permute-start | bytes 884744 | tf_op jit(solution)/shard_map/ppermute | solution.py:21
  344.4 11.6 %collective-permute-start.21 = (f32[6,1,64,128]{3,2,0,1:T(8,128)S(1)}, f32[6,1,64,128]{3,2,0,1:T(8,128)S(1)}, u32[]{:S(2)}, u32[]{:S(2)}) collective-permute-start(f32[6,1,64,128]{3,2,0,1:T(8,128)S(1)} %get-tuple-element.83), channel_id=1, source_target_pairs={{2,0},{4,2},{6,4},{8,6},{10,8},{12,10},{14,12},{0,14},{3,1},{5,3},... | collective-permute-start | bytes 589832 | tf_op jit(solution)/shard_map/ppermute | solution.py:22
  366.6 25.4 %collective-permute-start.25 = (f32[16,1,64,128]{3,0,2,1:T(8,128)S(1)}, f32[16,1,64,128]{3,0,2,1:T(8,128)S(1)}, u32[]{:S(2)}, u32[]{:S(2)}) collective-permute-start(f32[16,1,64,128]{3,0,2,1:T(8,128)S(1)} %bitcast.1525), channel_id=1, source_target_pairs={{2,0},{4,2},{6,4},{8,6},{10,8},{12,10},{14,12},{0,14},{3,1},{5,3},... | collective-permute-start | bytes 1572872 | tf_op jit(solution)/shard_map/ppermute | solution.py:22
  368.2 23.8 %collective-permute-start.24 = (f32[16,1,64,128]{3,0,2,1:T(8,128)S(1)}, f32[16,1,64,128]{3,0,2,1:T(8,128)}, u32[]{:S(2)}, u32[]{:S(2)}) collective-permute-start(f32[16,1,64,128]{3,0,2,1:T(8,128)S(1)} %bitcast.1526), channel_id=1, source_target_pairs={{0,2},{2,4},{4,6},{6,8},{8,10},{10,12},{12,14},{14,0},{1,3},{3,5},... | collective-permute-start | bytes 1572872 | tf_op jit(solution)/shard_map/ppermute | solution.py:21
  479.9 12.6 %all-to-all-start.9 = ((f32[8,1,6144]{2,1,0:T(1,128)}), f32[8,1,6144]{2,1,0:T(1,128)S(1)}, u32[]{:S(2)}, u32[]{:S(2)}) async-start(f32[8,1,6144]{2,1,0:T(1,128)} %reshape.3166), calls=%async_computation.9 | async-start | bytes 393216 | tf_op jit(solution)/shard_map/all_to_all | solution.py:33
  521.0 17.2 %collective-permute-start.29 = (f32[9,1,64,128]{3,2,0,1:T(8,128)S(1)}, f32[9,1,64,128]{3,2,0,1:T(8,128)S(1)}, u32[]{:S(2)}, u32[]{:S(2)}) collective-permute-start(f32[9,1,64,128]{3,2,0,1:T(8,128)S(1)} %pad_maximum_fusion.24), channel_id=1, source_target_pairs={{2,0},{4,2},{6,4},{8,6},{10,8},{12,10},{14,12},{0,14},{3,1},{5,3},... | collective-permute-start | bytes 884744 | tf_op jit(solution)/shard_map/ppermute | solution.py:22
  522.7 15.5 %collective-permute-start.28 = (f32[9,1,64,128]{3,2,0,1:T(8,128)S(1)}, f32[9,1,64,128]{3,2,0,1:T(8,128)S(1)}, u32[]{:S(2)}, u32[]{:S(2)}) collective-permute-start(f32[9,1,64,128]{3,2,0,1:T(8,128)S(1)} %pad_maximum_fusion.24), channel_id=1, source_target_pairs={{0,2},{2,4},{4,6},{6,8},{8,10},{10,12},{12,14},{14,0},{1,3},{3,5},... | collective-permute-start | bytes 884744 | tf_op jit(solution)/shard_map/ppermute | solution.py:21
  576.8 25.5 %collective-permute-start.37 = (f32[16,1,64,128]{3,0,2,1:T(8,128)S(1)}, f32[16,1,64,128]{3,0,2,1:T(8,128)S(1)}, u32[]{:S(2)}, u32[]{:S(2)}) collective-permute-start(f32[16,1,64,128]{3,0,2,1:T(8,128)S(1)} %bitcast.1530), channel_id=1, source_target_pairs={{2,0},{4,2},{6,4},{8,6},{10,8},{12,10},{14,12},{0,14},{3,1},{5,3},... | collective-permute-start | bytes 1572872 | tf_op jit(solution)/shard_map/ppermute | solution.py:22
  578.7 23.5 %collective-permute-start.36 = (f32[16,1,64,128]{3,0,2,1:T(8,128)S(1)}, f32[16,1,64,128]{3,0,2,1:T(8,128)S(1)}, u32[]{:S(2)}, u32[]{:S(2)}) collective-permute-start(f32[16,1,64,128]{3,0,2,1:T(8,128)S(1)} %bitcast.1531), channel_id=1, source_target_pairs={{0,2},{2,4},{4,6},{6,8},{8,10},{10,12},{12,14},{14,0},{1,3},{3,5},... | collective-permute-start | bytes 1572872 | tf_op jit(solution)/shard_map/ppermute | solution.py:21
  602.2 62.9 %collective-permute-start.38 = (f32[16,3,1,128]{3,0,2,1:T(8,128)S(1)}, f32[16,3,1,128]{3,0,2,1:T(8,128)S(1)}, u32[]{:S(2)}, u32[]{:S(2)}) collective-permute-start(f32[16,3,1,128]{3,0,2,1:T(8,128)S(1)} %get-tuple-element.251), channel_id=1, source_target_pairs={{0,1},{1,0},{2,3},{3,2},{4,5},{5,4},{6,7},{7,6},{8,9},{9,8},{10,11... | collective-permute-start | bytes 73736 | tf_op jit(solution)/shard_map/ppermute | solution.py:21
  602.3 62.8 %collective-permute-start.39 = (f32[16,3,1,128]{3,0,2,1:T(8,128)S(1)}, f32[16,3,1,128]{3,0,2,1:T(8,128)S(1)}, u32[]{:S(2)}, u32[]{:S(2)}) collective-permute-start(f32[16,3,1,128]{3,0,2,1:T(8,128)S(1)} %get-tuple-element.252), channel_id=1, source_target_pairs={{1,0},{0,1},{3,2},{2,3},{5,4},{4,5},{7,6},{6,7},{9,8},{8,9},{11,10... | collective-permute-start | bytes 73736 | tf_op jit(solution)/shard_map/ppermute | solution.py:22
  (127 other events, 1279.9 us)
where the time goes:
time: 725 us; the launch traced here: 713 us
  local copies, waits for them, and re-layouts  246 us (34%)
  matrix products  127 us (18%)
  waiting for transfers between devices  119 us (16%)
  blocking collectives  84.5 us (12%)
  other arithmetic  65.8 us (9%)
  starting transfers between devices  64.7 us (9%)
    unnamed x442, local copies, waits for them, and re-layouts  156 us
    ppermute x20, waiting for transfers between devices, padded_2(): after = lax.ppermute(initial, axis, down)  85 us
    psum x1, blocking collectives, summed(): return lax.psum((grads[0], grads[1], grads[2], grads[3]), ('px', 'py'))  61 us
    another operation x28, local copies, waits for them, and re-layouts  43 us
    dot_general x12, matrix products, scatter_conv(): jnp.einsum('km,mxyz->kxyz', matrix, padded[:, shift_x:shift_x + size_x],...  40.7 us
    ppermute x20, starting transfers between devices, padded_2(): after = lax.ppermute(initial, axis, down)  29.4 us
    dot_general x60, matrix products, mix(): return jnp.einsum(form, data, table, precision=lax.Precision.HIGHEST)  28.6 us
    all_to_all x6, waiting for transfers between devices, across_columns(): lax.all_to_all(spectrum, 'px', split_axis=2, concat_axis=4, tiled=True)  26.7 us
  transfers between devices with their start and end apart: 46, of which 24 were waited for; matrix products, arithmetic and copies ran while one was open for 13% of the time, Pallas kernels for 0%

commit v1 on v0

--- a/solution.py
+++ b/solution.py
@@ -1,8 +1,12 @@
+import functools
 import math
 
 import jax
 import jax.numpy as jnp
+import numpy as np
 from jax import lax
+from jax.experimental import pallas as pl
+from jax.experimental.pallas import tpu as pltpu
 from jax.sharding import PartitionSpec as P
 
 ITERS = 2
@@ -279,9 +283,658 @@
     return (upstream, totals[0], totals[1], totals[2], totals[3])
 
 
+SLAB = 8
+RIM = 2
+REACH = SLAB + 2 * RIM
+WIDE = SLAB + 2
+PLANES = 8
+DEPTH = 128
+ROWS = 128
+CHANNELS = 16
+COEFFS = 6
+BAND = 32
+HID = CHANNELS * WIDE
+LOG = COEFFS * SLAB
+STACK = 9 * 48
+FLAT = PLANES * DEPTH
+NN = ((1,), (0,))
+NT = ((1,), (1,))
+
+
+def real_basis(count):
+    half = count // 2
+    angle = 2.0 * np.pi * np.arange(count) / count
+    rows = [np.full(count, 1.0 / np.sqrt(count))]
+    rows += [np.sqrt(2.0 / count) * np.cos(k * angle) for k in range(1, half)]
+    rows += [np.cos(half * angle) / np.sqrt(count)]
+    rows += [np.sqrt(2.0 / count) * np.sin(k * angle) for k in range(1, half)]
+    return np.stack(rows)
+
+
+def halves(table):
+    high = table.astype(np.float32).astype(jnp.bfloat16)
+    low = (table - high.astype(np.float64)).astype(np.float32).astype(jnp.bfloat16)
+    return high, low
+
+
+def slab_of(device):
+    return (device % 2) * PLANES + device // 2
+
+
+@functools.cache
+def constants():
+    basis_x = real_basis(PLANES)
+    mode_x = np.stack([basis_x[(k // 2) + (PLANES // 2) * (k % 2)] for k in range(PLANES)])
+    basis_z = real_basis(DEPTH)
+    order = []
+    for group in range(4):
+        order += [16 * group + i for i in range(16)] + [64 + 16 * group + i for i in range(16)]
+    mode_z = basis_z[order]
+    basis_y = real_basis(ROWS)
+
+    def columns(device, offset, count):
+        return basis_y[:, (SLAB * slab_of(device) + offset + np.arange(count)) % ROWS]
+
+    def table(block, offset, count):
+        out = np.zeros((3, ROWS, 16, block))
+        for device in range(16):
+            for m in range(3):
+                out[m, :, device, m * count : (m + 1) * count] = columns(device, offset, count)
+        return out.reshape(3 * ROWS, 16 * block)
+
+    both_in = table(24, 0, 8)
+    both_out = table(40, -RIM, REACH).T
+    one_in = np.concatenate([table(24, -RIM, 6), table(24, -RIM + 6, 6)])
+    one_out = np.concatenate([table(16, 0, 4).T, table(16, 4, 4).T])
+
+    spread = np.zeros((2 * STACK, 96))
+    mask = np.zeros((3, 2 * STACK, HID))
+    for tap in range(9):
+        for o in range(COEFFS):
+            for q in range(SLAB):
+                row = tap * 48 + o * SLAB + q
+                spread[row, tap * COEFFS + o] = 1.0
+                for b in range(3):
+                    mask[b, row, np.arange(CHANNELS) * WIDE + q + b] = 1.0
+        for m in range(3):
+            for r in range(REACH):
+                row = STACK + tap * 48 + m * REACH + r
+                spread[row, 54 + tap * 3 + m] = 1.0
+                for b in range(3):
+                    if 0 <= r - b < WIDE:
+                        mask[b, row, np.arange(CHANNELS) * WIDE + r - b] = 1.0
+    lift = np.zeros((HID, 128))
+    lift[np.arange(HID), np.arange(HID) // WIDE] = 1.0
+    count = np.zeros((LOG, 128))
+    count[np.arange(LOG), 16 + np.arange(LOG) // SLAB] = 1.0
+    half = jnp.bfloat16
+    return dict(
+        mode_x=mode_x,
+        to_z=halves(mode_z.T),
+        from_z=halves(mode_z),
+        both_in=halves(both_in),
+        both_out=halves(both_out),
+        one_in=halves(one_in),
+        one_out=halves(one_out),
+        spread=spread.astype(half),
+        spread_t=np.ascontiguousarray(spread.T).astype(half),
+        mask=mask.astype(half),
+        mask_t=np.ascontiguousarray(mask.transpose(0, 2, 1)).astype(half),
+        lift=lift.astype(half),
+        lift_t=np.ascontiguousarray(lift[:, :CHANNELS].T).astype(half),
+        count=count.astype(half),
+    )
+
+
+def dot(left, right, dims=NN):
+    return lax.dot_general(left, right, (dims, ((), ())), preferred_element_type=jnp.float32)
+
+
+def split(value):
+    high = value.astype(jnp.bfloat16)
+    return high, (value - high.astype(jnp.float32)).astype(jnp.bfloat16)
+
+
+def dot3(left, right, dims=NN):
+    return dot(left[0], right[0], dims) + (dot(left[0], right[1], dims) + dot(left[1], right[0], dims))
+
+
+def turn(value, shift):
+    shift = shift % value.shape[-1]
+    return value if shift == 0 else pltpu.roll(value, shift, value.ndim - 1)
+
+
+def plane(x):
+    x = x % PLANES
+    return slice(x * DEPTH, (x + 1) * DEPTH)
+
+
+def call(kernel, outs, args, scratch=()):
+    single = not isinstance(outs, (list, tuple))
+    shapes = [outs] if single else outs
+    return pl.pallas_call(
+        kernel,
+        out_shape=outs,
+        in_specs=[pl.BlockSpec(memory_space=pltpu.VMEM)] * len(args),
+        out_specs=(
+            pl.BlockSpec(memory_space=pltpu.VMEM)
+            if single
+            else [pl.BlockSpec(memory_space=pltpu.VMEM)] * len(shapes)
+        ),
+        scratch_shapes=list(scratch),
+        compiler_params=pltpu.CompilerParams(vmem_limit_bytes=56 * 2**20),
+    )(*args)
+
+
+def shape(*dims, kind=jnp.float32):
+    return jax.ShapeDtypeStruct(dims, kind)
+
+
+def weights_kernel(taps, spread, spread_t, mask, mask_t, lift, lift_t, fwd2, fwd1, back2, back1):
+    parts = split(taps[...])
+    for half in range(2):
+        tall = jnp.zeros((2 * STACK, HID), jnp.float32)
+        wide = jnp.zeros((HID, 2 * STACK), jnp.float32)
+        for b in range(3):
+            block = parts[half][:, b * 16 : (b + 1) * 16]
+            rows = dot(spread[...], block).astype(jnp.bfloat16)
+            tall = tall + mask[b].astype(jnp.float32) * dot(rows, lift_t[...])
+            cols = dot(lift[:, :CHANNELS], block, NT).astype(jnp.bfloat16)
+            wide = wide + mask_t[b].astype(jnp.float32) * dot(cols, spread_t[...])
+        fwd2[half] = tall[:STACK].astype(jnp.bfloat16)
+        back1[half] = tall[STACK:].astype(jnp.bfloat16)
+        back2[half] = wide[:, :STACK].astype(jnp.bfloat16)
+        fwd1[half] = wide[:, STACK:].astype(jnp.bfloat16)
+
+
+def pack_kernel(field, cot, edges, out, ext):
+    for m in range(3):
+        ext[m, 6:8, :] = edges[m, 2:4, :]
+        ext[m, 8:72, :] = field[m, 0]
+        ext[m, 72:74, :] = edges[m, 0:2, :]
+    for q in range(PLANES):
+        for m in range(3):
+            out[q, m * REACH : (m + 1) * REACH, :] = ext[m, 8 * q + 6 : 8 * q + 18, :]
+            out[q, 36 + 8 * m : 44 + 8 * m, :] = cot[m, 0, 8 * q : 8 * q + 8, :]
+        out[q, 60:64, :] = jnp.zeros((4, DEPTH), jnp.float32)
+
+
+def stack_field(field, high, low):
+    for x in range(PLANES):
+        whole = field[x, 0:48, :]
+        for e in range(3):
+            parts = split(turn(whole, 1 - e))
+            for a in range(3):
+                rows = slice((a * 3 + e) * 48, (a * 3 + e) * 48 + 48)
+                high[rows, plane(x - a + 1)] = parts[0]
+                low[rows, plane(x - a + 1)] = parts[1]
+
+
+def network(field, fwd1, fwd2, bias1, bias2, hidden, weights, u_hi, u_lo, h_hi, h_lo, work):
+    stack_field(field, u_hi, u_lo)
+    for pair in range(4):
+        cut = slice(pair * 256, pair * 256 + 256)
+        out = dot3((fwd1[0], fwd1[1]), (u_hi[:, cut], u_lo[:, cut]))
+        value = jnp.tanh(out + bias1[...])
+        hidden[:, cut] = value
+        parts = split(value)
+        h_hi[:, cut] = parts[0]
+        h_lo[:, cut] = parts[1]
+        work[:, cut] = dot3((fwd2[0], fwd2[1]), parts)
+    for x in range(PLANES):
+        total = bias2[:, :DEPTH]
+        for a in range(3):
+            for e in range(3):
+                tap = a * 3 + e
+                total = total + turn(work[tap * 48 : tap * 48 + 48, plane(x + a - 1)], 1 - e)
+        weights[:, plane(x)] = jax.nn.sigmoid(total)
+
+
+def around(field, x, direction, sign):
+    if direction == 0:
+        return [field[(x + sign) % PLANES, m * REACH + RIM : m * REACH + RIM + SLAB, :] for m in range(3)]
+    if direction == 1:
+        first = RIM + sign
+        return [field[x, m * REACH + first : m * REACH + first + SLAB, :] for m in range(3)]
+    return [turn(field[x, m * REACH + RIM : m * REACH + RIM + SLAB, :], -sign) for m in range(3)]
+
+
+def advected(field, weights, x):
+    center = around(field, x, 0, 0)
+    total = [jnp.zeros((SLAB, DEPTH), jnp.float32)] * 3
+    for d in range(3):
+        ahead = around(field, x, d, 1)
+        behind = around(field, x, d, -1)
+        plus = 0.5 * (center[d] + ahead[d])
+        minus = 0.5 * (behind[d] + center[d])
+        rate_up = weights[2 * d * SLAB : (2 * d + 1) * SLAB, plane(x)]
+        rate_low = weights[(2 * d + 1) * SLAB : (2 * d + 2) * SLAB, plane(x)]
+        for m in range(3):
+            upper = center[m] + rate_up * (ahead[m] - center[m])
+            lower = center[m] + rate_low * (behind[m] - center[m])
+            total[m] = total[m] + plus * upper - minus * lower
+    return [center[m] - KAPPA * total[m] for m in range(3)]
+
+
+def mixed(values, table):
+    outs = []
+    for row in table:
+        total = None
+        for weight, value in zip(row, values):
+            term = value * float(weight)
+            total = term if total is None else total + term
+        outs.append(total)
+    return outs
+
+
+def lane_groups(size):
+    return lax.broadcasted_iota(jnp.int32, (size, DEPTH), 1) // BAND
+
+
+def scatter_modes(source, rows, out):
+    groups = lane_groups(rows)
+    for p in range(4):
+        for g in range(4):
+            total = None
+            for f in range(2):
+                for t in range(2):
+                    slot = 2 * f + t
+                    value = turn(source(f, 2 * p + t), BAND * (slot - g))
+                    total = value if total is None else jnp.where(groups == slot, value, total)
+            out[p * 4 + g] = total
+
+
+def gather_modes(recv, f, k, rows):
+    groups = lane_groups(rows)
+    slot = 2 * f + k % 2
+    total = None
+    for g in range(4):
+        value = turn(recv[(k // 2) * 4 + g, 0:rows, :], BAND * (g - slot))
+        total = value if total is None else jnp.where(groups == g, value, total)
+    return total
+
+
+def first_kernel_body(mode_x, recv, fwd1, fwd2, bias1, bias2, z_hi, z_lo, out, hidden, weights, u_hi, u_lo, h_hi, h_lo, work, modes):
+    network(recv, fwd1, fwd2, bias1, bias2, hidden, weights, u_hi, u_lo, h_hi, h_lo, work)
+    table = (z_hi[...], z_lo[...])
+    moved_field = [jnp.concatenate(advected(recv, weights, x), axis=0) for x in range(PLANES)]
+    for f in range(2):
+        planes = moved_field if f == 0 else [recv[x, 36:60, :] for x in range(PLANES)]
+        for k, value in enumerate(mixed(planes, mode_x)):
+            modes[f, k] = value
+    for f in range(2):
+        flat = modes[f].reshape(PLANES * 24, DEPTH)
+        modes[f] = dot3(split(flat), table).reshape(PLANES, 24, DEPTH)
+    scatter_modes(lambda f, k: modes[f, k], 24, out)
+
+
+def leray(parts):
+    device = lax.axis_index("px") * 2 + lax.axis_index("py")
+    pair = device // 4
+    group = device % 4
+    lane = lax.broadcasted_iota(jnp.int32, (ROWS, DEPTH), 1)
+    row = lax.broadcasted_iota(jnp.int32, (ROWS, DEPTH), 0)
+    odd_x = (lane // BAND) % 2
+    odd_z = (lane // 16) % 2
+    number_z = 16 * group + lane % 16
+    top_x = (odd_x == 1) & (pair == 0)
+    top_y = row == ROWS // 2
+    top_z = (odd_z == 1) & (number_z == 0)
+    number_y = row % (ROWS // 2)
+    real = lambda value: value.astype(jnp.float32)
+    rate_x = real(jnp.where(odd_x == 1, -pair, pair))
+    rate_y = real(jnp.where(row < ROWS // 2, number_y, -number_y))
+    rate_z = real(jnp.where(odd_z == 1, -number_z, number_z))
+    high_x = real(jnp.where(top_x, PLANES // 2, 0))
+    high_y = real(jnp.where(top_y, ROWS // 2, 0))
+    high_z = real(jnp.where(top_z, DEPTH // 2, 0))
+    size = rate_x * rate_x + rate_y * rate_y + rate_z * rate_z
+    size = size + high_x * high_x + high_y * high_y + high_z * high_z
+    inverse = 1.0 / jnp.maximum(size, 1.0)
+
+    def slope_x(value):
+        return rate_x * jnp.where(odd_x == 1, turn(value, BAND), turn(value, -BAND))
+
+    def slope_y(value):
+        return rate_y * jnp.concatenate([value[ROWS // 2 :], value[: ROWS // 2]], axis=0)
+
+    def slope_z(value):
+        return rate_z * jnp.where(odd_z == 1, turn(value, 16), turn(value, -16))
+
+    spread = (slope_x(parts[0]) + slope_y(parts[1]) + slope_z(parts[2])) * inverse
+    high = (high_x * parts[0] + high_y * parts[1] + high_z * parts[2]) * inverse
+    return (
+        parts[0] + slope_x(spread) - high_x * high,
+        parts[1] + slope_y(spread) - high_y * high,
+        parts[2] + slope_z(spread) - high_z * high,
+    )
+
+
+def both_kernel(recv, in_hi, in_lo, out_hi, out_lo, out):
+    data = split(recv[...].reshape(16 * 24, DEPTH))
+    modes = dot3((in_hi[...], in_lo[...]), data)
+    fixed = leray([modes[m * ROWS : (m + 1) * ROWS] for m in range(3)])
+    back = dot3((out_hi[...], out_lo[...]), split(jnp.concatenate(fixed, axis=0)))
+    out[...] = back.reshape(16, 40, DEPTH)
+
+
+def one_kernel(recv, in_hi, in_lo, out_hi, out_lo, out):
+    data = split(recv[...].reshape(16 * 24, DEPTH))
+    modes = dot3((in_hi[...], in_lo[...]), data)
+    modes = modes[: 3 * ROWS] + turn(modes[3 * ROWS :], DEPTH // 2)
+    fixed = leray([modes[m * ROWS : (m + 1) * ROWS] for m in range(3)])
+    back = dot3((out_hi[...], out_lo[...]), split(jnp.concatenate(fixed, axis=0)))
+    lane = lax.broadcasted_iota(jnp.int32, (256, DEPTH), 1)
+    whole = jnp.where(lane < DEPTH // 2, back[:256], turn(back[256:], DEPTH // 2))
+    out[...] = whole.reshape(16, 16, DEPTH)
+
+
+def pullback(field, grad, hidden, weights, back2, back1, u_hi, u_lo, h_hi, h_lo, l_hi, l_lo, p_hi, p_lo, work, slope, sums, ends, earlier):
+    slope[...] = jnp.zeros_like(slope)
+    for x in range(PLANES):
+        center = around(field, x, 0, 0)
+        source = [-KAPPA * grad[x, m * SLAB : (m + 1) * SLAB, :] for m in range(3)]
+        own = [grad[x, m * SLAB : (m + 1) * SLAB, :] for m in range(3)]
+        logits = []
+        for d in range(3):
+            ahead = around(field, x, d, 1)
+            behind = around(field, x, d, -1)
+            plus = 0.5 * (center[d] + ahead[d])
+            minus = 0.5 * (behind[d] + center[d])
+            rate_up = weights[2 * d * SLAB : (2 * d + 1) * SLAB, plane(x)]
+            rate_low = weights[(2 * d + 1) * SLAB : (2 * d + 2) * SLAB, plane(x)]
+            grad_up = grad_low = grad_plus = grad_minus = None
+            to_ahead, to_behind = [], []
+            add = lambda total, term: term if total is None else total + term
+            for m in range(3):
+                gap_up = ahead[m] - center[m]
+                gap_low = behind[m] - center[m]
+                grad_plus = add(grad_plus, source[m] * (center[m] + rate_up * gap_up))
+                grad_minus = add(grad_minus, -source[m] * (center[m] + rate_low * gap_low))
+                grad_up = add(grad_up, source[m] * gap_up)
+                grad_low = add(grad_low, -source[m] * gap_low)
+                push_up = source[m] * plus
+                push_low = -source[m] * minus
+                to_ahead.append(push_up * rate_up)
+                to_behind.append(push_low * rate_low)
+                own[m] = own[m] + (push_up - to_ahead[m]) + (push_low - to_behind[m])
+            own[d] = own[d] + 0.5 * (grad_plus + grad_minus)
+            to_ahead[d] = to_ahead[d] + 0.5 * grad_plus
+            to_behind[d] = to_behind[d] + 0.5 * grad_minus
+            logits.append(grad_up * plus * rate_up * (1.0 - rate_up))
+            logits.append(grad_low * minus * rate_low * (1.0 - rate_low))
+            for m in range(3):
+                first = m * REACH + RIM
+                if d == 0:
+                    slope[(x + 1) % PLANES, first : first + SLAB, :] += to_ahead[m]
+                    slope[(x - 1) % PLANES, first : first + SLAB, :] += to_behind[m]
+                elif d == 1:
+                    slope[x, first + 1 : first + 1 + SLAB, :] += to_ahead[m]
+                    slope[x, first - 1 : first - 1 + SLAB, :] += to_behind[m]
+                else:
+                    own[m] = own[m] + turn(to_ahead[m], 1) + turn(to_behind[m], -1)
+        for m in range(3):
+            slope[x, m * REACH + RIM : m * REACH + RIM + SLAB, :] += own[m]
+        whole = jnp.concatenate(logits, axis=0)
+        for e in range(3):
+            parts = split(turn(whole, e - 1))
+            for a in range(3):
+                rows = slice((a * 3 + e) * 48, (a * 3 + e) * 48 + 48)
+                l_hi[rows, plane(x + a - 1)] = parts[0]
+                l_lo[rows, plane(x + a - 1)] = parts[1]
+    for pair in range(4):
+        cut = slice(pair * 256, pair * 256 + 256)
+        value = dot3((back2[0], back2[1]), (l_hi[:, cut], l_lo[:, cut]))
+        parts = split(value * (1.0 - hidden[:, cut] * hidden[:, cut]))
+        p_hi[:, cut] = parts[0]
+        p_lo[:, cut] = parts[1]
+        work[:, cut] = dot3((back1[0], back1[1]), parts)
+    for x in range(PLANES):
+        total = slope[x, 0:40, :]
+        for a in range(3):
+            for e in range(3):
+                tap = a * 3 + e
+                total = total + turn(work[tap * 48 : tap * 48 + 40, plane(x - a + 1)], e - 1)
+        slope[x, 0:40, :] = total
+    second = dot3((l_hi[...], l_lo[...]), (h_hi[...], h_lo[...]), NT)
+    first = dot3((u_hi[...], u_lo[...]), (p_hi[...], p_lo[...]), NT)
+    ones = jnp.ones((16, FLAT), jnp.bfloat16)
+    end1 = dot(ones, p_hi[...], NT) + dot(ones, p_lo[...], NT)
+    end2 = dot(ones, l_hi[4 * 48 : 5 * 48, :], NT) + dot(ones, l_lo[4 * 48 : 5 * 48, :], NT)
+    if earlier is None:
+        sums[0:STACK, :] = second
+        sums[STACK:, :] = first
+        ends[0:16, :] = end1
+        ends[16:32, 0:LOG] = end2
+    else:
+        old_sums, old_ends = earlier
+        sums[0:STACK, :] = old_sums[0:STACK, :] + second
+        sums[STACK:, :] = old_sums[STACK:, :] + first
+        ends[0:16, :] = old_ends[0:16, :] + end1
+        ends[16:32, 0:LOG] = old_ends[16:32, 0:LOG] + end2
+
+
+def second_kernel_body(
+    mode_x, recv, fwd1, fwd2, back2, back1, bias1, bias2, to_hi, to_lo, from_hi, from_lo,
+    out, sums, ends,
+    field, grad, modes, rows6, hidden, weights, u_hi, u_lo, h_hi, h_lo, l_hi, l_lo, p_hi, p_lo, work, slope,
+):
+    back_z = (from_hi[...], from_lo[...])
+    for f in range(2):
+        for k in range(PLANES):
+            modes[k] = gather_modes(recv, f, k, 40)
+        flat = dot3(split(modes[...].reshape(PLANES * 40, DEPTH)), back_z)
+        modes[...] = flat.reshape(PLANES, 40, DEPTH)
+        for x, value in enumerate(mixed([modes[k] for k in range(PLANES)], mode_x.T)):
+            field[x, 0:40, :] = value
+            field[x, 40:48, :] = jnp.zeros((8, DEPTH), jnp.float32)
+        if f == 0:
+            network(field, fwd1, fwd2, bias1, bias2, hidden, weights, u_hi, u_lo, h_hi, h_lo, work)
+            for x in range(PLANES):
+                slope[x] = field[x]
+        else:
+            for x in range(PLANES):
+                for m in range(3):
+                    first = m * REACH + RIM
+                    grad[x, m * SLAB : (m + 1) * SLAB, :] = field[x, first : first + SLAB, :]
+    for x in range(PLANES):
+        field[x] = slope[x]
+    pullback(
+        field, grad, hidden, weights, back2, back1, u_hi, u_lo, h_hi, h_lo, l_hi, l_lo, p_hi, p_lo,
+        work, slope, sums, ends, None,
+    )
+    for k, value in enumerate(mixed([slope[x, 0:40, :] for x in range(PLANES)], mode_x)):
+        modes[k] = value
+    flat = dot3(split(modes[...].reshape(PLANES * 40, DEPTH)), (to_hi[...], to_lo[...]))
+    modes[...] = flat.reshape(PLANES, 40, DEPTH)
+    for h in range(2):
+        for k in range(PLANES):
+            for m in range(3):
+                rows6[h, k, m * 6 : m * 6 + 6, :] = modes[k, m * REACH + 6 * h : m * REACH + 6 * h + 6, :]
+            rows6[h, k, 18:24, :] = jnp.zeros((6, DEPTH), jnp.float32)
+    scatter_modes(lambda h, k: rows6[h, k], 24, out)
+
+
+def third_kernel_body(
+    mode_x, recv, field, hidden, weights, back2, back1, from_hi, from_lo, old_sums, old_ends,
+    spread_t, mask, lift, count,
+    out,
+    grad, modes, u_hi, u_lo, h_hi, h_lo, l_hi, l_lo, p_hi, p_lo, work, slope, sums, ends, pieces,
+):
+    back_z = (from_hi[...], from_lo[...])
+    for h in range(2):
+        for k in range(PLANES):
+            modes[k] = gather_modes(recv, h, k, 16)
+        flat = dot3(split(modes[...].reshape(PLANES * 16, DEPTH)), back_z)
+        modes[...] = flat.reshape(PLANES, 16, DEPTH)
+        for x, value in enumerate(mixed([modes[k] for k in range(PLANES)], mode_x.T)):
+            for m in range(3):
+                grad[x, m * SLAB + 4 * h : m * SLAB + 4 * h + 4, :] = value[m * 4 : m * 4 + 4, :]
+    stack_field(field, u_hi, u_lo)
+    parts = split(hidden[...])
+    h_hi[...] = parts[0]
+    h_lo[...] = parts[1]
+    pullback(
+        field, grad, hidden, weights, back2, back1, u_hi, u_lo, h_hi, h_lo, l_hi, l_lo, p_hi, p_lo,
+        work, slope, sums, ends, (old_sums, old_ends),
+    )
+    for x in range(PLANES):
+        out[x, 0:40, :] = slope[x, 0:40, :]
+        out[x, 36:40, :] = jnp.zeros((4, DEPTH), jnp.float32)
+    pack_grads(sums, ends, spread_t, mask, lift, count, pieces)
+    for x in range(PLANES):
+        out[x, 40:80, :] = pieces[96:136, :]
+
+
+def pack_grads(sums, ends, spread_t, mask, lift, count, pieces):
+    pieces[...] = jnp.zeros_like(pieces)
+    for b in range(3):
+        parts = split(sums[...] * mask[b].astype(jnp.float32))
+        rows = dot(spread_t[...], parts[0]) + dot(spread_t[...], parts[1])
+        parts = split(rows)
+        pieces[0:96, :] = dot(parts[0], lift[...]) + dot(parts[1], lift[...])
+        for c in range(3):
+            slot = b * 3 + c
+            if slot < 8:
+                pieces[96:123, :] += turn(pieces[c * 27 : c * 27 + 27, :], 16 * slot)
+            else:
+                for third in range(3):
+                    first = c * 27 + third * 9
+                    pieces[123:132, :] += turn(pieces[first : first + 9, :], 16 * third)
+    parts = split(ends[0:16, :])
+    total = dot(parts[0], lift[...]) + dot(parts[1], lift[...])
+    parts = split(ends[16:32, 0:LOG])
+    total = total + dot(parts[0], count[...]) + dot(parts[1], count[...])
+    pieces[135:136, :] = total[0:1, :]
+
+
+def fold_kernel(recv, main, edge, ext):
+    ext[...] = jnp.zeros_like(ext)
+    total = None
+    for q in range(PLANES):
+        for m in range(3):
+            ext[m, 8 * q + 6 : 8 * q + 18, :] += recv[q, m * REACH : (m + 1) * REACH, :]
+        block = recv[q, 40:80, :]
+        total = block if total is None else total + block
+    for m in range(3):
+        main[m, 0] = ext[m, 8:72, :]
+        edge[m * 8 : m * 8 + 2, :] = ext[m, 72:74, :]
+        edge[m * 8 + 2 : m * 8 + 4, :] = ext[m, 6:8, :]
+        edge[m * 8 + 4 : m * 8 + 8, :] = jnp.zeros((4, DEPTH), jnp.float32)
+    edge[24:64, :] = total
+
+
+def last_kernel(main, edge, other, out, grads):
+    for m in range(3):
+        out[m, 0] = main[m, 0]
+        out[m, 0, 0:2, :] += other[m * 8 : m * 8 + 2, :]
+        out[m, 0, 62:64, :] += other[m * 8 + 2 : m * 8 + 4, :]
+    grads[...] = edge[24:64, :] + other[24:64, :]
+
+
+def slab_device(velocity, cotangent, first_kernel, first_bias, second_kernel, second_bias):
+    c = constants()
+    mode_x = c["mode_x"]
+    half = jnp.bfloat16
+    f32 = lambda *dims: pltpu.VMEM(dims, jnp.float32)
+    b16 = lambda *dims: pltpu.VMEM(dims, half)
+    swap = [(0, 1), (1, 0)]
+
+    edges = jnp.concatenate([velocity[:, 0, :RIM], velocity[:, 0, -RIM:]], axis=1)
+    edges = lax.ppermute(edges, "py", swap)
+    packed = call(pack_kernel, shape(PLANES, 64, DEPTH), (velocity, cotangent, edges), [f32(3, 80, DEPTH)])
+    recv = lax.all_to_all(packed, "px", 0, 0)
+
+    taps = jnp.concatenate(
+        [
+            jnp.transpose(second_kernel, (2, 4, 0, 3, 1)).reshape(54, 48),
+            jnp.transpose(first_kernel, (2, 4, 1, 3, 0)).reshape(27, 48),
+            jnp.zeros((15, 48), jnp.float32),
+        ]
+    )
+    fwd2, fwd1, back2, back1 = call(
+        weights_kernel,
+        [
+            shape(2, STACK, HID, kind=half),
+            shape(2, HID, STACK, kind=half),
+            shape(2, HID, STACK, kind=half),
+            shape(2, STACK, HID, kind=half),
+        ],
+        (taps, c["spread"], c["spread_t"], c["mask"], c["mask_t"], c["lift"], c["lift_t"]),
+    )
+    bias1 = jnp.broadcast_to(jnp.repeat(first_bias, WIDE)[:, None], (HID, 256))
+    bias2 = jnp.broadcast_to(jnp.repeat(second_bias, SLAB)[:, None], (LOG, 256))
+
+    stacks = lambda rows: [b16(rows, FLAT), b16(rows, FLAT)]
+    sent, hidden, weights = call(
+        functools.partial(first_kernel_body, mode_x),
+        [shape(16, 24, DEPTH), shape(HID, FLAT), shape(LOG, FLAT)],
+        (recv, fwd1, fwd2, bias1, bias2, *c["to_z"]),
+        stacks(STACK) + stacks(HID) + [f32(STACK, FLAT), f32(2, PLANES, 24, DEPTH)],
+    )
+    both = ("px", "py")
+    moved_modes = lax.all_to_all(sent, both, 0, 0)
+    moved_modes = call(both_kernel, shape(16, 40, DEPTH), (moved_modes, *c["both_in"], *c["both_out"]))
+    moved_modes = lax.all_to_all(moved_modes, both, 0, 0)
+
+    sent, sums, ends = call(
+        functools.partial(second_kernel_body, mode_x),
+        [shape(16, 24, DEPTH), shape(2 * STACK, HID), shape(32, HID)],
+        (moved_modes, fwd1, fwd2, back2, back1, bias1, bias2, *c["to_z"], *c["from_z"]),
+        [f32(PLANES, 48, DEPTH), f32(PLANES, 24, DEPTH), f32(PLANES, 40, DEPTH), f32(2, PLANES, 24, DEPTH)]
+        + [f32(HID, FLAT), f32(LOG, FLAT)]
+        + stacks(STACK) + stacks(HID) + stacks(STACK) + stacks(HID)
+        + [f32(STACK, FLAT), f32(PLANES, 48, DEPTH)],
+    )
+    moved_modes = lax.all_to_all(sent, both, 0, 0)
+    moved_modes = call(one_kernel, shape(16, 16, DEPTH), (moved_modes, *c["one_in"], *c["one_out"]))
+    moved_modes = lax.all_to_all(moved_modes, both, 0, 0)
+
+    sent = call(
+        functools.partial(third_kernel_body, mode_x),
+        shape(PLANES, 80, DEPTH),
+        (
+            moved_modes, recv, hidden, weights, back2, back1, *c["from_z"], sums, ends,
+            c["spread_t"], c["mask"], c["lift"], c["count"],
+        ),
+        [f32(PLANES, 24, DEPTH), f32(PLANES, 16, DEPTH)]
+        + stacks(STACK) + stacks(HID) + stacks(STACK) + stacks(HID)
+        + [f32(STACK, FLAT), f32(PLANES, 48, DEPTH), f32(2 * STACK, HID), f32(32, HID), f32(136, DEPTH)],
+    )
+    recv = lax.all_to_all(sent, "px", 0, 0)
+    main, edge = call(
+        fold_kernel, [shape(3, 1, 64, DEPTH), shape(64, DEPTH)], (recv,), [f32(3, 80, DEPTH)]
+    )
+    other = lax.ppermute(edge, "py", swap)
+    grad_velocity, grads = call(
+        last_kernel, [shape(3, 1, 64, DEPTH), shape(40, DEPTH)], (main, edge, other)
+    )
+
+    def piece(b, kind):
+        slot = b * 3 + kind
+        if slot < 8:
+            return grads[0:27, 16 * slot : 16 * slot + 16]
+        return jnp.concatenate([grads[27:36, 16 * i : 16 * i + 16] for i in range(3)])
+
+    first = jnp.stack([piece(b, 2) for b in range(3)]).reshape(3, 3, 3, 3, CHANNELS)
+    second = jnp.stack([jnp.concatenate([piece(b, 0), piece(b, 1)]) for b in range(3)])
+    second = second.reshape(3, 3, 3, COEFFS, CHANNELS)
+    return (
+        grad_velocity,
+        jnp.transpose(first, (4, 3, 1, 0, 2)),
+        grads[39, 0:16],
+        jnp.transpose(second, (3, 4, 1, 0, 2)),
+        grads[39, 16:22],
+    )
+
+
+def fits_slabs(mesh):
+    return mesh.shape["px"] == PLANES and mesh.shape["py"] == 2
+
+
 def solution(mesh):
     return jax.shard_map(
-        on_device,
+        slab_device if fits_slabs(mesh) else on_device,
         mesh=mesh,
         in_specs=(
             P(None, ("groups", "px"), "py", None),

time: 725 us -> 134 us (0.18); the launches traced: 713 us -> 133 us
  local copies, waits for them, and re-layouts: 246 us -> 12.8 us
  matrix products: 127 us -> 0 us
  waiting for transfers between devices: 119 us -> 2.24 us
  other arithmetic: 65.8 us -> 0.78 us
  starting transfers between devices: 64.7 us -> 7.66 us
  Pallas kernels: 0 us -> 38.3 us
  blocking collectives: 84.5 us -> 70.6 us
    unnamed x442 -> x8, local copies, waits for them, and re-layouts: 156 us -> 2.51 us
    dot_general x80 -> x0, matrix products: 127 us -> none  [the longest x12 40.7 us: scatter_conv(): jnp.einsum('km,mxyz->kxyz', matrix, padded[:, shift_x:shift_x + size_x],...]
    ppermute x40 -> x2, waiting for transfers between devices: 92.8 us -> 2.24 us  [the longest x1 1.42 us: slab_device(): other = lax.ppermute(edge, 'py', swap)]
    psum x1 -> x0, blocking collectives: 61 us -> none  [summed(): return lax.psum((grads[0], grads[1], grads[2], grads[3]), ('px', 'py'))]
    all_to_all x6 -> x5, blocking collectives: 23.5 us -> 70.6 us  [the longest x2 28.4 us: slab_device(): moved_modes = lax.all_to_all(sent, both, 0, 0)]
    another operation x44 -> x6, local copies, waits for them, and re-layouts: 45.7 us -> 0.05 us  [the longest x3 0.03 us: slab_device(): jnp.stack([piece(b, 2) for b in range(3)]).reshape(3, 3, 3, 3, CHANNELS)]
    ppermute x40 -> x2, starting transfers between devices: 40.1 us -> 0.52 us  [the longest x1 0.52 us: slab_device(): edges = lax.ppermute(edges, 'py', swap)]
    pallas_call x0 -> x9, Pallas kernels: none -> 38.3 us  [call(): pl.pallas_call(kernel, out_shape=outs, in_specs=[pl.BlockSpec(memory_spac...]
  transfers between devices with their start and end apart: 46 -> 3, of which waited for: 24 -> 2; matrix products, arithmetic and copies ran while one was open for 13% -> 3% of each run, Pallas kernels for 0% -> 4%
where the time goes in v1:
time: 134 us; the launch traced here: 133 us
  blocking collectives  70.6 us (53%)
  Pallas kernels  38.3 us (29%)
  local copies, waits for them, and re-layouts  12.8 us (10%)
  starting transfers between devices  7.66 us (6%)
  waiting for transfers between devices  2.24 us (2%)
    pallas_call x9, Pallas kernels, call(): pl.pallas_call(kernel, out_shape=outs, in_specs=[pl.BlockSpec(memory_spac...  38.3 us
    all_to_all x2, blocking collectives, slab_device(): moved_modes = lax.all_to_all(sent, both, 0, 0)  28.4 us
    all_to_all x2, blocking collectives, slab_device(): moved_modes = lax.all_to_all(moved_modes, both, 0, 0)  27.4 us
    all_to_all x1, blocking collectives, slab_device(): recv = lax.all_to_all(sent, 'px', 0, 0)  14.8 us
    all_to_all x1, starting transfers between devices, slab_device(): recv = lax.all_to_all(packed, 'px', 0, 0)  7.14 us
  transfers between devices with their start and end apart: 3, of which 2 were waited for; matrix products, arithmetic and copies ran while one was open for 3% of the time, Pallas kernels for 4%

profile of v1, /device:TPU:0, one launch (start us, length us, event | category | flops | bytes accessed | tf_op | source)
XLA Modules:
  0.0 133.1 jit_solution(3174167415544011620)
XLA Ops:
  1.9 0.8 collective-permute-done.edges
  3.3 1.7 %shard_map.272 = f32[8,64,128]{2,1,0:T(8,128)} custom-call(f32[3,1,64,128]{3,2,1,0:T(8,128)} %field.1, f32[3,1,64,128]{3,2,1,0:T(8,128)} %cot.1, f32[3,4,128]{2,1,0:T(4,128)} %copy-done.2), custom_call_target="tpu_custom_call" | custom-call | tf_op jit(solution)/shard_map/pallas_call | solution.py:415
  5.0 7.1 %all-to-all-start = ((f32[8,64,128]{2,1,0:T(8,128)}), f32[8,64,128]{2,1,0:T(8,128)S(1)}, u32[]{:S(2)}, u32[]{:S(2)}) async-start(f32[8,64,128]{2,1,0:T(8,128)} %shard_map.272), calls=%async_computation | async-start | bytes 524288 | tf_op jit(solution)/shard_map/all_to_all | solution.py:846
  13.7 0.8 copy.64
  14.7 0.9 copy.63
  16.5 5.1 %shard_map.273 = (bf16[2,432,160]{2,1,0:T(8,128)(2,1)}, bf16[2,160,432]{2,1,0:T(8,128)(2,1)}, bf16[2,160,432]{2,1,0:T(8,128)(2,1)}, bf16[2,432,160]{2,1,0:T(8,128)(2,1)}) custom-call(f32[96,48]{1,0:T(8,128)} %maximum_maximum_fusion.taps, bf16[864,96]{1,0:T(8,128)(2,1)} %constant.40.clone.spread, bf16[96,864]{1,0:T(8,128)(2,1)} %constant.41.clone.spread_t, ...), custom_call_target="tpu_custom_call" | custom-call | tf_op jit(solution)/shard_map/pallas_call | solution.py:415
  22.3 0.7 broadcast_in_dim.26.bias1
  23.1 4.3 %shard_map.274 = (f32[16,24,128]{2,1,0:T(8,128)}, f32[160,1024]{1,0:T(8,128)}, f32[48,1024]{1,0:T(8,128)}) custom-call(f32[8,64,128]{2,1,0:T(8,128)} %copy-done, bf16[2,160,432]{2,1,0:T(8,128)(2,1)} %get-tuple-element.19.fwd1, bf16[2,432,160]{2,1,0:T(8,128)(2,1)} %get-tuple-element.20.fwd2, f32[160,256]{1,0:T(8,128)} %broadcast_in_dim.26.bias1, ...), custom_call_target="tpu_custom_call" | custom-call | tf_op jit(solution)/shard_map/pallas_call | solution.py:415
  27.4 15.2 %all_to_all.30.recv = f32[16,24,128]{2,1,0:T(8,128)} all-to-all(f32[16,24,128]{2,1,0:T(8,128)} %get-tuple-element.21), channel_id=1, replica_groups=mesh['groups'=2,'px'=8,'py'=2] {'px','py'}, dimensions={0} | all-to-all | bytes 393216 | tf_op jit(solution)/shard_map/all_to_all | solution.py:876
  42.6 3.2 %shard_map.275 = f32[16,40,128]{2,1,0:T(8,128)} custom-call(f32[16,24,128]{2,1,0:T(8,128)} %all_to_all.30.recv, bf16[384,384]{1,0:T(8,128)(2,1)} %constant.48.clone.in_hi, bf16[384,384]{1,0:T(8,128)(2,1)} %constant.49.clone.in_lo, bf16[640,384]{1,0:T(8,128)(2,1)} %constant.50.clone.out_hi, bf16[640,384]{1,0:T(8,128)(2,1)} %constant.51.clone.out_lo), custom_call_target="tpu_custom_call" | custom-call | tf_op jit(solution)/shard_map/pallas_call | solution.py:415
  45.8 15.3 %all_to_all.31.recv = f32[16,40,128]{2,1,0:T(8,128)} all-to-all(f32[16,40,128]{2,1,0:T(8,128)} %shard_map.275), channel_id=1, replica_groups=mesh['groups'=2,'px'=8,'py'=2] {'px','py'}, dimensions={0} | all-to-all | bytes 655360 | tf_op jit(solution)/shard_map/all_to_all | solution.py:878
  61.1 8.5 %shard_map.276 = (f32[16,24,128]{2,1,0:T(8,128)}, f32[864,160]{1,0:T(8,128)}, f32[32,160]{1,0:T(8,128)}) custom-call(f32[16,40,128]{2,1,0:T(8,128)} %all_to_all.31.recv, bf16[2,160,432]{2,1,0:T(8,128)(2,1)} %get-tuple-element.19.fwd1, bf16[2,432,160]{2,1,0:T(8,128)(2,1)} %get-tuple-element.20.fwd2, bf16[2,160,432]{2,1,0:T(8,128)(2,1)} %get-tuple-element.22.back2, ...), custom_call_target="tpu_custom_call" | custom-call | tf_op jit(solution)/shard_map/pallas_call | solution.py:415
  69.7 13.2 %all_to_all.32.recv = f32[16,24,128]{2,1,0:T(8,128)} all-to-all(f32[16,24,128]{2,1,0:T(8,128)} %get-tuple-element.24), channel_id=1, replica_groups=mesh['groups'=2,'px'=8,'py'=2] {'px','py'}, dimensions={0} | all-to-all | bytes 393216 | tf_op jit(solution)/shard_map/all_to_all | solution.py:889
  82.9 3.6 %shard_map.277 = f32[16,16,128]{2,1,0:T(8,128)} custom-call(f32[16,24,128]{2,1,0:T(8,128)} %all_to_all.32.recv, bf16[768,384]{1,0:T(8,128)(2,1)} %constant.54.clone.in_hi, bf16[768,384]{1,0:T(8,128)(2,1)} %constant.55.clone.in_lo, bf16[512,384]{1,0:T(8,128)(2,1)} %constant.56.clone.out_hi, bf16[512,384]{1,0:T(8,128)(2,1)} %constant.57.clone.out_lo), custom_call_target="tpu_custom_call" | custom-call | tf_op jit(solution)/shard_map/pallas_call | solution.py:415
  86.5 12.1 %all_to_all.33.recv = f32[16,16,128]{2,1,0:T(8,128)} all-to-all(f32[16,16,128]{2,1,0:T(8,128)} %shard_map.277), channel_id=1, replica_groups=mesh['groups'=2,'px'=8,'py'=2] {'px','py'}, dimensions={0} | all-to-all | bytes 262144 | tf_op jit(solution)/shard_map/all_to_all | solution.py:891
  98.6 8.5 %shard_map.278 = f32[8,80,128]{2,1,0:T(8,128)} custom-call(f32[16,16,128]{2,1,0:T(8,128)} %all_to_all.33.recv, f32[8,64,128]{2,1,0:T(8,128)} %copy-done, f32[160,1024]{1,0:T(8,128)} %get-tuple-element.25.hidden, f32[48,1024]{1,0:T(8,128)} %get-tuple-element.26.weights, bf16[2,160,432]{2,1,0:T(8,128)(2,1)} %get-tuple-element.22.back2, ...), custom_call_target="tpu_custom_call" | custom-call | tf_op jit(solution)/shard_map/pallas_call | solution.py:415
  107.1 14.8 %all_to_all.34.recv = f32[8,80,128]{2,1,0:T(8,128)} all-to-all(f32[8,80,128]{2,1,0:T(8,128)} %shard_map.278), channel_id=1, replica_groups=mesh['groups'=2,'px'=8,'py'=2] {'px'}, dimensions={0} | all-to-all | bytes 655360 | tf_op jit(solution)/shard_map/all_to_all | solution.py:904
  121.9 1.7 %shard_map.279 = (f32[3,1,64,128]{3,2,1,0:T(8,128)}, f32[64,128]{1,0:T(8,128)}) custom-call(f32[8,80,128]{2,1,0:T(8,128)} %all_to_all.34.recv), custom_call_target="tpu_custom_call" | custom-call | tf_op jit(solution)/shard_map/pallas_call | solution.py:415
  123.5 1.4 %collective-permute-done.1.other = f32[64,128]{1,0:T(8,128)S(1)} collective-permute-done((f32[64,128]{1,0:T(8,128)}, f32[64,128]{1,0:T(8,128)S(1)}, u32[]{:S(2)}, u32[]{:S(2)}) %collective-permute-start.1) | collective-permute-done | bytes 32800 | tf_op jit(solution)/shard_map/ppermute | solution.py:908
  125.6 1.6 %shard_map.280 = (f32[3,1,64,128]{3,2,1,0:T(8,128)}, f32[40,128]{1,0:T(8,128)}) custom-call(f32[3,1,64,128]{3,2,1,0:T(8,128)} %get-tuple-element.29.main, f32[64,128]{1,0:T(8,128)} %get-tuple-element.30.edge, f32[64,128]{1,0:T(8,128)} %copy-done.1), custom_call_target="tpu_custom_call" | custom-call | tf_op jit(solution)/shard_map/pallas_call | solution.py:415
  127.1 1.2 slice_bitcast_fusion.3
  128.3 1.3 slice_bitcast_fusion.2
  129.6 0.9 fusion.1
  130.5 1.1 fusion
  (34 shorter events, 7.2 us)
Async XLA Ops:
  1.4 1.3 %collective-permute-start = (f32[3,4,128]{2,1,0:T(4,128)S(1)}, f32[3,4,128]{2,1,0:T(4,128)S(1)}, u32[]{:S(2)}, u32[]{:S(2)}) collective-permute-start(f32[3,4,128]{2,1,0:T(4,128)S(1)} %pad_maximum_fusion.4), channel_id=1, source_target_pairs={{0,1},{1,0},{2,3},{3,2},{4,5},{5,4},{6,7},{7,6},{8,9},{9,8},{10,11... | collective-permute-start | bytes 18440 | tf_op jit(solution)/shard_map/ppermute | solution.py:844
  2.7 0.6 copy-start.2
  5.0 16.7 %all-to-all-start = ((f32[8,64,128]{2,1,0:T(8,128)}), f32[8,64,128]{2,1,0:T(8,128)S(1)}, u32[]{:S(2)}, u32[]{:S(2)}) async-start(f32[8,64,128]{2,1,0:T(8,128)} %shard_map.272), calls=%async_computation | async-start | bytes 524288 | tf_op jit(solution)/shard_map/all_to_all | solution.py:846
  21.6 1.4 %copy-start = (f32[8,64,128]{2,1,0:T(8,128)}, f32[8,64,128]{2,1,0:T(8,128)S(1)}, u32[]{:S(2)}) copy-start(f32[8,64,128]{2,1,0:T(8,128)S(1)} %all-to-all-done.recv.field) | copy-start | bytes 786436
  123.5 1.4 %collective-permute-start.1 = (f32[64,128]{1,0:T(8,128)}, f32[64,128]{1,0:T(8,128)S(1)}, u32[]{:S(2)}, u32[]{:S(2)}) collective-permute-start(f32[64,128]{1,0:T(8,128)} %get-tuple-element.30.edge), channel_id=1, source_target_pairs={{0,1},{1,0},{2,3},{3,2},{4,5},{5,4},{6,7},{7,6},{8,9},{9,8},{10,11... | collective-permute-start | bytes 98312 | tf_op jit(solution)/shard_map/ppermute | solution.py:908
  125.0 0.6 copy-start.1

commit v2 on v1

--- a/solution.py
+++ b/solution.py
@@ -343,7 +343,10 @@
         return out.reshape(3 * ROWS, 16 * block)
 
     both_in = table(24, 0, 8)
-    both_out = table(40, -RIM, REACH).T
+    wide_out = table(40, -RIM, REACH).T.reshape(16, 40, 3 * ROWS)
+    own_out = table(24, 0, 8).T.reshape(16, 24, 3 * ROWS)
+    rest = np.concatenate([own_out, wide_out[:, 32:]], axis=1)
+    both_out = np.stack([wide_out[:, :32], rest]).reshape(2 * 16 * 32, 3 * ROWS)
     one_in = np.concatenate([table(24, -RIM, 6), table(24, -RIM + 6, 6)])
     one_out = np.concatenate([table(16, 0, 4).T, table(16, 4, 4).T])
 
@@ -376,12 +379,9 @@
         both_out=halves(both_out),
         one_in=halves(one_in),
         one_out=halves(one_out),
-        spread=spread.astype(half),
         spread_t=np.ascontiguousarray(spread.T).astype(half),
         mask=mask.astype(half),
-        mask_t=np.ascontiguousarray(mask.transpose(0, 2, 1)).astype(half),
         lift=lift.astype(half),
-        lift_t=np.ascontiguousarray(lift[:, :CHANNELS].T).astype(half),
         count=count.astype(half),
     )
 
@@ -409,7 +409,7 @@
     return slice(x * DEPTH, (x + 1) * DEPTH)
 
 
-def call(kernel, outs, args, scratch=()):
+def call(kernel, outs, args, scratch=(), room=16):
     single = not isinstance(outs, (list, tuple))
     shapes = [outs] if single else outs
     return pl.pallas_call(
@@ -422,7 +422,7 @@
             else [pl.BlockSpec(memory_space=pltpu.VMEM)] * len(shapes)
         ),
         scratch_shapes=list(scratch),
-        compiler_params=pltpu.CompilerParams(vmem_limit_bytes=56 * 2**20),
+        compiler_params=pltpu.CompilerParams(vmem_limit_bytes=room * 2**20),
     )(*args)
 
 
@@ -430,28 +430,77 @@
     return jax.ShapeDtypeStruct(dims, kind)
 
 
-def weights_kernel(taps, spread, spread_t, mask, mask_t, lift, lift_t, fwd2, fwd1, back2, back1):
-    parts = split(taps[...])
+def counting(size, dim):
+    return lax.broadcasted_iota(jnp.int32, size, dim).astype(jnp.float32)
+
+
+def remainder(value, count):
+    return value - count * jnp.floor((value + 0.5) / count)
+
+
+def band_tables(tall):
+    row, col = (0, 1) if tall else (1, 0)
+    size = lambda rows, cols: (rows, cols) if tall else (cols, rows)
+    where = counting(size(2 * STACK, 96), row)
+    to = counting(size(2 * STACK, 96), col)
+    first = where - 8.0 * to
+    third = to - 54.0
+    second = where - STACK - (16.0 * third - 4.0 * remainder(third, 3.0))
+    picks = ((to < 54.0) & (first >= 0.0) & (first < 8.0)) | (
+        (to >= 54.0) & (to < 81.0) & (second >= 0.0) & (second < 12.0)
+    )
+    where = counting(size(2 * STACK, HID), row)
+    inner = remainder(counting(size(2 * STACK, HID), col), 10.0)
+    outer = where - STACK
+    offset = jnp.where(
+        where < STACK,
+        inner - remainder(where, 8.0),
+        remainder(remainder(outer, 48.0), 12.0) - inner,
+    )
+    gap = counting(size(HID, CHANNELS), row) - 10.0 * counting(size(HID, CHANNELS), col)
+    lift = (gap >= 0.0) & (gap < 10.0)
+    half = jnp.bfloat16
+    return picks.astype(jnp.float32).astype(half), offset, lift.astype(jnp.float32).astype(half)
+
+
+def weights_kernel(taps1, taps2, bias1, bias2, fwd2, fwd1, back2, back1, wide1, wide2, blocks):
+    blocks[...] = jnp.zeros_like(blocks)
+    for b in range(3):
+        for a in range(3):
+            for e in range(3):
+                tap = a * 3 + e
+                for o in range(COEFFS):
+                    blocks[b, tap * 6 + o, :] = taps2[o * 9 + a * 3 + b, e, :]
+                for m in range(3):
+                    blocks[b, 54 + tap * 3 + m, :] = taps1[m * 9 + a * 3 + b, e, :]
+    spread, offset, lift = band_tables(True)
+    spread_t, offset_t, lift_t = band_tables(False)
+    tall = [jnp.zeros((2 * STACK, HID), jnp.float32)] * 2
+    wide = [jnp.zeros((HID, 2 * STACK), jnp.float32)] * 2
+    for b in range(3):
+        for half, block in enumerate(split(blocks[b])):
+            rows = dot(spread, block).astype(jnp.bfloat16)
+            tall[half] = jnp.where(offset == float(b), dot(rows, lift_t), tall[half])
+            cols = dot(lift, block, NT).astype(jnp.bfloat16)
+            wide[half] = jnp.where(offset_t == float(b), dot(cols, spread_t), wide[half])
     for half in range(2):
-        tall = jnp.zeros((2 * STACK, HID), jnp.float32)
-        wide = jnp.zeros((HID, 2 * STACK), jnp.float32)
-        for b in range(3):
-            block = parts[half][:, b * 16 : (b + 1) * 16]
-            rows = dot(spread[...], block).astype(jnp.bfloat16)
-            tall = tall + mask[b].astype(jnp.float32) * dot(rows, lift_t[...])
-            cols = dot(lift[:, :CHANNELS], block, NT).astype(jnp.bfloat16)
-            wide = wide + mask_t[b].astype(jnp.float32) * dot(cols, spread_t[...])
-        fwd2[half] = tall[:STACK].astype(jnp.bfloat16)
-        back1[half] = tall[STACK:].astype(jnp.bfloat16)
-        back2[half] = wide[:, :STACK].astype(jnp.bfloat16)
-        fwd1[half] = wide[:, STACK:].astype(jnp.bfloat16)
-
-
-def pack_kernel(field, cot, edges, out, ext):
+        fwd2[half] = tall[half][:STACK].astype(jnp.bfloat16)
+        back1[half] = tall[half][STACK:].astype(jnp.bfloat16)
+        back2[half] = wide[half][:, :STACK].astype(jnp.bfloat16)
+        fwd1[half] = wide[half][:, STACK:].astype(jnp.bfloat16)
+    one = split(jnp.broadcast_to(bias1[...], (256, CHANNELS)))
+    wide1[...] = dot(lift, one[0], NT) + dot(lift, one[1], NT)
+    gap = counting((LOG, COEFFS), 0) - 8.0 * counting((LOG, COEFFS), 1)
+    pick = ((gap >= 0.0) & (gap < 8.0)).astype(jnp.float32).astype(jnp.bfloat16)
+    two = split(jnp.broadcast_to(bias2[...], (DEPTH, COEFFS)))
+    wide2[...] = dot(pick, two[0], NT) + dot(pick, two[1], NT)
+
+
+def pack_kernel(field, cot, other, out, ext):
     for m in range(3):
-        ext[m, 6:8, :] = edges[m, 2:4, :]
+        ext[m, 6:8, :] = other[m, 0, 62:64, :]
         ext[m, 8:72, :] = field[m, 0]
-        ext[m, 72:74, :] = edges[m, 0:2, :]
+        ext[m, 72:74, :] = other[m, 0, 0:2, :]
     for q in range(PLANES):
         for m in range(3):
             out[q, m * REACH : (m + 1) * REACH, :] = ext[m, 8 * q + 6 : 8 * q + 18, :]
@@ -482,7 +531,7 @@
         h_lo[:, cut] = parts[1]
         work[:, cut] = dot3((fwd2[0], fwd2[1]), parts)
     for x in range(PLANES):
-        total = bias2[:, :DEPTH]
+        total = bias2[...]
         for a in range(3):
             for e in range(3):
                 tap = a * 3 + e
@@ -544,12 +593,12 @@
             out[p * 4 + g] = total
 
 
-def gather_modes(recv, f, k, rows):
+def gather_modes(recv, f, k, first, rows):
     groups = lane_groups(rows)
     slot = 2 * f + k % 2
     total = None
     for g in range(4):
-        value = turn(recv[(k // 2) * 4 + g, 0:rows, :], BAND * (g - slot))
+        value = turn(recv[(k // 2) * 4 + g, first : first + rows, :], BAND * (g - slot))
         total = value if total is None else jnp.where(groups == g, value, total)
     return total
 
@@ -615,7 +664,10 @@
     modes = dot3((in_hi[...], in_lo[...]), data)
     fixed = leray([modes[m * ROWS : (m + 1) * ROWS] for m in range(3)])
     back = dot3((out_hi[...], out_lo[...]), split(jnp.concatenate(fixed, axis=0)))
-    out[...] = back.reshape(16, 40, DEPTH)
+    wide, rest = back[:512].reshape(16, 32, DEPTH), back[512:].reshape(16, 32, DEPTH)
+    low = lax.broadcasted_iota(jnp.int32, (16, 24, DEPTH), 2) < DEPTH // 2
+    out[:, 0:24, :] = jnp.where(low, wide[:, :24], rest[:, :24])
+    out[:, 24:32, :] = jnp.where(low[:, :8], wide[:, 24:], turn(rest[:, 24:], DEPTH // 2))
 
 
 def one_kernel(recv, in_hi, in_lo, out_hi, out_lo, out):
@@ -720,25 +772,21 @@
     field, grad, modes, rows6, hidden, weights, u_hi, u_lo, h_hi, h_lo, l_hi, l_lo, p_hi, p_lo, work, slope,
 ):
     back_z = (from_hi[...], from_lo[...])
-    for f in range(2):
-        for k in range(PLANES):
-            modes[k] = gather_modes(recv, f, k, 40)
-        flat = dot3(split(modes[...].reshape(PLANES * 40, DEPTH)), back_z)
-        modes[...] = flat.reshape(PLANES, 40, DEPTH)
-        for x, value in enumerate(mixed([modes[k] for k in range(PLANES)], mode_x.T)):
-            field[x, 0:40, :] = value
-            field[x, 40:48, :] = jnp.zeros((8, DEPTH), jnp.float32)
-        if f == 0:
-            network(field, fwd1, fwd2, bias1, bias2, hidden, weights, u_hi, u_lo, h_hi, h_lo, work)
-            for x in range(PLANES):
-                slope[x] = field[x]
-        else:
-            for x in range(PLANES):
-                for m in range(3):
-                    first = m * REACH + RIM
-                    grad[x, m * SLAB : (m + 1) * SLAB, :] = field[x, first : first + SLAB, :]
-    for x in range(PLANES):
-        field[x] = slope[x]
+    for k in range(PLANES):
+        modes[k, 0:32, :] = gather_modes(recv, 0, k, 0, 32)
+        modes[k, 32:40, :] = gather_modes(recv, 1, k, 24, 8)
+    flat = dot3(split(modes[...].reshape(PLANES * 40, DEPTH)), back_z)
+    modes[...] = flat.reshape(PLANES, 40, DEPTH)
+    for x, value in enumerate(mixed([modes[k] for k in range(PLANES)], mode_x.T)):
+        field[x, 0:40, :] = value
+        field[x, 40:48, :] = jnp.zeros((8, DEPTH), jnp.float32)
+    for k in range(PLANES):
+        grad[k] = gather_modes(recv, 1, k, 0, 24)
+    flat = dot3(split(grad[...].reshape(PLANES * 24, DEPTH)), back_z)
+    flat = flat.reshape(PLANES, 24, DEPTH)
+    for x, value in enumerate(mixed([flat[k] for k in range(PLANES)], mode_x.T)):
+        grad[x] = value
+    network(field, fwd1, fwd2, bias1, bias2, hidden, weights, u_hi, u_lo, h_hi, h_lo, work)
     pullback(
         field, grad, hidden, weights, back2, back1, u_hi, u_lo, h_hi, h_lo, l_hi, l_lo, p_hi, p_lo,
         work, slope, sums, ends, None,
@@ -764,7 +812,7 @@
     back_z = (from_hi[...], from_lo[...])
     for h in range(2):
         for k in range(PLANES):
-            modes[k] = gather_modes(recv, h, k, 16)
+            modes[k] = gather_modes(recv, h, k, 0, 16)
         flat = dot3(split(modes[...].reshape(PLANES * 16, DEPTH)), back_z)
         modes[...] = flat.reshape(PLANES, 16, DEPTH)
         for x, value in enumerate(mixed([modes[k] for k in range(PLANES)], mode_x.T)):
@@ -783,7 +831,7 @@
         out[x, 36:40, :] = jnp.zeros((4, DEPTH), jnp.float32)
     pack_grads(sums, ends, spread_t, mask, lift, count, pieces)
     for x in range(PLANES):
-        out[x, 40:80, :] = pieces[96:136, :]
+        out[x, 40:72, :] = pieces[96:128, :]
 
 
 def pack_grads(sums, ends, spread_t, mask, lift, count, pieces):
@@ -798,14 +846,17 @@
             if slot < 8:
                 pieces[96:123, :] += turn(pieces[c * 27 : c * 27 + 27, :], 16 * slot)
             else:
-                for third in range(3):
-                    first = c * 27 + third * 9
-                    pieces[123:132, :] += turn(pieces[first : first + 9, :], 16 * third)
+                for part in range(7):
+                    first = c * 27 + part * 4
+                    count_rows = min(4, c * 27 + 27 - first)
+                    pieces[123 : 123 + count_rows, :] += turn(
+                        pieces[first : first + count_rows, :], 16 * part
+                    )
     parts = split(ends[0:16, :])
     total = dot(parts[0], lift[...]) + dot(parts[1], lift[...])
     parts = split(ends[16:32, 0:LOG])
     total = total + dot(parts[0], count[...]) + dot(parts[1], count[...])
-    pieces[135:136, :] = total[0:1, :]
+    pieces[127:128, :] = total[0:1, :]
 
 
 def fold_kernel(recv, main, edge, ext):
@@ -814,22 +865,39 @@
     for q in range(PLANES):
         for m in range(3):
             ext[m, 8 * q + 6 : 8 * q + 18, :] += recv[q, m * REACH : (m + 1) * REACH, :]
-        block = recv[q, 40:80, :]
+        block = recv[q, 40:72, :]
         total = block if total is None else total + block
     for m in range(3):
         main[m, 0] = ext[m, 8:72, :]
         edge[m * 8 : m * 8 + 2, :] = ext[m, 72:74, :]
         edge[m * 8 + 2 : m * 8 + 4, :] = ext[m, 6:8, :]
         edge[m * 8 + 4 : m * 8 + 8, :] = jnp.zeros((4, DEPTH), jnp.float32)
-    edge[24:64, :] = total
-
-
-def last_kernel(main, edge, other, out, grads):
+    edge[24:56, :] = total
+
+
+def last_kernel(main, edge, other, out, first, end1, second, end2, turned):
     for m in range(3):
         out[m, 0] = main[m, 0]
         out[m, 0, 0:2, :] += other[m * 8 : m * 8 + 2, :]
         out[m, 0, 62:64, :] += other[m * 8 + 2 : m * 8 + 4, :]
-    grads[...] = edge[24:64, :] + other[24:64, :]
+    grads = edge[24:56, :] + other[24:56, :]
+    for slot in range(8):
+        turned[slot] = turn(grads, -16 * slot)
+    for b in range(3):
+        for a in range(3):
+            for e in range(3):
+                for i in range(9):
+                    row = (a * 3 + e) * 6 + i if i < 6 else 54 + (a * 3 + e) * 3 + i - 6
+                    slot, inner = b * 3 + row // 27, row % 27
+                    if slot == 8:
+                        slot, inner = inner // 4, 27 + inner % 4
+                    line = turned[slot, inner, 0:16]
+                    if i < 6:
+                        second[i * 9 + a * 3 + b, e, :] = line
+                    else:
+                        first[(i - 6) * 9 + a * 3 + b, e, :] = line
+    end1[...] = turned[0, 31:32, 0:16]
+    end2[...] = turned[1, 31:32, 0:6]
 
 
 def slab_device(velocity, cotangent, first_kernel, first_bias, second_kernel, second_bias):
@@ -840,30 +908,30 @@
     b16 = lambda *dims: pltpu.VMEM(dims, half)
     swap = [(0, 1), (1, 0)]
 
-    edges = jnp.concatenate([velocity[:, 0, :RIM], velocity[:, 0, -RIM:]], axis=1)
-    edges = lax.ppermute(edges, "py", swap)
-    packed = call(pack_kernel, shape(PLANES, 64, DEPTH), (velocity, cotangent, edges), [f32(3, 80, DEPTH)])
+    other = lax.ppermute(velocity, "py", swap)
+    packed = call(
+        pack_kernel, shape(PLANES, 64, DEPTH), (velocity, cotangent, other), [f32(3, 80, DEPTH)], 56
+    )
     recv = lax.all_to_all(packed, "px", 0, 0)
 
-    taps = jnp.concatenate(
-        [
-            jnp.transpose(second_kernel, (2, 4, 0, 3, 1)).reshape(54, 48),
-            jnp.transpose(first_kernel, (2, 4, 1, 3, 0)).reshape(27, 48),
-            jnp.zeros((15, 48), jnp.float32),
-        ]
-    )
-    fwd2, fwd1, back2, back1 = call(
+    fwd2, fwd1, back2, back1, bias1, bias2 = call(
         weights_kernel,
         [
             shape(2, STACK, HID, kind=half),
             shape(2, HID, STACK, kind=half),
             shape(2, HID, STACK, kind=half),
             shape(2, STACK, HID, kind=half),
+            shape(HID, 256),
+            shape(LOG, DEPTH),
         ],
-        (taps, c["spread"], c["spread_t"], c["mask"], c["mask_t"], c["lift"], c["lift_t"]),
-    )
-    bias1 = jnp.broadcast_to(jnp.repeat(first_bias, WIDE)[:, None], (HID, 256))
-    bias2 = jnp.broadcast_to(jnp.repeat(second_bias, SLAB)[:, None], (LOG, 256))
+        (
+            jnp.transpose(first_kernel, (1, 2, 3, 4, 0)).reshape(27, 3, CHANNELS),
+            jnp.transpose(second_kernel, (0, 2, 3, 4, 1)).reshape(54, 3, CHANNELS),
+            first_bias.reshape(1, CHANNELS),
+            second_bias.reshape(1, COEFFS),
+        ),
+        [f32(3, 96, CHANNELS)],
+    )
 
     stacks = lambda rows: [b16(rows, FLAT), b16(rows, FLAT)]
     sent, hidden, weights = call(
@@ -874,7 +942,7 @@
     )
     both = ("px", "py")
     moved_modes = lax.all_to_all(sent, both, 0, 0)
-    moved_modes = call(both_kernel, shape(16, 40, DEPTH), (moved_modes, *c["both_in"], *c["both_out"]))
+    moved_modes = call(both_kernel, shape(16, 32, DEPTH), (moved_modes, *c["both_in"], *c["both_out"]))
     moved_modes = lax.all_to_all(moved_modes, both, 0, 0)
 
     sent, sums, ends = call(
@@ -892,39 +960,38 @@
 
     sent = call(
         functools.partial(third_kernel_body, mode_x),
-        shape(PLANES, 80, DEPTH),
+        shape(PLANES, 72, DEPTH),
         (
             moved_modes, recv, hidden, weights, back2, back1, *c["from_z"], sums, ends,
             c["spread_t"], c["mask"], c["lift"], c["count"],
         ),
         [f32(PLANES, 24, DEPTH), f32(PLANES, 16, DEPTH)]
         + stacks(STACK) + stacks(HID) + stacks(STACK) + stacks(HID)
-        + [f32(STACK, FLAT), f32(PLANES, 48, DEPTH), f32(2 * STACK, HID), f32(32, HID), f32(136, DEPTH)],
+        + [f32(STACK, FLAT), f32(PLANES, 48, DEPTH), f32(2 * STACK, HID), f32(32, HID), f32(128, DEPTH)],
     )
     recv = lax.all_to_all(sent, "px", 0, 0)
     main, edge = call(
-        fold_kernel, [shape(3, 1, 64, DEPTH), shape(64, DEPTH)], (recv,), [f32(3, 80, DEPTH)]
+        fold_kernel, [shape(3, 1, 64, DEPTH), shape(56, DEPTH)], (recv,), [f32(3, 80, DEPTH)]
     )
     other = lax.ppermute(edge, "py", swap)
-    grad_velocity, grads = call(
-        last_kernel, [shape(3, 1, 64, DEPTH), shape(40, DEPTH)], (main, edge, other)
-    )
-
-    def piece(b, kind):
-        slot = b * 3 + kind
-        if slot < 8:
-            return grads[0:27, 16 * slot : 16 * slot + 16]
-        return jnp.concatenate([grads[27:36, 16 * i : 16 * i + 16] for i in range(3)])
-
-    first = jnp.stack([piece(b, 2) for b in range(3)]).reshape(3, 3, 3, 3, CHANNELS)
-    second = jnp.stack([jnp.concatenate([piece(b, 0), piece(b, 1)]) for b in range(3)])
-    second = second.reshape(3, 3, 3, COEFFS, CHANNELS)
+    grad_velocity, first, end1, second, end2 = call(
+        last_kernel,
+        [
+            shape(3, 1, 64, DEPTH),
+            shape(27, 3, CHANNELS),
+            shape(1, CHANNELS),
+            shape(54, 3, CHANNELS),
+            shape(1, COEFFS),
+        ],
+        (main, edge, other),
+        [f32(8, 32, DEPTH)],
+    )
     return (
         grad_velocity,
-        jnp.transpose(first, (4, 3, 1, 0, 2)),
-        grads[39, 0:16],
-        jnp.transpose(second, (3, 4, 1, 0, 2)),
-        grads[39, 16:22],
+        jnp.transpose(first.reshape(3, 3, 3, 3, CHANNELS), (4, 0, 1, 2, 3)),
+        end1.reshape(CHANNELS),
+        jnp.transpose(second.reshape(COEFFS, 3, 3, 3, CHANNELS), (0, 4, 1, 2, 3)),
+        end2.reshape(COEFFS),
     )
 
 

time: 134 us -> 104 us (0.78)
  Pallas kernels: 38.3 us -> 22.6 us
  blocking collectives: 70.6 us -> 60.1 us
  local copies, waits for them, and re-layouts: 12.8 us -> 6.66 us
  waiting for transfers between devices: 2.24 us -> 4.92 us
    pallas_call x9, Pallas kernels: 38.3 us -> 22.6 us  [call(): pl.pallas_call(kernel, out_shape=outs, in_specs=[pl.BlockSpec(memory_spac...]
    all_to_all x2, blocking collectives: 27.4 us -> 23.2 us  [slab_device(): moved_modes = lax.all_to_all(moved_modes, both, 0, 0)]
    unnamed x8 -> x52, local copies, waits for them, and re-layouts: 2.51 us -> 6.66 us
    all_to_all x2, blocking collectives: 28.4 us -> 24.3 us  [slab_device(): moved_modes = lax.all_to_all(sent, both, 0, 0)]
    squeeze x3 -> x0, local copies, waits for them, and re-layouts: 3.18 us -> none  [the longest x1 1.26 us: slab_device(): grads[39, 16:22]]
    broadcast_in_dim x7 -> x0, local copies, waits for them, and re-layouts: 3.06 us -> none  [the longest x3 1.55 us: slab_device(): bias1 = jnp.broadcast_to(jnp.repeat(first_bias, WIDE)[:, None], (HID, 256))]
    all_to_all x1, waiting for transfers between devices: 0.01 us -> 2.58 us  [slab_device(): recv = lax.all_to_all(packed, 'px', 0, 0)]
    all_to_all x1, blocking collectives: 14.8 us -> 12.7 us  [slab_device(): recv = lax.all_to_all(sent, 'px', 0, 0)]
  transfers between devices with their start and end apart: 3 -> 3, of which waited for: 2 -> 3; matrix products, arithmetic and copies ran while one was open for 3% -> 0% of each run, Pallas kernels for 4% -> 3%
where the time goes in v2:
time: 104 us; the launch traced here: 103 us
  blocking collectives  60.1 us (58%)
  Pallas kernels  22.6 us (22%)
  starting transfers between devices  7.88 us (8%)
  local copies, waits for them, and re-layouts  6.66 us (6%)
  waiting for transfers between devices  4.92 us (5%)
    all_to_all x2, blocking collectives, slab_device(): moved_modes = lax.all_to_all(sent, both, 0, 0)  24.3 us
    all_to_all x2, blocking collectives, slab_device(): moved_modes = lax.all_to_all(moved_modes, both, 0, 0)  23.2 us
    pallas_call x9, Pallas kernels, call(): pl.pallas_call(kernel, out_shape=outs, in_specs=[pl.BlockSpec(memory_spac...  22.6 us
    all_to_all x1, blocking collectives, slab_device(): recv = lax.all_to_all(sent, 'px', 0, 0)  12.7 us
    all_to_all x1, starting transfers between devices, slab_device(): recv = lax.all_to_all(packed, 'px', 0, 0)  7.29 us
    unnamed x52, local copies, waits for them, and re-layouts  6.66 us
    all_to_all x1, waiting for transfers between devices, slab_device(): recv = lax.all_to_all(packed, 'px', 0, 0)  2.58 us
  transfers between devices with their start and end apart: 3, of which 3 were waited for; matrix products, arithmetic and copies ran while one was open for 0% of the time, Pallas kernels for 3%

profile of v2, /device:TPU:0, one launch (start us, length us, event | category | flops | bytes accessed | tf_op | source)
XLA Modules:
  0.0 103.0 jit_solution(6641316000911996140)
XLA Ops:
  1.1 1.2 %collective-permute-done.other = f32[3,1,64,128]{3,2,1,0:T(8,128)S(1)} collective-permute-done((f32[3,1,64,128]{3,2,1,0:T(8,128)}, f32[3,1,64,128]{3,2,1,0:T(8,128)S(1)}, u32[]{:S(2)}, u32[]{:S(2)}) %collective-permute-start) | collective-permute-done | bytes 98336 | tf_op jit(solution)/shard_map/ppermute | solution.py:911
  2.9 1.7 %shard_map.245 = f32[8,64,128]{2,1,0:T(8,128)} custom-call(f32[3,1,64,128]{3,2,1,0:T(8,128)} %field.1, f32[3,1,64,128]{3,2,1,0:T(8,128)} %cot.1, f32[3,1,64,128]{3,2,1,0:T(8,128)} %copy-done.25), custom_call_target="tpu_custom_call" | custom-call | tf_op jit(solution)/shard_map/pallas_call | solution.py:415
  4.7 7.3 %all-to-all-start = ((f32[8,64,128]{2,1,0:T(8,128)}), f32[8,64,128]{2,1,0:T(8,128)S(1)}, u32[]{:S(2)}, u32[]{:S(2)}) async-start(f32[8,64,128]{2,1,0:T(8,128)} %shard_map.245), calls=%async_computation | async-start | bytes 524288 | tf_op jit(solution)/shard_map/all_to_all | solution.py:915
  12.0 0.9 copy-done.16
  12.9 0.8 copy-done.20
  13.7 0.7 copy-done.23
  14.3 0.7 copy-done.24
  15.0 3.0 %shard_map.246 = (bf16[2,432,160]{2,1,0:T(8,128)(2,1)S(1)}, bf16[2,160,432]{2,1,0:T(8,128)(2,1)S(1)}, bf16[2,160,432]{2,1,0:T(8,128)(2,1)S(1)}, bf16[2,432,160]{...) custom-call(f32[27,3,16]{2,1,0:T(4,128)S(1)} %bitcast.17, f32[54,3,16]{2,1,0:T(4,128)S(1)} %bitcast.16, ...), custom_call_target="tpu_custom_call" | custom-call | tf_op jit(solution)/shard_map/pallas_call | solution.py:415
  18.6 2.6 %all-to-all-done.recv.field = f32[8,64,128]{2,1,0:T(8,128)S(1)} async-done(((f32[8,64,128]{2,1,0:T(8,128)}), f32[8,64,128]{2,1,0:T(8,128)S(1)}, u32[]{:S(2)}, u32[]{:S(2)}) %all-to-all-start) | async-done | bytes 262176 | tf_op jit(solution)/shard_map/all_to_all | solution.py:915
  21.2 0.8 copy-done.12
  22.0 0.8 copy-done.14
  22.8 0.7 copy-done.18
  23.5 2.3 %shard_map.247 = (f32[16,24,128]{2,1,0:T(8,128)S(1)}, f32[160,1024]{1,0:T(8,128)S(1)}, f32[48,1024]{1,0:T(8,128)S(1)}) custom-call(f32[8,64,128]{2,1,0:T(8,128)S(1)} %all-to-all-done.recv.field, bf16[2,160,432]{2,1,0:T(8,128)(2,1)S(1)} %get-tuple-element.24.fwd1, bf16[2,432,160]{2,1,0:T(8,128)(2,1)S(1)} %get-tuple-element.25.fwd2, ...), custom_call_target="tpu_custom_call" | custom-call | tf_op jit(solution)/shard_map/pallas_call | solution.py:415
  25.9 12.5 %all_to_all.30.recv = f32[16,24,128]{2,1,0:T(8,128)S(1)} all-to-all(f32[16,24,128]{2,1,0:T(8,128)S(1)} %get-tuple-element.28), channel_id=1, replica_groups=mesh['groups'=2,'px'=8,'py'=2] {'px','py'}, dimensions={0} | all-to-all | bytes 393216 | tf_op jit(solution)/shard_map/all_to_all | solution.py:944
  38.4 1.5 %shard_map.248 = f32[16,32,128]{2,1,0:T(8,128)S(1)} custom-call(f32[16,24,128]{2,1,0:T(8,128)S(1)} %all_to_all.30.recv, bf16[384,384]{1,0:T(8,128)(2,1)S(1)} %copy-done.8, bf16[384,384]{1,0:T(8,128)(2,1)S(1)} %copy-done.7, bf16[1024,384]{1,0:T(8,128)(2,1)S(1)} %copy-done.2, bf16[1024,384]{1,0:T(8,128)(2,1)S(1)} %copy-done.1), custom_call_target="tpu_custom_call" | custom-call | tf_op jit(solution)/shard_map/pallas_call | solution.py:415
  39.9 12.6 %all_to_all.31.recv = f32[16,32,128]{2,1,0:T(8,128)S(1)} all-to-all(f32[16,32,128]{2,1,0:T(8,128)S(1)} %shard_map.248), channel_id=1, replica_groups=mesh['groups'=2,'px'=8,'py'=2] {'px','py'}, dimensions={0} | all-to-all | bytes 524288 | tf_op jit(solution)/shard_map/all_to_all | solution.py:946
  52.6 6.0 %shard_map.249 = (f32[16,24,128]{2,1,0:T(8,128)S(1)}, f32[864,160]{1,0:T(8,128)S(1)}, f32[32,160]{1,0:T(8,128)S(1)}) custom-call(f32[16,32,128]{2,1,0:T(8,128)S(1)} %all_to_all.31.recv, bf16[2,160,432]{2,1,0:T(8,128)(2,1)S(1)} %get-tuple-element.24.fwd1, bf16[2,432,160]{2,1,0:T(8,128)(2,1)S(1)} %get-tuple-element.25.fwd2, ...), custom_call_target="tpu_custom_call" | custom-call | tf_op jit(solution)/shard_map/pallas_call | solution.py:415
  58.7 11.8 %all_to_all.32.recv = f32[16,24,128]{2,1,0:T(8,128)S(1)} all-to-all(f32[16,24,128]{2,1,0:T(8,128)S(1)} %get-tuple-element.31), channel_id=1, replica_groups=mesh['groups'=2,'px'=8,'py'=2] {'px','py'}, dimensions={0} | all-to-all | bytes 393216 | tf_op jit(solution)/shard_map/all_to_all | solution.py:957
  70.5 1.4 %shard_map.250 = f32[16,16,128]{2,1,0:T(8,128)S(1)} custom-call(f32[16,24,128]{2,1,0:T(8,128)S(1)} %all_to_all.32.recv, bf16[768,384]{1,0:T(8,128)(2,1)S(1)} %copy-done.4, bf16[768,384]{1,0:T(8,128)(2,1)S(1)} %copy-done.3, bf16[512,384]{1,0:T(8,128)(2,1)S(1)} %copy-done.6, bf16[512,384]{1,0:T(8,128)(2,1)S(1)} %copy-done.5), custom_call_target="tpu_custom_call" | custom-call | tf_op jit(solution)/shard_map/pallas_call | solution.py:415
  72.0 10.5 %all_to_all.33.recv = f32[16,16,128]{2,1,0:T(8,128)S(1)} all-to-all(f32[16,16,128]{2,1,0:T(8,128)S(1)} %shard_map.250), channel_id=1, replica_groups=mesh['groups'=2,'px'=8,'py'=2] {'px','py'}, dimensions={0} | all-to-all | bytes 262144 | tf_op jit(solution)/shard_map/all_to_all | solution.py:959
  82.5 5.6 %shard_map.251 = f32[8,72,128]{2,1,0:T(8,128)S(1)} custom-call(f32[16,16,128]{2,1,0:T(8,128)S(1)} %all_to_all.33.recv, f32[8,64,128]{2,1,0:T(8,128)S(1)} %all-to-all-done.recv.field, f32[160,1024]{1,0:T(8,128)S(1)} %get-tuple-element.32.hidden, f32[48,1024]{1,0:T(8,128)S(1)} %get-tuple-element.33.weights, bf16[2,160,432]{2,1,0:T(8,128)(2,1)S(1)} %get-tuple-element.29.back2, ...), custom_call_target="tpu_custom_call" | custom-call | tf_op jit(solution)/shard_map/pallas_call | solution.py:415
  88.1 12.7 %all_to_all.34.recv = f32[8,72,128]{2,1,0:T(8,128)S(1)} all-to-all(f32[8,72,128]{2,1,0:T(8,128)S(1)} %shard_map.251), channel_id=1, replica_groups=mesh['groups'=2,'px'=8,'py'=2] {'px'}, dimensions={0} | all-to-all | bytes 589824 | tf_op jit(solution)/shard_map/all_to_all | solution.py:972
  100.9 1.2 %collective-permute-done.1.other = f32[56,128]{1,0:T(8,128)S(1)} collective-permute-done((f32[56,128]{1,0:T(8,128)S(1)}, f32[56,128]{1,0:T(8,128)S(1)}, u32[]{:S(2)}, u32[]{:S(2)}) %collective-permute-start.1) | collective-permute-done | bytes 28704 | tf_op jit(solution)/shard_map/ppermute | solution.py:976
  102.1 0.8 shard_map.253
  (48 shorter events, 2.0 us)
Async XLA Ops:
  0.6 1.7 %collective-permute-start = (f32[3,1,64,128]{3,2,1,0:T(8,128)}, f32[3,1,64,128]{3,2,1,0:T(8,128)S(1)}, u32[]{:S(2)}, u32[]{:S(2)}) collective-permute-start(f32[3,1,64,128]{3,2,1,0:T(8,128)} %field.1), channel_id=1, source_target_pairs={{0,1},{1,0},{2,3},{3,2},{4,5},{5,4},{6,7},{7,6},{8,9},{9,8},{10,11... | collective-permute-start | bytes 294920 | tf_op jit(solution)/shard_map/ppermute | solution.py:911
  4.7 33.7 %copy-start.1 = (bf16[1024,384]{1,0:T(8,128)(2,1)S(1)}, bf16[1024,384]{1,0:T(8,128)(2,1)}, u32[]{:S(2)}) copy-start(bf16[1024,384]{1,0:T(8,128)(2,1)} %constant.37.clone.out_lo) | copy-start | bytes 2359300
  4.7 33.7 %copy-start.2 = (bf16[1024,384]{1,0:T(8,128)(2,1)S(1)}, bf16[1024,384]{1,0:T(8,128)(2,1)}, u32[]{:S(2)}) copy-start(bf16[1024,384]{1,0:T(8,128)(2,1)} %constant.36.clone.out_hi) | copy-start | bytes 2359300
  4.7 16.5 %all-to-all-start = ((f32[8,64,128]{2,1,0:T(8,128)}), f32[8,64,128]{2,1,0:T(8,128)S(1)}, u32[]{:S(2)}, u32[]{:S(2)}) async-start(f32[8,64,128]{2,1,0:T(8,128)} %shard_map.245), calls=%async_computation | async-start | bytes 524288 | tf_op jit(solution)/shard_map/all_to_all | solution.py:915
  12.0 0.9 copy-start.16
  12.8 0.8 copy-start.20
  21.2 17.2 %copy-start.7 = (bf16[384,384]{1,0:T(8,128)(2,1)S(1)}, bf16[384,384]{1,0:T(8,128)(2,1)}, u32[]{:S(2)}) copy-start(bf16[384,384]{1,0:T(8,128)(2,1)} %constant.35.clone.in_lo) | copy-start | bytes 884740
  21.2 17.2 %copy-start.8 = (bf16[384,384]{1,0:T(8,128)(2,1)S(1)}, bf16[384,384]{1,0:T(8,128)(2,1)}, u32[]{:S(2)}) copy-start(bf16[384,384]{1,0:T(8,128)(2,1)} %constant.34.clone.in_hi) | copy-start | bytes 884740
  21.2 0.8 copy-start.12
  22.0 0.8 copy-start.14
  38.4 14.2 %copy-start.10 = (bf16[128,128]{1,0:T(8,128)(2,1)S(1)}, bf16[128,128]{1,0:T(8,128)(2,1)}, u32[]{:S(2)}) copy-start(bf16[128,128]{1,0:T(8,128)(2,1)} %constant.39.clone.from_lo) | copy-start | bytes 98308
  38.4 14.2 %copy-start.11 = (bf16[128,128]{1,0:T(8,128)(2,1)S(1)}, bf16[128,128]{1,0:T(8,128)(2,1)}, u32[]{:S(2)}) copy-start(bf16[128,128]{1,0:T(8,128)(2,1)} %constant.38.clone.from_hi) | copy-start | bytes 98308
  38.4 14.2 %copy-start.13 = (bf16[128,128]{1,0:T(8,128)(2,1)S(1)}, bf16[128,128]{1,0:T(8,128)(2,1)}, u32[]{:S(2)}) copy-start(bf16[128,128]{1,0:T(8,128)(2,1)} %constant.33.clone.z_lo.to_lo) | copy-start | bytes 98308
  38.4 14.2 %copy-start.15 = (bf16[128,128]{1,0:T(8,128)(2,1)S(1)}, bf16[128,128]{1,0:T(8,128)(2,1)}, u32[]{:S(2)}) copy-start(bf16[128,128]{1,0:T(8,128)(2,1)} %constant.32.clone.z_hi.to_hi) | copy-start | bytes 98308
  38.4 14.2 %copy-start.19 = (f32[48,128]{1,0:T(8,128)S(1)}, f32[48,128]{1,0:T(8,128)}, u32[]{:S(2)}) copy-start(f32[48,128]{1,0:T(8,128)} %copy-done.17) | copy-start | bytes 73732
  52.5 17.9 %copy-start.3 = (bf16[768,384]{1,0:T(8,128)(2,1)S(1)}, bf16[768,384]{1,0:T(8,128)(2,1)}, u32[]{:S(2)}) copy-start(bf16[768,384]{1,0:T(8,128)(2,1)} %constant.41.clone.in_lo) | copy-start | bytes 1769476
  52.6 17.9 %copy-start.4 = (bf16[768,384]{1,0:T(8,128)(2,1)S(1)}, bf16[768,384]{1,0:T(8,128)(2,1)}, u32[]{:S(2)}) copy-start(bf16[768,384]{1,0:T(8,128)(2,1)} %constant.40.clone.in_hi) | copy-start | bytes 1769476
  52.6 17.9 %copy-start.5 = (bf16[512,384]{1,0:T(8,128)(2,1)S(1)}, bf16[512,384]{1,0:T(8,128)(2,1)}, u32[]{:S(2)}) copy-start(bf16[512,384]{1,0:T(8,128)(2,1)} %constant.43.clone.out_lo) | copy-start | bytes 1179652
  52.6 17.9 %copy-start.6 = (bf16[512,384]{1,0:T(8,128)(2,1)S(1)}, bf16[512,384]{1,0:T(8,128)(2,1)}, u32[]{:S(2)}) copy-start(bf16[512,384]{1,0:T(8,128)(2,1)} %constant.42.clone.out_hi) | copy-start | bytes 1179652
  70.5 12.0 %copy-start = (bf16[3,864,160]{2,1,0:T(8,128)(2,1)S(1)}, bf16[3,864,160]{2,1,0:T(8,128)(2,1)}, u32[]{:S(2)}) copy-start(bf16[3,864,160]{2,1,0:T(8,128)(2,1)} %constant.45.clone.mask) | copy-start | bytes 2488324
  70.5 12.0 %copy-start.9 = (bf16[96,864]{1,0:T(8,128)(2,1)S(1)}, bf16[96,864]{1,0:T(8,128)(2,1)}, u32[]{:S(2)}) copy-start(bf16[96,864]{1,0:T(8,128)(2,1)} %constant.44.clone.spread_t) | copy-start | bytes 497668
  70.5 12.0 %copy-start.21 = (bf16[160,128]{1,0:T(8,128)(2,1)S(1)}, bf16[160,128]{1,0:T(8,128)(2,1)}, u32[]{:S(2)}) copy-start(bf16[160,128]{1,0:T(8,128)(2,1)} %constant.46.clone.lift) | copy-start | bytes 122884
  70.5 12.0 %copy-start.22 = (bf16[48,128]{1,0:T(8,128)(2,1)S(1)}, bf16[48,128]{1,0:T(8,128)(2,1)}, u32[]{:S(2)}) copy-start(bf16[48,128]{1,0:T(8,128)(2,1)} %constant.47.clone.count) | copy-start | bytes 36868
  100.9 1.3 %collective-permute-start.1 = (f32[56,128]{1,0:T(8,128)S(1)}, f32[56,128]{1,0:T(8,128)S(1)}, u32[]{:S(2)}, u32[]{:S(2)}) collective-permute-start(f32[56,128]{1,0:T(8,128)S(1)} %get-tuple-element.37.edge), channel_id=1, source_target_pairs={{0,1},{1,0},{2,3},{3,2},{4,5},{5,4},{6,7},{7,6},{8,9},{9,8},{10,11... | collective-permute-start | bytes 86024 | tf_op jit(solution)/shard_map/ppermute | solution.py:976
  (5 other events, 3.3 us)

commit v3 on v2

--- a/solution.py
+++ b/solution.py
@@ -296,6 +296,10 @@
 HID = CHANNELS * WIDE
 LOG = COEFFS * SLAB
 STACK = 9 * 48
+TALL = STACK + 16
+BROAD = HID + 16
+DEEP = 3 * HID + 16
+PLACE = (0, 2, 1)
 FLAT = PLANES * DEPTH
 NN = ((1,), (0,))
 NT = ((1,), (1,))
@@ -309,6 +313,10 @@
     rows += [np.cos(half * angle) / np.sqrt(count)]
     rows += [np.sqrt(2.0 / count) * np.sin(k * angle) for k in range(1, half)]
     return np.stack(rows)
+
+
+def stacked_table(table):
+    return np.concatenate(halves(table))
 
 
 def halves(table):
@@ -350,8 +358,8 @@
     one_in = np.concatenate([table(24, -RIM, 6), table(24, -RIM + 6, 6)])
     one_out = np.concatenate([table(16, 0, 4).T, table(16, 4, 4).T])
 
-    spread = np.zeros((2 * STACK, 96))
-    mask = np.zeros((3, 2 * STACK, HID))
+    spread = np.zeros((STACK + TALL, 96))
+    mask = np.zeros((3, STACK + TALL, BROAD))
     for tap in range(9):
         for o in range(COEFFS):
             for q in range(SLAB):
@@ -366,19 +374,19 @@
                 for b in range(3):
                     if 0 <= r - b < WIDE:
                         mask[b, row, np.arange(CHANNELS) * WIDE + r - b] = 1.0
-    lift = np.zeros((HID, 128))
+    lift = np.zeros((BROAD, 128))
     lift[np.arange(HID), np.arange(HID) // WIDE] = 1.0
     count = np.zeros((LOG, 128))
     count[np.arange(LOG), 16 + np.arange(LOG) // SLAB] = 1.0
     half = jnp.bfloat16
     return dict(
         mode_x=mode_x,
-        to_z=halves(mode_z.T),
-        from_z=halves(mode_z),
-        both_in=halves(both_in),
-        both_out=halves(both_out),
-        one_in=halves(one_in),
-        one_out=halves(one_out),
+        to_z=np.stack(halves(mode_z.T)),
+        from_z=np.stack(halves(mode_z)),
+        both_in=stacked_table(both_in),
+        both_out=stacked_table(both_out),
+        one_in=stacked_table(one_in),
+        one_out=stacked_table(one_out),
         spread_t=np.ascontiguousarray(spread.T).astype(half),
         mask=mask.astype(half),
         lift=lift.astype(half),
@@ -395,8 +403,14 @@
     return high, (value - high.astype(jnp.float32)).astype(jnp.bfloat16)
 
 
-def dot3(left, right, dims=NN):
-    return dot(left[0], right[0], dims) + (dot(left[0], right[1], dims) + dot(left[1], right[0], dims))
+def dot_stacked(left, right, dims=NN):
+    rows = left.shape[0] // 2
+    main = dot(left[...], right[0], dims)
+    return main[:rows] + (main[rows:] + dot(left[0:rows, :], right[1], dims))
+
+
+def stacked(value):
+    return jnp.concatenate(split(value), axis=0)
 
 
 def turn(value, shift):
@@ -409,21 +423,28 @@
     return slice(x * DEPTH, (x + 1) * DEPTH)
 
 
-def call(kernel, outs, args, scratch=(), room=16):
+def call(kernel, outs, args, scratch=(), room=16, away=()):
     single = not isinstance(outs, (list, tuple))
-    shapes = [outs] if single else outs
+    vmem = pl.BlockSpec(memory_space=pltpu.VMEM)
+    cost = pl.CostEstimate(flops=1, bytes_accessed=1, transcendentals=0) if away else None
     return pl.pallas_call(
         kernel,
         out_shape=outs,
-        in_specs=[pl.BlockSpec(memory_space=pltpu.VMEM)] * len(args),
-        out_specs=(
-            pl.BlockSpec(memory_space=pltpu.VMEM)
-            if single
-            else [pl.BlockSpec(memory_space=pltpu.VMEM)] * len(shapes)
-        ),
+        in_specs=[
+            pl.BlockSpec(memory_space=pltpu.HBM) if i in away else vmem for i in range(len(args))
+        ],
+        out_specs=vmem if single else [vmem] * len(outs),
         scratch_shapes=list(scratch),
+        cost_estimate=cost,
         compiler_params=pltpu.CompilerParams(vmem_limit_bytes=room * 2**20),
     )(*args)
+
+
+def fetch(pairs, sems):
+    copies = [pltpu.make_async_copy(src, dst, sems.at[i]) for i, (src, dst) in enumerate(pairs)]
+    for copy in copies:
+        copy.start()
+    return copies
 
 
 def shape(*dims, kind=jnp.float32):
@@ -463,8 +484,16 @@
     return picks.astype(jnp.float32).astype(half), offset, lift.astype(jnp.float32).astype(half)
 
 
-def weights_kernel(taps1, taps2, bias1, bias2, fwd2, fwd1, back2, back1, wide1, wide2, blocks):
+def weights_kernel(
+    far1, far2, far3, far4, z_in, fwd2, fwd1, back2, back1, z_out, blocks, taps1, taps2, bias1, bias2, sems
+):
+    copies = fetch([(far1, taps1), (far2, taps2), (far3, bias1), (far4, bias2)], sems)
     blocks[...] = jnp.zeros_like(blocks)
+    z_out[...] = z_in[...]
+    spread, offset, lift = band_tables(True)
+    spread_t, offset_t, lift_t = band_tables(False)
+    for copy in copies:
+        copy.wait()
     for b in range(3):
         for a in range(3):
             for e in range(3):
@@ -473,34 +502,44 @@
                     blocks[b, tap * 6 + o, :] = taps2[o * 9 + a * 3 + b, e, :]
                 for m in range(3):
                     blocks[b, 54 + tap * 3 + m, :] = taps1[m * 9 + a * 3 + b, e, :]
-    spread, offset, lift = band_tables(True)
-    spread_t, offset_t, lift_t = band_tables(False)
     tall = [jnp.zeros((2 * STACK, HID), jnp.float32)] * 2
-    wide = [jnp.zeros((HID, 2 * STACK), jnp.float32)] * 2
+    flat = [jnp.zeros((HID, 2 * STACK), jnp.float32)] * 2
     for b in range(3):
         for half, block in enumerate(split(blocks[b])):
             rows = dot(spread, block).astype(jnp.bfloat16)
             tall[half] = jnp.where(offset == float(b), dot(rows, lift_t), tall[half])
             cols = dot(lift, block, NT).astype(jnp.bfloat16)
-            wide[half] = jnp.where(offset_t == float(b), dot(cols, spread_t), wide[half])
+            flat[half] = jnp.where(offset_t == float(b), dot(cols, spread_t), flat[half])
     for half in range(2):
-        fwd2[half] = tall[half][:STACK].astype(jnp.bfloat16)
-        back1[half] = tall[half][STACK:].astype(jnp.bfloat16)
-        back2[half] = wide[half][:, :STACK].astype(jnp.bfloat16)
-        fwd1[half] = wide[half][:, STACK:].astype(jnp.bfloat16)
-    one = split(jnp.broadcast_to(bias1[...], (256, CHANNELS)))
-    wide1[...] = dot(lift, one[0], NT) + dot(lift, one[1], NT)
+        rows, cols = slice(half * 144, half * 144 + 144), slice(half * HID, half * HID + HID)
+        for a in range(3):
+            first = PLACE[a] * HID
+            part = tall[half][a * 144 : a * 144 + 144]
+            fwd2[rows, first : first + HID] = part.astype(jnp.bfloat16)
+            part = tall[half][STACK + a * 144 : STACK + a * 144 + 144]
+            back1[rows, first : first + HID] = part.astype(jnp.bfloat16)
+        back2[cols, :] = flat[half][:, :STACK].astype(jnp.bfloat16)
+        fwd1[cols, 0:STACK] = flat[half][:, STACK:].astype(jnp.bfloat16)
     gap = counting((LOG, COEFFS), 0) - 8.0 * counting((LOG, COEFFS), 1)
     pick = ((gap >= 0.0) & (gap < 8.0)).astype(jnp.float32).astype(jnp.bfloat16)
-    two = split(jnp.broadcast_to(bias2[...], (DEPTH, COEFFS)))
-    wide2[...] = dot(pick, two[0], NT) + dot(pick, two[1], NT)
-
-
-def pack_kernel(field, cot, other, out, ext):
+    first = counting((HID, 16), 1) < 1.0
+    second = counting((LOG, 16), 1) < 1.0
+    one = split(jnp.broadcast_to(bias1[...], (16, CHANNELS)))
+    two = split(jnp.broadcast_to(bias2[...], (16, COEFFS)))
+    fwd2[:, 3 * HID :] = jnp.zeros((288, 16), jnp.bfloat16)
+    back1[:, 3 * HID :] = jnp.zeros((288, 16), jnp.bfloat16)
+    for half in range(2):
+        value = jnp.where(first, dot(lift, one[half], NT), 0.0)
+        fwd1[half * HID : half * HID + HID, STACK:] = value.astype(jnp.bfloat16)
+        value = jnp.where(second, dot(pick, two[half], NT), 0.0)
+        start = half * 144 + LOG
+        fwd2[start : start + LOG, 3 * HID :] = value.astype(jnp.bfloat16)
+
+
+def pack_kernel(field, cot, out, ext):
+    ext[...] = jnp.zeros_like(ext)
     for m in range(3):
-        ext[m, 6:8, :] = other[m, 0, 62:64, :]
         ext[m, 8:72, :] = field[m, 0]
-        ext[m, 72:74, :] = other[m, 0, 0:2, :]
     for q in range(PLANES):
         for m in range(3):
             out[q, m * REACH : (m + 1) * REACH, :] = ext[m, 8 * q + 6 : 8 * q + 18, :]
@@ -508,34 +547,69 @@
         out[q, 60:64, :] = jnp.zeros((4, DEPTH), jnp.float32)
 
 
-def stack_field(field, high, low):
+def rim_kernel(packed, other, out):
+    out[...] = packed[...]
+    for m in range(3):
+        out[0, m * REACH : m * REACH + 2, :] = other[m, 0, 62:64, :]
+        out[PLANES - 1, m * REACH + 10 : m * REACH + 12, :] = other[m, 0, 0:2, :]
+
+
+def unit_row():
+    row = lax.broadcasted_iota(jnp.int32, (16, FLAT), 0)
+    return jnp.where(row == 0, 1.0, 0.0).astype(jnp.bfloat16)
+
+
+def stack_planes(value, first, sign, high, low):
+    parts = split(value)
+    for i in range(value.shape[1] // DEPTH):
+        for a in range(3):
+            rows = slice(PLACE[a] * HID, PLACE[a] * HID + HID)
+            to = plane(first + i + sign * (a - 1))
+            high[rows, to] = parts[0][:, i * DEPTH : (i + 1) * DEPTH]
+            low[rows, to] = parts[1][:, i * DEPTH : (i + 1) * DEPTH]
+
+
+def finish_planes(high, low):
+    high[3 * HID :, :] = unit_row()
+    low[3 * HID :, :] = jnp.zeros((16, FLAT), jnp.bfloat16)
+
+
+def stack_logits(whole, x, l_taps):
+    for e in range(3):
+        parts = split(turn(whole, e - 1))
+        for a in range(3):
+            for half in range(2):
+                first = half * STACK + (a * 3 + e) * 48
+                l_taps[first : first + 48, plane(x + a - 1)] = parts[half]
+
+
+def stack_field(field, taps):
     for x in range(PLANES):
         whole = field[x, 0:48, :]
         for e in range(3):
             parts = split(turn(whole, 1 - e))
             for a in range(3):
                 rows = slice((a * 3 + e) * 48, (a * 3 + e) * 48 + 48)
-                high[rows, plane(x - a + 1)] = parts[0]
-                low[rows, plane(x - a + 1)] = parts[1]
-
-
-def network(field, fwd1, fwd2, bias1, bias2, hidden, weights, u_hi, u_lo, h_hi, h_lo, work):
-    stack_field(field, u_hi, u_lo)
+                taps[rows, plane(x - a + 1)] = parts[0]
+                taps[TALL + rows.start : TALL + rows.stop, plane(x - a + 1)] = parts[1]
+    taps[STACK:TALL, :] = unit_row()
+    taps[TALL + STACK :, :] = jnp.zeros((16, FLAT), jnp.bfloat16)
+
+
+def network(field, fwd1, fwd2, hidden, weights, u_taps, h_hi, h_lo, work):
+    stack_field(field, u_taps)
+    finish_planes(h_hi, h_lo)
     for pair in range(4):
         cut = slice(pair * 256, pair * 256 + 256)
-        out = dot3((fwd1[0], fwd1[1]), (u_hi[:, cut], u_lo[:, cut]))
-        value = jnp.tanh(out + bias1[...])
+        value = jnp.tanh(dot_stacked(fwd1, (u_taps[0:TALL, cut], u_taps[TALL:, cut])))
         hidden[:, cut] = value
-        parts = split(value)
-        h_hi[:, cut] = parts[0]
-        h_lo[:, cut] = parts[1]
-        work[:, cut] = dot3((fwd2[0], fwd2[1]), parts)
+        stack_planes(value, 2 * pair, -1, h_hi, h_lo)
+    for pair in range(4):
+        cut = slice(pair * 256, pair * 256 + 256)
+        work[:, cut] = dot_stacked(fwd2, (h_hi[:, cut], h_lo[:, cut]))
     for x in range(PLANES):
-        total = bias2[...]
-        for a in range(3):
-            for e in range(3):
-                tap = a * 3 + e
-                total = total + turn(work[tap * 48 : tap * 48 + 48, plane(x + a - 1)], 1 - e)
+        total = work[LOG : 2 * LOG, plane(x)]
+        total = total + turn(work[0:LOG, plane(x)], 1) + turn(work[2 * LOG : 3 * LOG, plane(x)], -1)
         weights[:, plane(x)] = jax.nn.sigmoid(total)
 
 
@@ -603,9 +677,11 @@
     return total
 
 
-def first_kernel_body(mode_x, recv, fwd1, fwd2, bias1, bias2, z_hi, z_lo, out, hidden, weights, u_hi, u_lo, h_hi, h_lo, work, modes):
-    network(recv, fwd1, fwd2, bias1, bias2, hidden, weights, u_hi, u_lo, h_hi, h_lo, work)
-    table = (z_hi[...], z_lo[...])
+def first_kernel_body(
+    mode_x, recv, fwd1, fwd2, to_z, out, hidden, weights, u_taps, h_hi, h_lo, work, modes
+):
+    network(recv, fwd1, fwd2, hidden, weights, u_taps, h_hi, h_lo, work)
+    table = (to_z[0], to_z[1])
     moved_field = [jnp.concatenate(advected(recv, weights, x), axis=0) for x in range(PLANES)]
     for f in range(2):
         planes = moved_field if f == 0 else [recv[x, 36:60, :] for x in range(PLANES)]
@@ -613,7 +689,7 @@
             modes[f, k] = value
     for f in range(2):
         flat = modes[f].reshape(PLANES * 24, DEPTH)
-        modes[f] = dot3(split(flat), table).reshape(PLANES, 24, DEPTH)
+        modes[f] = dot_stacked(stacked(flat), table).reshape(PLANES, 24, DEPTH)
     scatter_modes(lambda f, k: modes[f, k], 24, out)
 
 
@@ -659,29 +735,29 @@
     )
 
 
-def both_kernel(recv, in_hi, in_lo, out_hi, out_lo, out):
+def both_kernel(recv, table_in, table_out, out):
     data = split(recv[...].reshape(16 * 24, DEPTH))
-    modes = dot3((in_hi[...], in_lo[...]), data)
+    modes = dot_stacked(table_in, data)
     fixed = leray([modes[m * ROWS : (m + 1) * ROWS] for m in range(3)])
-    back = dot3((out_hi[...], out_lo[...]), split(jnp.concatenate(fixed, axis=0)))
+    back = dot_stacked(table_out, split(jnp.concatenate(fixed, axis=0)))
     wide, rest = back[:512].reshape(16, 32, DEPTH), back[512:].reshape(16, 32, DEPTH)
     low = lax.broadcasted_iota(jnp.int32, (16, 24, DEPTH), 2) < DEPTH // 2
     out[:, 0:24, :] = jnp.where(low, wide[:, :24], rest[:, :24])
     out[:, 24:32, :] = jnp.where(low[:, :8], wide[:, 24:], turn(rest[:, 24:], DEPTH // 2))
 
 
-def one_kernel(recv, in_hi, in_lo, out_hi, out_lo, out):
+def one_kernel(recv, table_in, table_out, out):
     data = split(recv[...].reshape(16 * 24, DEPTH))
-    modes = dot3((in_hi[...], in_lo[...]), data)
+    modes = dot_stacked(table_in, data)
     modes = modes[: 3 * ROWS] + turn(modes[3 * ROWS :], DEPTH // 2)
     fixed = leray([modes[m * ROWS : (m + 1) * ROWS] for m in range(3)])
-    back = dot3((out_hi[...], out_lo[...]), split(jnp.concatenate(fixed, axis=0)))
+    back = dot_stacked(table_out, split(jnp.concatenate(fixed, axis=0)))
     lane = lax.broadcasted_iota(jnp.int32, (256, DEPTH), 1)
     whole = jnp.where(lane < DEPTH // 2, back[:256], turn(back[256:], DEPTH // 2))
     out[...] = whole.reshape(16, 16, DEPTH)
 
 
-def pullback(field, grad, hidden, weights, back2, back1, u_hi, u_lo, h_hi, h_lo, l_hi, l_lo, p_hi, p_lo, work, slope, sums, ends, earlier):
+def pullback(field, grad, hidden, weights, back2, back1, l_taps, p_hi, p_lo, work, slope):
     slope[...] = jnp.zeros_like(slope)
     for x in range(PLANES):
         center = around(field, x, 0, 0)
@@ -728,72 +804,56 @@
         for m in range(3):
             slope[x, m * REACH + RIM : m * REACH + RIM + SLAB, :] += own[m]
         whole = jnp.concatenate(logits, axis=0)
-        for e in range(3):
-            parts = split(turn(whole, e - 1))
-            for a in range(3):
-                rows = slice((a * 3 + e) * 48, (a * 3 + e) * 48 + 48)
-                l_hi[rows, plane(x + a - 1)] = parts[0]
-                l_lo[rows, plane(x + a - 1)] = parts[1]
+        stack_logits(whole, x, l_taps)
     for pair in range(4):
         cut = slice(pair * 256, pair * 256 + 256)
-        value = dot3((back2[0], back2[1]), (l_hi[:, cut], l_lo[:, cut]))
-        parts = split(value * (1.0 - hidden[:, cut] * hidden[:, cut]))
-        p_hi[:, cut] = parts[0]
-        p_lo[:, cut] = parts[1]
-        work[:, cut] = dot3((back1[0], back1[1]), parts)
+        value = dot_stacked(back2, (l_taps[0:STACK, cut], l_taps[STACK:, cut]))
+        value = value * (1.0 - hidden[:, cut] * hidden[:, cut])
+        stack_planes(value, 2 * pair, 1, p_hi, p_lo)
+    finish_planes(p_hi, p_lo)
+    for pair in range(4):
+        cut = slice(pair * 256, pair * 256 + 256)
+        work[:, cut] = dot_stacked(back1, (p_hi[:, cut], p_lo[:, cut]))
     for x in range(PLANES):
-        total = slope[x, 0:40, :]
-        for a in range(3):
-            for e in range(3):
-                tap = a * 3 + e
-                total = total + turn(work[tap * 48 : tap * 48 + 40, plane(x - a + 1)], e - 1)
-        slope[x, 0:40, :] = total
-    second = dot3((l_hi[...], l_lo[...]), (h_hi[...], h_lo[...]), NT)
-    first = dot3((u_hi[...], u_lo[...]), (p_hi[...], p_lo[...]), NT)
-    ones = jnp.ones((16, FLAT), jnp.bfloat16)
-    end1 = dot(ones, p_hi[...], NT) + dot(ones, p_lo[...], NT)
-    end2 = dot(ones, l_hi[4 * 48 : 5 * 48, :], NT) + dot(ones, l_lo[4 * 48 : 5 * 48, :], NT)
-    if earlier is None:
-        sums[0:STACK, :] = second
-        sums[STACK:, :] = first
-        ends[0:16, :] = end1
-        ends[16:32, 0:LOG] = end2
-    else:
-        old_sums, old_ends = earlier
-        sums[0:STACK, :] = old_sums[0:STACK, :] + second
-        sums[STACK:, :] = old_sums[STACK:, :] + first
-        ends[0:16, :] = old_ends[0:16, :] + end1
-        ends[16:32, 0:LOG] = old_ends[16:32, 0:LOG] + end2
+        total = slope[x, 0:40, :] + work[48:88, plane(x)]
+        slope[x, 0:40, :] = total + turn(work[0:40, plane(x)], -1) + turn(work[96:136, plane(x)], 1)
+
+
+def kernel_sums(u_taps, h_hi, h_lo, l_taps, p_hi, p_lo, sums):
+    here = slice(2 * HID, DEEP)
+    sums[0:STACK, :] = dot_stacked(l_taps, (h_hi[here, :], h_lo[here, :]), NT)
+    sums[STACK:, :] = dot_stacked(u_taps, (p_hi[here, :], p_lo[here, :]), NT)
 
 
 def second_kernel_body(
-    mode_x, recv, fwd1, fwd2, back2, back1, bias1, bias2, to_hi, to_lo, from_hi, from_lo,
-    out, sums, ends,
-    field, grad, modes, rows6, hidden, weights, u_hi, u_lo, h_hi, h_lo, l_hi, l_lo, p_hi, p_lo, work, slope,
+    mode_x, recv, fwd1, fwd2, back2, back1, to_z, from_z,
+    out, sums,
+    field, hidden, grad, modes, rows6, weights, work, slope,
+    u_taps, h_hi, h_lo, l_taps, p_hi, p_lo,
 ):
-    back_z = (from_hi[...], from_lo[...])
+    back_z = (from_z[0], from_z[1])
     for k in range(PLANES):
         modes[k, 0:32, :] = gather_modes(recv, 0, k, 0, 32)
         modes[k, 32:40, :] = gather_modes(recv, 1, k, 24, 8)
-    flat = dot3(split(modes[...].reshape(PLANES * 40, DEPTH)), back_z)
+    flat = dot_stacked(stacked(modes[...].reshape(PLANES * 40, DEPTH)), back_z)
     modes[...] = flat.reshape(PLANES, 40, DEPTH)
     for x, value in enumerate(mixed([modes[k] for k in range(PLANES)], mode_x.T)):
         field[x, 0:40, :] = value
         field[x, 40:48, :] = jnp.zeros((8, DEPTH), jnp.float32)
     for k in range(PLANES):
         grad[k] = gather_modes(recv, 1, k, 0, 24)
-    flat = dot3(split(grad[...].reshape(PLANES * 24, DEPTH)), back_z)
+    flat = dot_stacked(stacked(grad[...].reshape(PLANES * 24, DEPTH)), back_z)
     flat = flat.reshape(PLANES, 24, DEPTH)
     for x, value in enumerate(mixed([flat[k] for k in range(PLANES)], mode_x.T)):
         grad[x] = value
-    network(field, fwd1, fwd2, bias1, bias2, hidden, weights, u_hi, u_lo, h_hi, h_lo, work)
+    network(field, fwd1, fwd2, hidden, weights, u_taps, h_hi, h_lo, work)
     pullback(
-        field, grad, hidden, weights, back2, back1, u_hi, u_lo, h_hi, h_lo, l_hi, l_lo, p_hi, p_lo,
-        work, slope, sums, ends, None,
-    )
+        field, grad, hidden, weights, back2, back1, l_taps, p_hi, p_lo, work, slope
+    )
+    kernel_sums(u_taps, h_hi, h_lo, l_taps, p_hi, p_lo, sums)
     for k, value in enumerate(mixed([slope[x, 0:40, :] for x in range(PLANES)], mode_x)):
         modes[k] = value
-    flat = dot3(split(modes[...].reshape(PLANES * 40, DEPTH)), (to_hi[...], to_lo[...]))
+    flat = dot_stacked(stacked(modes[...].reshape(PLANES * 40, DEPTH)), (to_z[0], to_z[1]))
     modes[...] = flat.reshape(PLANES, 40, DEPTH)
     for h in range(2):
         for k in range(PLANES):
@@ -804,41 +864,39 @@
 
 
 def third_kernel_body(
-    mode_x, recv, field, hidden, weights, back2, back1, from_hi, from_lo, old_sums, old_ends,
+    mode_x, recv, field, hidden, weights, back2, back1, from_z, old_sums,
     spread_t, mask, lift, count,
     out,
-    grad, modes, u_hi, u_lo, h_hi, h_lo, l_hi, l_lo, p_hi, p_lo, work, slope, sums, ends, pieces,
+    grad, modes, u_taps, h_hi, h_lo, l_taps, p_hi, p_lo, work, slope, sums, pieces,
 ):
-    back_z = (from_hi[...], from_lo[...])
+    back_z = (from_z[0], from_z[1])
     for h in range(2):
         for k in range(PLANES):
             modes[k] = gather_modes(recv, h, k, 0, 16)
-        flat = dot3(split(modes[...].reshape(PLANES * 16, DEPTH)), back_z)
+        flat = dot_stacked(stacked(modes[...].reshape(PLANES * 16, DEPTH)), back_z)
         modes[...] = flat.reshape(PLANES, 16, DEPTH)
         for x, value in enumerate(mixed([modes[k] for k in range(PLANES)], mode_x.T)):
             for m in range(3):
                 grad[x, m * SLAB + 4 * h : m * SLAB + 4 * h + 4, :] = value[m * 4 : m * 4 + 4, :]
-    stack_field(field, u_hi, u_lo)
-    parts = split(hidden[...])
-    h_hi[...] = parts[0]
-    h_lo[...] = parts[1]
-    pullback(
-        field, grad, hidden, weights, back2, back1, u_hi, u_lo, h_hi, h_lo, l_hi, l_lo, p_hi, p_lo,
-        work, slope, sums, ends, (old_sums, old_ends),
-    )
+    stack_field(field, u_taps)
+    stack_planes(hidden[...], 0, -1, h_hi, h_lo)
+    finish_planes(h_hi, h_lo)
+    pullback(field, grad, hidden, weights, back2, back1, l_taps, p_hi, p_lo, work, slope)
+    kernel_sums(u_taps, h_hi, h_lo, l_taps, p_hi, p_lo, sums)
+    sums[...] += old_sums[...]
     for x in range(PLANES):
         out[x, 0:40, :] = slope[x, 0:40, :]
         out[x, 36:40, :] = jnp.zeros((4, DEPTH), jnp.float32)
-    pack_grads(sums, ends, spread_t, mask, lift, count, pieces)
+    pack_grads(sums, spread_t, mask, lift, count, pieces)
     for x in range(PLANES):
         out[x, 40:72, :] = pieces[96:128, :]
 
 
-def pack_grads(sums, ends, spread_t, mask, lift, count, pieces):
+def pack_grads(sums, spread_t, mask, lift, count, pieces):
     pieces[...] = jnp.zeros_like(pieces)
+    whole = split(sums[...])
     for b in range(3):
-        parts = split(sums[...] * mask[b].astype(jnp.float32))
-        rows = dot(spread_t[...], parts[0]) + dot(spread_t[...], parts[1])
+        rows = dot(spread_t[...], whole[0] * mask[b]) + dot(spread_t[...], whole[1] * mask[b])
         parts = split(rows)
         pieces[0:96, :] = dot(parts[0], lift[...]) + dot(parts[1], lift[...])
         for c in range(3):
@@ -852,11 +910,12 @@
                     pieces[123 : 123 + count_rows, :] += turn(
                         pieces[first : first + count_rows, :], 16 * part
                     )
-    parts = split(ends[0:16, :])
+    parts = split(sums[2 * STACK :, :])
     total = dot(parts[0], lift[...]) + dot(parts[1], lift[...])
-    parts = split(ends[16:32, 0:LOG])
-    total = total + dot(parts[0], count[...]) + dot(parts[1], count[...])
-    pieces[127:128, :] = total[0:1, :]
+    parts = split(sums[4 * LOG : 5 * LOG, 128:BROAD])
+    across = ((0,), (0,))
+    other = dot(parts[0], count[...], across) + dot(parts[1], count[...], across)
+    pieces[127:128, :] = total[0:1, :] + other[HID - 128 : HID - 127, :]
 
 
 def fold_kernel(recv, main, edge, ext):
@@ -910,64 +969,86 @@
 
     other = lax.ppermute(velocity, "py", swap)
     packed = call(
-        pack_kernel, shape(PLANES, 64, DEPTH), (velocity, cotangent, other), [f32(3, 80, DEPTH)], 56
-    )
+        pack_kernel, shape(PLANES, 64, DEPTH), (velocity, cotangent), [f32(3, 80, DEPTH)], room=4
+    )
+    packed = call(rim_kernel, shape(PLANES, 64, DEPTH), (packed, other), room=4)
     recv = lax.all_to_all(packed, "px", 0, 0)
 
-    fwd2, fwd1, back2, back1, bias1, bias2 = call(
+    fwd2, fwd1, back2, back1, to_z = call(
         weights_kernel,
         [
-            shape(2, STACK, HID, kind=half),
-            shape(2, HID, STACK, kind=half),
-            shape(2, HID, STACK, kind=half),
-            shape(2, STACK, HID, kind=half),
-            shape(HID, 256),
-            shape(LOG, DEPTH),
+            shape(288, DEEP, kind=half),
+            shape(2 * HID, TALL, kind=half),
+            shape(2 * HID, STACK, kind=half),
+            shape(288, DEEP, kind=half),
+            shape(2, DEPTH, DEPTH, kind=half),
         ],
         (
             jnp.transpose(first_kernel, (1, 2, 3, 4, 0)).reshape(27, 3, CHANNELS),
             jnp.transpose(second_kernel, (0, 2, 3, 4, 1)).reshape(54, 3, CHANNELS),
             first_bias.reshape(1, CHANNELS),
             second_bias.reshape(1, COEFFS),
+            c["to_z"],
         ),
-        [f32(3, 96, CHANNELS)],
-    )
-
-    stacks = lambda rows: [b16(rows, FLAT), b16(rows, FLAT)]
+        [
+            f32(3, 96, CHANNELS),
+            f32(27, 3, CHANNELS),
+            f32(54, 3, CHANNELS),
+            f32(1, CHANNELS),
+            f32(1, COEFFS),
+            pltpu.SemaphoreType.DMA((4,)),
+        ],
+        away=(0, 1, 2, 3),
+    )
+
+    near = lambda rows: [b16(rows, FLAT), b16(rows, FLAT)]
+    stacks = near(2 * TALL)[:1] + near(DEEP) + near(2 * STACK)[:1] + near(DEEP)
     sent, hidden, weights = call(
         functools.partial(first_kernel_body, mode_x),
         [shape(16, 24, DEPTH), shape(HID, FLAT), shape(LOG, FLAT)],
-        (recv, fwd1, fwd2, bias1, bias2, *c["to_z"]),
-        stacks(STACK) + stacks(HID) + [f32(STACK, FLAT), f32(2, PLANES, 24, DEPTH)],
+        (recv, fwd1, fwd2, to_z),
+        near(2 * TALL)[:1] + near(DEEP) + [f32(144, FLAT), f32(2, PLANES, 24, DEPTH)],
     )
     both = ("px", "py")
     moved_modes = lax.all_to_all(sent, both, 0, 0)
-    moved_modes = call(both_kernel, shape(16, 32, DEPTH), (moved_modes, *c["both_in"], *c["both_out"]))
+    moved_modes = call(both_kernel, shape(16, 32, DEPTH), (moved_modes, c["both_in"], c["both_out"]))
     moved_modes = lax.all_to_all(moved_modes, both, 0, 0)
 
-    sent, sums, ends = call(
+    sent, sums = call(
         functools.partial(second_kernel_body, mode_x),
-        [shape(16, 24, DEPTH), shape(2 * STACK, HID), shape(32, HID)],
-        (moved_modes, fwd1, fwd2, back2, back1, bias1, bias2, *c["to_z"], *c["from_z"]),
-        [f32(PLANES, 48, DEPTH), f32(PLANES, 24, DEPTH), f32(PLANES, 40, DEPTH), f32(2, PLANES, 24, DEPTH)]
-        + [f32(HID, FLAT), f32(LOG, FLAT)]
-        + stacks(STACK) + stacks(HID) + stacks(STACK) + stacks(HID)
-        + [f32(STACK, FLAT), f32(PLANES, 48, DEPTH)],
+        [shape(16, 24, DEPTH), shape(STACK + TALL, BROAD)],
+        (moved_modes, fwd1, fwd2, back2, back1, to_z, c["from_z"]),
+        [
+            f32(PLANES, 48, DEPTH),
+            f32(HID, FLAT),
+            f32(PLANES, 24, DEPTH),
+            f32(PLANES, 40, DEPTH),
+            f32(2, PLANES, 24, DEPTH),
+            f32(LOG, FLAT),
+            f32(144, FLAT),
+            f32(PLANES, 48, DEPTH),
+        ]
+        + stacks,
     )
     moved_modes = lax.all_to_all(sent, both, 0, 0)
-    moved_modes = call(one_kernel, shape(16, 16, DEPTH), (moved_modes, *c["one_in"], *c["one_out"]))
+    moved_modes = call(one_kernel, shape(16, 16, DEPTH), (moved_modes, c["one_in"], c["one_out"]))
     moved_modes = lax.all_to_all(moved_modes, both, 0, 0)
 
     sent = call(
         functools.partial(third_kernel_body, mode_x),
         shape(PLANES, 72, DEPTH),
         (
-            moved_modes, recv, hidden, weights, back2, back1, *c["from_z"], sums, ends,
+            moved_modes, recv, hidden, weights, back2, back1, c["from_z"], sums,
             c["spread_t"], c["mask"], c["lift"], c["count"],
         ),
         [f32(PLANES, 24, DEPTH), f32(PLANES, 16, DEPTH)]
-        + stacks(STACK) + stacks(HID) + stacks(STACK) + stacks(HID)
-        + [f32(STACK, FLAT), f32(PLANES, 48, DEPTH), f32(2 * STACK, HID), f32(32, HID), f32(128, DEPTH)],
+        + stacks
+        + [
+            f32(144, FLAT),
+            f32(PLANES, 48, DEPTH),
+            f32(STACK + TALL, BROAD),
+            f32(128, DEPTH),
+        ],
     )
     recv = lax.all_to_all(sent, "px", 0, 0)
     main, edge = call(

time: 104 us -> 98.6 us (0.948)
  local copies, waits for them, and re-layouts: 6.66 us -> 1.85 us
  waiting for transfers between devices: 4.92 us -> 6.63 us
  Pallas kernels: 22.6 us -> 21.3 us
    unnamed x52 -> x32, local copies, waits for them, and re-layouts: 6.66 us -> 1.85 us
    all_to_all x1, waiting for transfers between devices: 2.58 us -> 5.44 us  [slab_device(): recv = lax.all_to_all(packed, 'px', 0, 0)]
    pallas_call x9 -> x10, Pallas kernels: 22.6 us -> 21.3 us  [call(): pl.pallas_call(kernel, out_shape=outs, in_specs=[pl.BlockSpec(memory_spac...]
    ppermute x1, waiting for transfers between devices: 1.15 us -> 0.01 us  [slab_device(): other = lax.ppermute(velocity, 'py', swap)]
  transfers between devices with their start and end apart: 3 -> 3, of which waited for: 3 -> 2; matrix products, arithmetic and copies ran while one was open for 0% -> 0% of each run, Pallas kernels for 3% -> 4%
where the time goes in v3:
time: 98.6 us; the launch traced here: 98.2 us
  blocking collectives  60.2 us (61%)
  Pallas kernels  21.3 us (22%)
  starting transfers between devices  7.4 us (8%)
  waiting for transfers between devices  6.63 us (7%)
  local copies, waits for them, and re-layouts  1.85 us (2%)
    all_to_all x2, blocking collectives, slab_device(): moved_modes = lax.all_to_all(sent, both, 0, 0)  24.2 us
    all_to_all x2, blocking collectives, slab_device(): moved_modes = lax.all_to_all(moved_modes, both, 0, 0)  23.3 us
    pallas_call x10, Pallas kernels, call(): pl.pallas_call(kernel, out_shape=outs, in_specs=[pl.BlockSpec(memory_spac...  21.3 us
    all_to_all x1, blocking collectives, slab_device(): recv = lax.all_to_all(sent, 'px', 0, 0)  12.7 us
    all_to_all x1, starting transfers between devices, slab_device(): recv = lax.all_to_all(packed, 'px', 0, 0)  6.81 us
    all_to_all x1, waiting for transfers between devices, slab_device(): recv = lax.all_to_all(packed, 'px', 0, 0)  5.44 us
  transfers between devices with their start and end apart: 3, of which 2 were waited for; matrix products, arithmetic and copies ran while one was open for 0% of the time, Pallas kernels for 4%

profile of v3, /device:TPU:0, one launch (start us, length us, event | category | flops | bytes accessed | tf_op | source)
XLA Modules:
  0.0 98.2 jit_solution(3245472949436906144)
XLA Ops:
  0.6 0.5 collective-permute-start
  1.2 0.9 copy-done.8
  2.1 0.9 copy-done.9
  3.0 0.0 copy-start
  3.0 0.7 shard_map.192
  3.8 6.8 %all-to-all-start = ((f32[8,64,128]{2,1,0:T(8,128)}), f32[8,64,128]{2,1,0:T(8,128)S(1)}, u32[]{:S(2)}, u32[]{:S(2)}) async-start(f32[8,64,128]{2,1,0:T(8,128)} %shard_map.192), calls=%async_computation | async-start | bytes 524288 | tf_op jit(solution)/shard_map/all_to_all | solution.py:975
  10.6 4.1 %shard_map.193 = (bf16[288,496]{1,0:T(8,128)(2,1)S(1)}, bf16[320,448]{1,0:T(8,128)(2,1)S(1)}, bf16[320,432]{1,0:T(8,128)(2,1)S(1)}, bf16[288,496]{1,0:T(8,128)(2,1)S(1)}, bf16[2,128,128]{2,1,0:T(8,128)(2,1)S(1)}) custom-call(f32[27,3,16]{2,1,0:T(4,128)S(1)} %bitcast.17, f32[54,3,16]{2,1,0:T(4,128)S(1)} %bitcast.16, f32[1,16]{1,0:T(1,128)S(1)} %bitcast.18, ...), custom_call_target="tpu_custom_call" | custom-call | flops 1 | bytes 1 | tf_op jit(solution)/shard_map/pallas_call | solution.py:430
  14.7 5.4 %all-to-all-done.recv.field = f32[8,64,128]{2,1,0:T(8,128)S(1)} async-done(((f32[8,64,128]{2,1,0:T(8,128)}), f32[8,64,128]{2,1,0:T(8,128)S(1)}, u32[]{:S(2)}, u32[]{:S(2)}) %all-to-all-start) | async-done | bytes 262176 | tf_op jit(solution)/shard_map/all_to_all | solution.py:975
  20.2 2.1 %shard_map.194 = (f32[16,24,128]{2,1,0:T(8,128)S(1)}, f32[160,1024]{1,0:T(8,128)S(1)}, f32[48,1024]{1,0:T(8,128)S(1)}) custom-call(f32[8,64,128]{2,1,0:T(8,128)S(1)} %all-to-all-done.recv.field, bf16[320,448]{1,0:T(8,128)(2,1)S(1)} %get-tuple-element.22.fwd1, bf16[288,496]{1,0:T(8,128)(2,1)S(1)} %get-tuple-element.23.fwd2, ...), custom_call_target="tpu_custom_call" | custom-call | tf_op jit(solution)/shard_map/pallas_call | solution.py:430
  22.2 12.5 %all_to_all.30.recv = f32[16,24,128]{2,1,0:T(8,128)S(1)} all-to-all(f32[16,24,128]{2,1,0:T(8,128)S(1)} %get-tuple-element.25), channel_id=1, replica_groups=mesh['groups'=2,'px'=8,'py'=2] {'px','py'}, dimensions={0} | all-to-all | bytes 393216 | tf_op jit(solution)/shard_map/all_to_all | solution.py:1013
  34.7 1.4 %shard_map.195 = f32[16,32,128]{2,1,0:T(8,128)S(1)} custom-call(f32[16,24,128]{2,1,0:T(8,128)S(1)} %all_to_all.30.recv, bf16[768,384]{1,0:T(8,128)(2,1)S(1)} %copy-done.4, bf16[2048,384]{1,0:T(8,128)(2,1)S(1)} %copy-done), custom_call_target="tpu_custom_call" | custom-call | tf_op jit(solution)/shard_map/pallas_call | solution.py:430
  36.2 12.8 %all_to_all.31.recv = f32[16,32,128]{2,1,0:T(8,128)S(1)} all-to-all(f32[16,32,128]{2,1,0:T(8,128)S(1)} %shard_map.195), channel_id=1, replica_groups=mesh['groups'=2,'px'=8,'py'=2] {'px','py'}, dimensions={0} | all-to-all | bytes 524288 | tf_op jit(solution)/shard_map/all_to_all | solution.py:1015
  48.9 5.3 %shard_map.196 = (f32[16,24,128]{2,1,0:T(8,128)S(1)}, f32[880,176]{1,0:T(8,128)S(1)}) custom-call(f32[16,32,128]{2,1,0:T(8,128)S(1)} %all_to_all.31.recv, bf16[320,448]{1,0:T(8,128)(2,1)S(1)} %get-tuple-element.22.fwd1, bf16[288,496]{1,0:T(8,128)(2,1)S(1)} %get-tuple-element.23.fwd2, bf16[320,432]{1,0:T(8,128)(2,1)S(1)} %get-tuple-element.26.back2, ...), custom_call_target="tpu_custom_call" | custom-call | tf_op jit(solution)/shard_map/pallas_call | solution.py:430
  54.3 11.7 %all_to_all.32.recv = f32[16,24,128]{2,1,0:T(8,128)S(1)} all-to-all(f32[16,24,128]{2,1,0:T(8,128)S(1)} %get-tuple-element.28), channel_id=1, replica_groups=mesh['groups'=2,'px'=8,'py'=2] {'px','py'}, dimensions={0} | all-to-all | bytes 393216 | tf_op jit(solution)/shard_map/all_to_all | solution.py:1033
  66.0 0.0 copy-start.12
  66.0 0.0 copy-start.13
  66.0 1.5 %shard_map.197 = f32[16,16,128]{2,1,0:T(8,128)S(1)} custom-call(f32[16,24,128]{2,1,0:T(8,128)S(1)} %all_to_all.32.recv, bf16[1536,384]{1,0:T(8,128)(2,1)S(1)} %copy-done.2, bf16[1024,384]{1,0:T(8,128)(2,1)S(1)} %copy-done.3), custom_call_target="tpu_custom_call" | custom-call | tf_op jit(solution)/shard_map/pallas_call | solution.py:430
  67.5 10.5 %all_to_all.33.recv = f32[16,16,128]{2,1,0:T(8,128)S(1)} all-to-all(f32[16,16,128]{2,1,0:T(8,128)S(1)} %shard_map.197), channel_id=1, replica_groups=mesh['groups'=2,'px'=8,'py'=2] {'px','py'}, dimensions={0} | all-to-all | bytes 262144 | tf_op jit(solution)/shard_map/all_to_all | solution.py:1035
  78.1 5.3 %shard_map.198 = f32[8,72,128]{2,1,0:T(8,128)S(1)} custom-call(f32[16,16,128]{2,1,0:T(8,128)S(1)} %all_to_all.33.recv, f32[8,64,128]{2,1,0:T(8,128)S(1)} %all-to-all-done.recv.field, f32[160,1024]{1,0:T(8,128)S(1)} %get-tuple-element.29.hidden, f32[48,1024]{1,0:T(8,128)S(1)} %get-tuple-element.30.weights, bf16[320,432]{1,0:T(8,128)(2,1)S(1)} %get-tuple-element.26.back2, ...), custom_call_target="tpu_custom_call" | custom-call | tf_op jit(solution)/shard_map/pallas_call | solution.py:430
  83.3 12.7 %all_to_all.34.recv = f32[8,72,128]{2,1,0:T(8,128)S(1)} all-to-all(f32[8,72,128]{2,1,0:T(8,128)S(1)} %shard_map.198), channel_id=1, replica_groups=mesh['groups'=2,'px'=8,'py'=2] {'px'}, dimensions={0} | all-to-all | bytes 589824 | tf_op jit(solution)/shard_map/all_to_all | solution.py:1053
  96.0 0.1 shard_map.199
  96.1 0.1 collective-permute-start.1
  96.1 1.2 %collective-permute-done.1.other = f32[56,128]{1,0:T(8,128)S(1)} collective-permute-done((f32[56,128]{1,0:T(8,128)S(1)}, f32[56,128]{1,0:T(8,128)S(1)}, u32[]{:S(2)}, u32[]{:S(2)}) %collective-permute-start.1) | collective-permute-done | bytes 28704 | tf_op jit(solution)/shard_map/ppermute | solution.py:1057
  97.3 0.8 shard_map.200
  (29 shorter events, 0.1 us)
Async XLA Ops:
  0.6 9.9 %copy-start.7 = (f32[6,16,3,3,3]{1,4,3,2,0:T(4,128)S(1)}, f32[6,16,3,3,3]{1,4,3,2,0:T(4,128)}, u32[]{:S(2)}) copy-start(f32[6,16,3,3,3]{1,4,3,2,0:T(4,128)} %param.20) | copy-start | bytes 31108
  0.6 2.4 %collective-permute-start = (f32[3,1,64,128]{3,2,1,0:T(8,128)}, f32[3,1,64,128]{3,2,1,0:T(8,128)S(1)}, u32[]{:S(2)}, u32[]{:S(2)}) collective-permute-start(f32[3,1,64,128]{3,2,1,0:T(8,128)} %field.1), channel_id=1, source_target_pairs={{0,1},{1,0},{2,3},{3,2},{4,5},{5,4},{6,7},{7,6},{8,9},{9,8},{10,11... | collective-permute-start | bytes 294920 | tf_op jit(solution)/shard_map/ppermute | solution.py:970
  1.2 0.9 copy-start.8
  2.1 0.9 copy-start.9
  2.9 7.6 %copy-start.10 = (bf16[2,128,128]{2,1,0:T(8,128)(2,1)S(1)}, bf16[2,128,128]{2,1,0:T(8,128)(2,1)}, u32[]{:S(2)}) copy-start(bf16[2,128,128]{2,1,0:T(8,128)(2,1)} %constant.20.clone.z_in) | copy-start | bytes 196612
  2.9 7.6 %copy-start.11 = (f32[16,3,3,3,3]{0,4,3,2,1:T(4,128)S(1)}, f32[16,3,3,3,3]{0,4,3,2,1:T(4,128)}, u32[]{:S(2)}) copy-start(f32[16,3,3,3,3]{0,4,3,2,1:T(4,128)} %param.18) | copy-start | bytes 15556
  3.0 7.6 %copy-start.14 = (f32[16]{0:T(128)S(1)}, f32[16]{0:T(128)}, u32[]{:S(2)}) copy-start(f32[16]{0:T(128)} %param.19) | copy-start | bytes 196
  3.0 7.7 %copy-start.15 = (f32[6]{0:T(128)S(1)}, f32[6]{0:T(128)}, u32[]{:S(2)}) copy-start(f32[6]{0:T(128)} %param.21) | copy-start | bytes 76
  3.0 31.7 %copy-start = (bf16[2048,384]{1,0:T(8,128)(2,1)S(1)}, bf16[2048,384]{1,0:T(8,128)(2,1)}, u32[]{:S(2)}) copy-start(bf16[2048,384]{1,0:T(8,128)(2,1)} %constant.22.clone.table_out) | copy-start | bytes 4718596
  3.8 16.4 %all-to-all-start = ((f32[8,64,128]{2,1,0:T(8,128)}), f32[8,64,128]{2,1,0:T(8,128)S(1)}, u32[]{:S(2)}, u32[]{:S(2)}) async-start(f32[8,64,128]{2,1,0:T(8,128)} %shard_map.192), calls=%async_computation | async-start | bytes 524288 | tf_op jit(solution)/shard_map/all_to_all | solution.py:975
  20.1 14.6 %copy-start.4 = (bf16[768,384]{1,0:T(8,128)(2,1)S(1)}, bf16[768,384]{1,0:T(8,128)(2,1)}, u32[]{:S(2)}) copy-start(bf16[768,384]{1,0:T(8,128)(2,1)} %constant.21.clone.table_in) | copy-start | bytes 1769476
  34.7 14.2 %copy-start.5 = (bf16[2,128,128]{2,1,0:T(8,128)(2,1)S(1)}, bf16[2,128,128]{2,1,0:T(8,128)(2,1)}, u32[]{:S(2)}) copy-start(bf16[2,128,128]{2,1,0:T(8,128)(2,1)} %constant.23.clone.from_z) | copy-start | bytes 196612
  36.2 29.9 %copy-start.2 = (bf16[1536,384]{1,0:T(8,128)(2,1)S(1)}, bf16[1536,384]{1,0:T(8,128)(2,1)}, u32[]{:S(2)}) copy-start(bf16[1536,384]{1,0:T(8,128)(2,1)} %constant.24.clone.table_in) | copy-start | bytes 3538948
  36.2 29.9 %copy-start.3 = (bf16[1024,384]{1,0:T(8,128)(2,1)S(1)}, bf16[1024,384]{1,0:T(8,128)(2,1)}, u32[]{:S(2)}) copy-start(bf16[1024,384]{1,0:T(8,128)(2,1)} %constant.25.clone.table_out) | copy-start | bytes 2359300
  66.0 12.0 %copy-start.1 = (bf16[3,880,176]{2,1,0:T(8,128)(2,1)S(1)}, bf16[3,880,176]{2,1,0:T(8,128)(2,1)}, u32[]{:S(2)}) copy-start(bf16[3,880,176]{2,1,0:T(8,128)(2,1)} %constant.27.clone.mask) | copy-start | bytes 2787844
  66.0 12.0 %copy-start.6 = (bf16[96,880]{1,0:T(8,128)(2,1)S(1)}, bf16[96,880]{1,0:T(8,128)(2,1)}, u32[]{:S(2)}) copy-start(bf16[96,880]{1,0:T(8,128)(2,1)} %constant.26.clone.spread_t) | copy-start | bytes 506884
  66.0 12.0 %copy-start.12 = (bf16[176,128]{1,0:T(8,128)(2,1)S(1)}, bf16[176,128]{1,0:T(8,128)(2,1)}, u32[]{:S(2)}) copy-start(bf16[176,128]{1,0:T(8,128)(2,1)} %constant.28.clone.lift) | copy-start | bytes 135172
  66.0 12.0 %copy-start.13 = (bf16[48,128]{1,0:T(8,128)(2,1)S(1)}, bf16[48,128]{1,0:T(8,128)(2,1)}, u32[]{:S(2)}) copy-start(bf16[48,128]{1,0:T(8,128)(2,1)} %constant.29.clone.count) | copy-start | bytes 36868
  96.1 1.3 %collective-permute-start.1 = (f32[56,128]{1,0:T(8,128)S(1)}, f32[56,128]{1,0:T(8,128)S(1)}, u32[]{:S(2)}, u32[]{:S(2)}) collective-permute-start(f32[56,128]{1,0:T(8,128)S(1)} %get-tuple-element.33.edge), channel_id=1, source_target_pairs={{0,1},{1,0},{2,3},{3,2},{4,5},{5,4},{6,7},{7,6},{8,9},{9,8},{10,11... | collective-permute-start | bytes 86024 | tf_op jit(solution)/shard_map/ppermute | solution.py:1057

commit v4 on v3

--- a/solution.py
+++ b/solution.py
@@ -296,8 +296,7 @@
 HID = CHANNELS * WIDE
 LOG = COEFFS * SLAB
 STACK = 9 * 48
-TALL = STACK + 16
-BROAD = HID + 16
+UNIT = 36
 DEEP = 3 * HID + 16
 PLACE = (0, 2, 1)
 FLAT = PLANES * DEPTH
@@ -340,44 +339,47 @@
     mode_z = basis_z[order]
     basis_y = real_basis(ROWS)
 
-    def columns(device, offset, count):
-        return basis_y[:, (SLAB * slab_of(device) + offset + np.arange(count)) % ROWS]
-
-    def table(block, offset, count):
-        out = np.zeros((3, ROWS, 16, block))
-        for device in range(16):
-            for m in range(3):
-                out[m, :, device, m * count : (m + 1) * count] = columns(device, offset, count)
-        return out.reshape(3 * ROWS, 16 * block)
-
-    both_in = table(24, 0, 8)
-    wide_out = table(40, -RIM, REACH).T.reshape(16, 40, 3 * ROWS)
-    own_out = table(24, 0, 8).T.reshape(16, 24, 3 * ROWS)
-    rest = np.concatenate([own_out, wide_out[:, 32:]], axis=1)
-    both_out = np.stack([wide_out[:, :32], rest]).reshape(2 * 16 * 32, 3 * ROWS)
-    one_in = np.concatenate([table(24, -RIM, 6), table(24, -RIM + 6, 6)])
-    one_out = np.concatenate([table(16, 0, 4).T, table(16, 4, 4).T])
-
-    spread = np.zeros((STACK + TALL, 96))
-    mask = np.zeros((3, STACK + TALL, BROAD))
-    for tap in range(9):
+    def rows(offset, count):
+        at = [SLAB * slab_of(j) + offset + i for j in range(16) for i in range(count)]
+        return basis_y[:, np.array(at) % ROWS]
+
+    own, half_one, half_two = rows(0, SLAB), rows(0, 4), rows(4, 4)
+    before, after = rows(-RIM, RIM), rows(SLAB, RIM)
+    both_in = own
+    both_out = np.concatenate([own, before, after], axis=1).T
+    one_in = np.concatenate(
+        [np.concatenate([half_one, before], axis=1), np.concatenate([half_two, after], axis=1)]
+    )
+    one_out = np.concatenate([half_one, half_two], axis=1).T
+
+    spread = np.zeros((288, 32))
+    mask = np.zeros((3, 288, DEEP))
+    lanes = np.arange(CHANNELS) * WIDE
+    for e in range(3):
         for o in range(COEFFS):
             for q in range(SLAB):
-                row = tap * 48 + o * SLAB + q
-                spread[row, tap * COEFFS + o] = 1.0
+                row = e * 48 + o * SLAB + q
+                spread[row, e * COEFFS + o] = 1.0
                 for b in range(3):
-                    mask[b, row, np.arange(CHANNELS) * WIDE + q + b] = 1.0
+                    for a in range(3):
+                        mask[b, row, a * HID + lanes + q + b] = 1.0
         for m in range(3):
             for r in range(REACH):
-                row = STACK + tap * 48 + m * REACH + r
-                spread[row, 54 + tap * 3 + m] = 1.0
+                row = 144 + e * 48 + m * REACH + r
+                spread[row, 18 + e * 3 + m] = 1.0
                 for b in range(3):
-                    if 0 <= r - b < WIDE:
-                        mask[b, row, np.arange(CHANNELS) * WIDE + r - b] = 1.0
-    lift = np.zeros((BROAD, 128))
-    lift[np.arange(HID), np.arange(HID) // WIDE] = 1.0
-    count = np.zeros((LOG, 128))
-    count[np.arange(LOG), 16 + np.arange(LOG) // SLAB] = 1.0
+                    for a in range(3):
+                        if 0 <= r - b < WIDE:
+                            mask[b, row, a * HID + lanes + r - b] = 1.0
+    spread[144 + 48 + UNIT, 27] = 1.0
+    mask[0, 144 + 48 + UNIT, PLACE[1] * HID : (PLACE[1] + 1) * HID] = 1.0
+    mask[0, 48:96, 3 * HID] = 1.0
+    lift = np.zeros((3, 512, 256))
+    for b in range(3):
+        for a in range(3):
+            lift[b, PLACE[a] * HID + np.arange(HID), 16 * (3 * b + a) + np.arange(HID) // WIDE] = 1.0
+    lift[0, 3 * HID, 128 + 64] = 1.0
+    lift = lift.reshape(3 * 512, 256)
     half = jnp.bfloat16
     return dict(
         mode_x=mode_x,
@@ -390,7 +392,6 @@
         spread_t=np.ascontiguousarray(spread.T).astype(half),
         mask=mask.astype(half),
         lift=lift.astype(half),
-        count=count.astype(half),
     )
 
 
@@ -519,18 +520,17 @@
             part = tall[half][STACK + a * 144 : STACK + a * 144 + 144]
             back1[rows, first : first + HID] = part.astype(jnp.bfloat16)
         back2[cols, :] = flat[half][:, :STACK].astype(jnp.bfloat16)
-        fwd1[cols, 0:STACK] = flat[half][:, STACK:].astype(jnp.bfloat16)
     gap = counting((LOG, COEFFS), 0) - 8.0 * counting((LOG, COEFFS), 1)
     pick = ((gap >= 0.0) & (gap < 8.0)).astype(jnp.float32).astype(jnp.bfloat16)
-    first = counting((HID, 16), 1) < 1.0
     second = counting((LOG, 16), 1) < 1.0
-    one = split(jnp.broadcast_to(bias1[...], (16, CHANNELS)))
+    one = split(jnp.broadcast_to(bias1[...], (STACK, CHANNELS)))
+    first = counting((HID, STACK), 1) == 4.0 * 48.0 + UNIT
     two = split(jnp.broadcast_to(bias2[...], (16, COEFFS)))
     fwd2[:, 3 * HID :] = jnp.zeros((288, 16), jnp.bfloat16)
     back1[:, 3 * HID :] = jnp.zeros((288, 16), jnp.bfloat16)
     for half in range(2):
-        value = jnp.where(first, dot(lift, one[half], NT), 0.0)
-        fwd1[half * HID : half * HID + HID, STACK:] = value.astype(jnp.bfloat16)
+        value = jnp.where(first, dot(lift, one[half], NT), flat[half][:, STACK:])
+        fwd1[half * HID : half * HID + HID, :] = value.astype(jnp.bfloat16)
         value = jnp.where(second, dot(pick, two[half], NT), 0.0)
         start = half * 144 + LOG
         fwd2[start : start + LOG, 3 * HID :] = value.astype(jnp.bfloat16)
@@ -543,8 +543,9 @@
     for q in range(PLANES):
         for m in range(3):
             out[q, m * REACH : (m + 1) * REACH, :] = ext[m, 8 * q + 6 : 8 * q + 18, :]
-            out[q, 36 + 8 * m : 44 + 8 * m, :] = cot[m, 0, 8 * q : 8 * q + 8, :]
-        out[q, 60:64, :] = jnp.zeros((4, DEPTH), jnp.float32)
+            out[q, 40 + 8 * m : 48 + 8 * m, :] = cot[m, 0, 8 * q : 8 * q + 8, :]
+        out[q, 36:37, :] = jnp.ones((1, DEPTH), jnp.float32)
+        out[q, 37:40, :] = jnp.zeros((3, DEPTH), jnp.float32)
 
 
 def rim_kernel(packed, other, out):
@@ -591,9 +592,7 @@
             for a in range(3):
                 rows = slice((a * 3 + e) * 48, (a * 3 + e) * 48 + 48)
                 taps[rows, plane(x - a + 1)] = parts[0]
-                taps[TALL + rows.start : TALL + rows.stop, plane(x - a + 1)] = parts[1]
-    taps[STACK:TALL, :] = unit_row()
-    taps[TALL + STACK :, :] = jnp.zeros((16, FLAT), jnp.bfloat16)
+                taps[STACK + rows.start : STACK + rows.stop, plane(x - a + 1)] = parts[1]
 
 
 def network(field, fwd1, fwd2, hidden, weights, u_taps, h_hi, h_lo, work):
@@ -601,7 +600,7 @@
     finish_planes(h_hi, h_lo)
     for pair in range(4):
         cut = slice(pair * 256, pair * 256 + 256)
-        value = jnp.tanh(dot_stacked(fwd1, (u_taps[0:TALL, cut], u_taps[TALL:, cut])))
+        value = jnp.tanh(dot_stacked(fwd1, (u_taps[0:STACK, cut], u_taps[STACK:, cut])))
         hidden[:, cut] = value
         stack_planes(value, 2 * pair, -1, h_hi, h_lo)
     for pair in range(4):
@@ -664,7 +663,11 @@
                     slot = 2 * f + t
                     value = turn(source(f, 2 * p + t), BAND * (slot - g))
                     total = value if total is None else jnp.where(groups == slot, value, total)
-            out[p * 4 + g] = total
+            if len(out.shape) == 3:
+                out[p * 4 + g] = total
+            else:
+                for i in range(out.shape[1]):
+                    out[p * 4 + g, i] = total[2 * i : 2 * i + 2]
 
 
 def gather_modes(recv, f, k, first, rows):
@@ -684,7 +687,7 @@
     table = (to_z[0], to_z[1])
     moved_field = [jnp.concatenate(advected(recv, weights, x), axis=0) for x in range(PLANES)]
     for f in range(2):
-        planes = moved_field if f == 0 else [recv[x, 36:60, :] for x in range(PLANES)]
+        planes = moved_field if f == 0 else [recv[x, 40:64, :] for x in range(PLANES)]
         for k, value in enumerate(mixed(planes, mode_x)):
             modes[f, k] = value
     for f in range(2):
@@ -735,30 +738,55 @@
     )
 
 
+def beside(parts):
+    return jnp.concatenate(parts, axis=1)
+
+
+def part(value, m):
+    return value[:, m * DEPTH : (m + 1) * DEPTH]
+
+
+def two_halves(first, second):
+    low = lax.broadcasted_iota(jnp.int32, first.shape, 1) < DEPTH // 2
+    return jnp.where(low, first, turn(second, DEPTH // 2))
+
+
 def both_kernel(recv, table_in, table_out, out):
-    data = split(recv[...].reshape(16 * 24, DEPTH))
-    modes = dot_stacked(table_in, data)
-    fixed = leray([modes[m * ROWS : (m + 1) * ROWS] for m in range(3)])
-    back = dot_stacked(table_out, split(jnp.concatenate(fixed, axis=0)))
-    wide, rest = back[:512].reshape(16, 32, DEPTH), back[512:].reshape(16, 32, DEPTH)
-    low = lax.broadcasted_iota(jnp.int32, (16, 24, DEPTH), 2) < DEPTH // 2
-    out[:, 0:24, :] = jnp.where(low, wide[:, :24], rest[:, :24])
-    out[:, 24:32, :] = jnp.where(low[:, :8], wide[:, 24:], turn(rest[:, 24:], DEPTH // 2))
-
-
-def one_kernel(recv, table_in, table_out, out):
-    data = split(recv[...].reshape(16 * 24, DEPTH))
-    modes = dot_stacked(table_in, data)
-    modes = modes[: 3 * ROWS] + turn(modes[3 * ROWS :], DEPTH // 2)
-    fixed = leray([modes[m * ROWS : (m + 1) * ROWS] for m in range(3)])
-    back = dot_stacked(table_out, split(jnp.concatenate(fixed, axis=0)))
-    lane = lax.broadcasted_iota(jnp.int32, (256, DEPTH), 1)
-    whole = jnp.where(lane < DEPTH // 2, back[:256], turn(back[256:], DEPTH // 2))
-    out[...] = whole.reshape(16, 16, DEPTH)
+    data = beside([recv[:, 8 * m : 8 * m + 8, :].reshape(ROWS, DEPTH) for m in range(3)])
+    modes = dot_stacked(table_in, split(data))
+    fixed = beside(leray([part(modes, m) for m in range(3)]))
+    back = dot_stacked(table_out, split(fixed))
+    for m in range(3):
+        whole = part(back, m)
+        out[:, 8 * m : 8 * m + 8, :] = whole[:ROWS].reshape(16, SLAB, DEPTH)
+        rim = two_halves(whole[ROWS : ROWS + 32], whole[ROWS + 32 :])
+        for device in range(16):
+            out[device, 24 + 2 * m : 26 + 2 * m, :] = rim[2 * device : 2 * device + 2]
+    out[:, 30:32, :] = jnp.zeros((16, 2, DEPTH), jnp.float32)
+
+
+def one_kernel(recv, table_in, table_out, out, data):
+    for device in range(16):
+        for m in range(3):
+            for i in range(2):
+                first = 4 * device + 2 * i
+                data[m, first : first + 2, :] = recv[device, 2 * m + i]
+            data[m, 64 + 2 * device : 66 + 2 * device, :] = recv[device, 6 + m]
+    modes = dot_stacked(table_in, split(beside([data[m] for m in range(3)])))
+    low, high = modes[:ROWS], modes[ROWS:]
+    fixed = beside(leray([part(low, m) + turn(part(high, m), DEPTH // 2) for m in range(3)]))
+    back = dot_stacked(table_out, split(fixed))
+    for m in range(3):
+        whole = two_halves(part(back, m)[:64], part(back, m)[64:])
+        for device in range(16):
+            out[device, m] = whole[4 * device : 4 * device + 4]
 
 
 def pullback(field, grad, hidden, weights, back2, back1, l_taps, p_hi, p_lo, work, slope):
     slope[...] = jnp.zeros_like(slope)
+    row = lax.broadcasted_iota(jnp.int32, (SLAB, DEPTH), 0)
+    stay = [None] * PLANES
+    pushed = {}
     for x in range(PLANES):
         center = around(field, x, 0, 0)
         source = [-KAPPA * grad[x, m * SLAB : (m + 1) * SLAB, :] for m in range(3)]
@@ -792,19 +820,24 @@
             logits.append(grad_up * plus * rate_up * (1.0 - rate_up))
             logits.append(grad_low * minus * rate_low * (1.0 - rate_low))
             for m in range(3):
-                first = m * REACH + RIM
                 if d == 0:
-                    slope[(x + 1) % PLANES, first : first + SLAB, :] += to_ahead[m]
-                    slope[(x - 1) % PLANES, first : first + SLAB, :] += to_behind[m]
+                    pushed[x, m, 1], pushed[x, m, -1] = to_ahead[m], to_behind[m]
                 elif d == 1:
-                    slope[x, first + 1 : first + 1 + SLAB, :] += to_ahead[m]
-                    slope[x, first - 1 : first - 1 + SLAB, :] += to_behind[m]
+                    first = m * REACH + RIM
+                    down = pltpu.roll(to_ahead[m], 1, 0)
+                    up = pltpu.roll(to_behind[m], SLAB - 1, 0)
+                    own[m] = own[m] + jnp.where(row > 0, down, 0.0) + jnp.where(row < SLAB - 1, up, 0.0)
+                    slope[x, first + SLAB : first + SLAB + 1, :] = down[0:1]
+                    slope[x, first - 1 : first, :] = up[SLAB - 1 :]
                 else:
                     own[m] = own[m] + turn(to_ahead[m], 1) + turn(to_behind[m], -1)
-        for m in range(3):
-            slope[x, m * REACH + RIM : m * REACH + RIM + SLAB, :] += own[m]
+        stay[x] = own
         whole = jnp.concatenate(logits, axis=0)
         stack_logits(whole, x, l_taps)
+    for x in range(PLANES):
+        for m in range(3):
+            value = stay[x][m] + pushed[(x - 1) % PLANES, m, 1] + pushed[(x + 1) % PLANES, m, -1]
+            slope[x, m * REACH + RIM : m * REACH + RIM + SLAB, :] = value
     for pair in range(4):
         cut = slice(pair * 256, pair * 256 + 256)
         value = dot_stacked(back2, (l_taps[0:STACK, cut], l_taps[STACK:, cut]))
@@ -820,9 +853,10 @@
 
 
 def kernel_sums(u_taps, h_hi, h_lo, l_taps, p_hi, p_lo, sums):
-    here = slice(2 * HID, DEEP)
-    sums[0:STACK, :] = dot_stacked(l_taps, (h_hi[here, :], h_lo[here, :]), NT)
-    sums[STACK:, :] = dot_stacked(u_taps, (p_hi[here, :], p_lo[here, :]), NT)
+    for first, taps, high, low in ((0, l_taps, h_hi, h_lo), (144, u_taps, p_hi, p_lo)):
+        left = jnp.concatenate([taps[144:288, :], taps[STACK + 144 : STACK + 288, :]], axis=0)
+        main = dot(left, high[...], NT)
+        sums[first : first + 144, :] = main[:144] + (main[144:] + dot(left[:144], low[...], NT))
 
 
 def second_kernel_body(
@@ -838,8 +872,13 @@
     flat = dot_stacked(stacked(modes[...].reshape(PLANES * 40, DEPTH)), back_z)
     modes[...] = flat.reshape(PLANES, 40, DEPTH)
     for x, value in enumerate(mixed([modes[k] for k in range(PLANES)], mode_x.T)):
-        field[x, 0:40, :] = value
-        field[x, 40:48, :] = jnp.zeros((8, DEPTH), jnp.float32)
+        for m in range(3):
+            first = m * REACH
+            field[x, first : first + RIM, :] = value[24 + 2 * m : 26 + 2 * m]
+            field[x, first + RIM : first + RIM + SLAB, :] = value[8 * m : 8 * m + 8]
+            field[x, first + RIM + SLAB : first + REACH, :] = value[32 + 2 * m : 34 + 2 * m]
+        field[x, 36:37, :] = jnp.ones((1, DEPTH), jnp.float32)
+        field[x, 37:48, :] = jnp.zeros((11, DEPTH), jnp.float32)
     for k in range(PLANES):
         grad[k] = gather_modes(recv, 1, k, 0, 24)
     flat = dot_stacked(stacked(grad[...].reshape(PLANES * 24, DEPTH)), back_z)
@@ -858,64 +897,57 @@
     for h in range(2):
         for k in range(PLANES):
             for m in range(3):
-                rows6[h, k, m * 6 : m * 6 + 6, :] = modes[k, m * REACH + 6 * h : m * REACH + 6 * h + 6, :]
+                first = m * REACH + RIM + 4 * h
+                rows6[h, k, 4 * m : 4 * m + 4, :] = modes[k, first : first + 4, :]
+                first = m * REACH + (RIM + SLAB) * h
+                rows6[h, k, 12 + 2 * m : 14 + 2 * m, :] = modes[k, first : first + 2, :]
             rows6[h, k, 18:24, :] = jnp.zeros((6, DEPTH), jnp.float32)
     scatter_modes(lambda h, k: rows6[h, k], 24, out)
 
 
 def third_kernel_body(
-    mode_x, recv, field, hidden, weights, back2, back1, from_z, old_sums,
-    spread_t, mask, lift, count,
+    mode_x, recv, field, hidden, weights, u_taps, h_hi, h_lo, back2, back1, from_z, old_sums,
+    spread_t, mask, lift,
     out,
-    grad, modes, u_taps, h_hi, h_lo, l_taps, p_hi, p_lo, work, slope, sums, pieces,
+    flat, grad, modes, l_taps, p_hi, p_lo, work, slope, sums, pieces,
 ):
     back_z = (from_z[0], from_z[1])
+    flat[...] = jnp.zeros_like(flat)
+    for device in range(16):
+        for m in range(3):
+            flat[device, 4 * m : 4 * m + 4, :] = recv[device, m]
     for h in range(2):
         for k in range(PLANES):
-            modes[k] = gather_modes(recv, h, k, 0, 16)
-        flat = dot_stacked(stacked(modes[...].reshape(PLANES * 16, DEPTH)), back_z)
-        modes[...] = flat.reshape(PLANES, 16, DEPTH)
+            modes[k] = gather_modes(flat, h, k, 0, 16)
+        moved_back = dot_stacked(stacked(modes[...].reshape(PLANES * 16, DEPTH)), back_z)
+        modes[...] = moved_back.reshape(PLANES, 16, DEPTH)
         for x, value in enumerate(mixed([modes[k] for k in range(PLANES)], mode_x.T)):
             for m in range(3):
                 grad[x, m * SLAB + 4 * h : m * SLAB + 4 * h + 4, :] = value[m * 4 : m * 4 + 4, :]
-    stack_field(field, u_taps)
-    stack_planes(hidden[...], 0, -1, h_hi, h_lo)
-    finish_planes(h_hi, h_lo)
     pullback(field, grad, hidden, weights, back2, back1, l_taps, p_hi, p_lo, work, slope)
     kernel_sums(u_taps, h_hi, h_lo, l_taps, p_hi, p_lo, sums)
     sums[...] += old_sums[...]
     for x in range(PLANES):
-        out[x, 0:40, :] = slope[x, 0:40, :]
-        out[x, 36:40, :] = jnp.zeros((4, DEPTH), jnp.float32)
-    pack_grads(sums, spread_t, mask, lift, count, pieces)
+        out[x, 0:36, :] = slope[x, 0:36, :]
+    pack_grads(sums, spread_t, mask, lift, pieces)
     for x in range(PLANES):
-        out[x, 40:72, :] = pieces[96:128, :]
-
-
-def pack_grads(sums, spread_t, mask, lift, count, pieces):
-    pieces[...] = jnp.zeros_like(pieces)
+        out[x, 36:72, :] = pieces[0:36, :]
+
+
+def pack_grads(sums, spread_t, mask, lift, pieces):
     whole = split(sums[...])
+    empty = jnp.zeros((32, 512 - DEEP), jnp.float32)
+    rows = []
     for b in range(3):
-        rows = dot(spread_t[...], whole[0] * mask[b]) + dot(spread_t[...], whole[1] * mask[b])
-        parts = split(rows)
-        pieces[0:96, :] = dot(parts[0], lift[...]) + dot(parts[1], lift[...])
-        for c in range(3):
-            slot = b * 3 + c
-            if slot < 8:
-                pieces[96:123, :] += turn(pieces[c * 27 : c * 27 + 27, :], 16 * slot)
-            else:
-                for part in range(7):
-                    first = c * 27 + part * 4
-                    count_rows = min(4, c * 27 + 27 - first)
-                    pieces[123 : 123 + count_rows, :] += turn(
-                        pieces[first : first + count_rows, :], 16 * part
-                    )
-    parts = split(sums[2 * STACK :, :])
-    total = dot(parts[0], lift[...]) + dot(parts[1], lift[...])
-    parts = split(sums[4 * LOG : 5 * LOG, 128:BROAD])
-    across = ((0,), (0,))
-    other = dot(parts[0], count[...], across) + dot(parts[1], count[...], across)
-    pieces[127:128, :] = total[0:1, :] + other[HID - 128 : HID - 127, :]
+        rows.append(dot(spread_t[...], whole[0] * mask[b]) + dot(spread_t[...], whole[1] * mask[b]))
+        rows.append(empty)
+    placed = dot(stacked(beside(rows)), lift[...])
+    placed = placed[:32] + placed[32:]
+    pieces[0:28, :] = placed[0:28, 0:128]
+    total = placed[0:8, 128:]
+    for i in range(1, 4):
+        total = total + turn(placed[8 * i : 8 * i + 8, 128:], 16 * i)
+    pieces[28:36, :] = total
 
 
 def fold_kernel(recv, main, edge, ext):
@@ -924,14 +956,15 @@
     for q in range(PLANES):
         for m in range(3):
             ext[m, 8 * q + 6 : 8 * q + 18, :] += recv[q, m * REACH : (m + 1) * REACH, :]
-        block = recv[q, 40:72, :]
+        block = recv[q, 36:72, :]
         total = block if total is None else total + block
     for m in range(3):
         main[m, 0] = ext[m, 8:72, :]
         edge[m * 8 : m * 8 + 2, :] = ext[m, 72:74, :]
         edge[m * 8 + 2 : m * 8 + 4, :] = ext[m, 6:8, :]
         edge[m * 8 + 4 : m * 8 + 8, :] = jnp.zeros((4, DEPTH), jnp.float32)
-    edge[24:56, :] = total
+    edge[24:60, :] = total
+    edge[60:64, :] = jnp.zeros((4, DEPTH), jnp.float32)
 
 
 def last_kernel(main, edge, other, out, first, end1, second, end2, turned):
@@ -939,24 +972,25 @@
         out[m, 0] = main[m, 0]
         out[m, 0, 0:2, :] += other[m * 8 : m * 8 + 2, :]
         out[m, 0, 62:64, :] += other[m * 8 + 2 : m * 8 + 4, :]
-    grads = edge[24:56, :] + other[24:56, :]
+    grads = edge[24:64, :] + other[24:64, :]
     for slot in range(8):
         turned[slot] = turn(grads, -16 * slot)
     for b in range(3):
         for a in range(3):
             for e in range(3):
                 for i in range(9):
-                    row = (a * 3 + e) * 6 + i if i < 6 else 54 + (a * 3 + e) * 3 + i - 6
-                    slot, inner = b * 3 + row // 27, row % 27
-                    if slot == 8:
-                        slot, inner = inner // 4, 27 + inner % 4
+                    row = e * 6 + i if i < 6 else 18 + e * 3 + i - 6
+                    slot = 3 * b + a
+                    slot, inner = (slot, row) if slot < 8 else (row // 8, 28 + row % 8)
                     line = turned[slot, inner, 0:16]
                     if i < 6:
                         second[i * 9 + a * 3 + b, e, :] = line
                     else:
                         first[(i - 6) * 9 + a * 3 + b, e, :] = line
-    end1[...] = turned[0, 31:32, 0:16]
-    end2[...] = turned[1, 31:32, 0:6]
+    end1[...] = turned[1, 27:28, 0:16]
+    for o in range(COEFFS):
+        slot, inner = (4, 34 + o) if o < 2 else (5, 26 + o)
+        end2[0:1, o : o + 1] = turned[slot, inner : inner + 1, 0:1]
 
 
 def slab_device(velocity, cotangent, first_kernel, first_bias, second_kernel, second_bias):
@@ -978,7 +1012,7 @@
         weights_kernel,
         [
             shape(288, DEEP, kind=half),
-            shape(2 * HID, TALL, kind=half),
+            shape(2 * HID, STACK, kind=half),
             shape(2 * HID, STACK, kind=half),
             shape(288, DEEP, kind=half),
             shape(2, DEPTH, DEPTH, kind=half),
@@ -1002,12 +1036,19 @@
     )
 
     near = lambda rows: [b16(rows, FLAT), b16(rows, FLAT)]
-    stacks = near(2 * TALL)[:1] + near(DEEP) + near(2 * STACK)[:1] + near(DEEP)
-    sent, hidden, weights = call(
+    stacks = near(2 * STACK)[:1] + near(DEEP) + near(2 * STACK)[:1] + near(DEEP)
+    sent, hidden, weights, *kept = call(
         functools.partial(first_kernel_body, mode_x),
-        [shape(16, 24, DEPTH), shape(HID, FLAT), shape(LOG, FLAT)],
+        [
+            shape(16, 24, DEPTH),
+            shape(HID, FLAT),
+            shape(LOG, FLAT),
+            shape(2 * STACK, FLAT, kind=half),
+            shape(DEEP, FLAT, kind=half),
+            shape(DEEP, FLAT, kind=half),
+        ],
         (recv, fwd1, fwd2, to_z),
-        near(2 * TALL)[:1] + near(DEEP) + [f32(144, FLAT), f32(2, PLANES, 24, DEPTH)],
+        [f32(144, FLAT), f32(2, PLANES, 24, DEPTH)],
     )
     both = ("px", "py")
     moved_modes = lax.all_to_all(sent, both, 0, 0)
@@ -1016,7 +1057,7 @@
 
     sent, sums = call(
         functools.partial(second_kernel_body, mode_x),
-        [shape(16, 24, DEPTH), shape(STACK + TALL, BROAD)],
+        [shape(16, 9, 2, DEPTH), shape(288, DEEP)],
         (moved_modes, fwd1, fwd2, back2, back1, to_z, c["from_z"]),
         [
             f32(PLANES, 48, DEPTH),
@@ -1031,28 +1072,33 @@
         + stacks,
     )
     moved_modes = lax.all_to_all(sent, both, 0, 0)
-    moved_modes = call(one_kernel, shape(16, 16, DEPTH), (moved_modes, c["one_in"], c["one_out"]))
+    moved_modes = call(
+        one_kernel,
+        shape(16, 3, 4, DEPTH),
+        (moved_modes, c["one_in"], c["one_out"]),
+        [f32(3, 96, DEPTH)],
+    )
     moved_modes = lax.all_to_all(moved_modes, both, 0, 0)
 
     sent = call(
         functools.partial(third_kernel_body, mode_x),
         shape(PLANES, 72, DEPTH),
         (
-            moved_modes, recv, hidden, weights, back2, back1, c["from_z"], sums,
-            c["spread_t"], c["mask"], c["lift"], c["count"],
+            moved_modes, recv, hidden, weights, *kept, back2, back1, c["from_z"], sums,
+            c["spread_t"], c["mask"], c["lift"],
         ),
-        [f32(PLANES, 24, DEPTH), f32(PLANES, 16, DEPTH)]
-        + stacks
+        [f32(16, 16, DEPTH), f32(PLANES, 24, DEPTH), f32(PLANES, 16, DEPTH)]
+        + stacks[3:]
         + [
             f32(144, FLAT),
             f32(PLANES, 48, DEPTH),
-            f32(STACK + TALL, BROAD),
-            f32(128, DEPTH),
+            f32(288, DEEP),
+            f32(36, DEPTH),
         ],
     )
     recv = lax.all_to_all(sent, "px", 0, 0)
     main, edge = call(
-        fold_kernel, [shape(3, 1, 64, DEPTH), shape(56, DEPTH)], (recv,), [f32(3, 80, DEPTH)]
+        fold_kernel, [shape(3, 1, 64, DEPTH), shape(64, DEPTH)], (recv,), [f32(3, 80, DEPTH)]
     )
     other = lax.ppermute(edge, "py", swap)
     grad_velocity, first, end1, second, end2 = call(
@@ -1065,7 +1111,7 @@
             shape(1, COEFFS),
         ],
         (main, edge, other),
-        [f32(8, 32, DEPTH)],
+        [f32(8, 40, DEPTH)],
     )
     return (
         grad_velocity,

time: 98.6 us -> 95.8 us (0.972)
  waiting for transfers between devices: 6.63 us -> 2.76 us
  local copies, waits for them, and re-layouts: 1.85 us -> 5.68 us
  Pallas kernels: 21.3 us -> 18.8 us
    all_to_all x1, waiting for transfers between devices: 5.44 us -> 1.57 us  [slab_device(): recv = lax.all_to_all(packed, 'px', 0, 0)]
    unnamed x32 -> x30, local copies, waits for them, and re-layouts: 1.85 us -> 5.68 us
    pallas_call x10, Pallas kernels: 21.3 us -> 18.8 us  [call(): pl.pallas_call(kernel, out_shape=outs, in_specs=[pl.BlockSpec(memory_spac...]
where the time goes in v4:
time: 95.8 us; the launch traced here: 95.2 us
  blocking collectives  59.7 us (62%)
  Pallas kernels  18.8 us (20%)
  starting transfers between devices  7.53 us (8%)
  local copies, waits for them, and re-layouts  5.68 us (6%)
  waiting for transfers between devices  2.76 us (3%)
    all_to_all x2, blocking collectives, slab_device(): moved_modes = lax.all_to_all(sent, both, 0, 0)  24.4 us
    all_to_all x2, blocking collectives, slab_device(): moved_modes = lax.all_to_all(moved_modes, both, 0, 0)  22.6 us
    pallas_call x10, Pallas kernels, call(): pl.pallas_call(kernel, out_shape=outs, in_specs=[pl.BlockSpec(memory_spac...  18.8 us
    all_to_all x1, blocking collectives, slab_device(): recv = lax.all_to_all(sent, 'px', 0, 0)  12.6 us
    all_to_all x1, starting transfers between devices, slab_device(): recv = lax.all_to_all(packed, 'px', 0, 0)  6.95 us
    unnamed x30, local copies, waits for them, and re-layouts  5.68 us
  transfers between devices with their start and end apart: 3, of which 2 were waited for; matrix products, arithmetic and copies ran while one was open for 0% of the time, Pallas kernels for 4%

profile of v4, /device:TPU:0, one launch (start us, length us, event | category | flops | bytes accessed | tf_op | source)
XLA Modules:
  0.0 95.2 jit_solution(6383346909072270693)
XLA Ops:
  0.6 0.5 collective-permute-start
  1.2 0.9 copy-done.5
  2.0 0.9 copy-done.6
  3.0 0.7 shard_map.183
  3.7 6.9 %all-to-all-start = ((f32[8,64,128]{2,1,0:T(8,128)}), f32[8,64,128]{2,1,0:T(8,128)S(1)}, u32[]{:S(2)}, u32[]{:S(2)}) async-start(f32[8,64,128]{2,1,0:T(8,128)} %shard_map.183), calls=%async_computation | async-start | bytes 524288 | tf_op jit(solution)/shard_map/all_to_all | solution.py:1009
  10.7 0.9 copy-done.4
  11.6 0.8 copy-done.10
  12.4 0.8 copy-done.11
  13.2 0.7 copy-done.13
  13.9 0.7 copy-done.14
  14.5 4.1 %shard_map.184 = (bf16[288,496]{1,0:T(8,128)(2,1)S(1)}, bf16[320,432]{1,0:T(8,128)(2,1)S(1)}, bf16[320,432]{1,0:T(8,128)(2,1)S(1)}, bf16[288,496]{1,0:T(8,128)(2,1)S(1)}, bf16[2,128,128]{2,1,0:T(8,128)(2,1)S(1)}) custom-call(f32[27,3,16]{2,1,0:T(4,128)S(1)} %bitcast.17, f32[54,3,16]{2,1,0:T(4,128)S(1)} %bitcast.16, f32[1,16]{1,0:T(1,128)S(1)} %bitcast.18, ...), custom_call_target="tpu_custom_call" | custom-call | flops 1 | bytes 1 | tf_op jit(solution)/shard_map/pallas_call | solution.py:431
  18.7 1.6 %all-to-all-done.recv.field = f32[8,64,128]{2,1,0:T(8,128)S(1)} async-done(((f32[8,64,128]{2,1,0:T(8,128)}), f32[8,64,128]{2,1,0:T(8,128)S(1)}, u32[]{:S(2)}, u32[]{:S(2)}) %all-to-all-start) | async-done | bytes 262176 | tf_op jit(solution)/shard_map/all_to_all | solution.py:1009
  20.2 2.1 %shard_map.185 = (f32[16,24,128]{2,1,0:T(8,128)S(1)}, f32[160,1024]{1,0:T(8,128)S(1)}, f32[48,1024]{1,0:T(8,128)S(1)}, bf16[864,1024]{1,0:T(8,128)(2,1)S(1)}, bf...) custom-call(f32[8,64,128]{2,1,0:T(8,128)S(1)} %all-to-all-done.recv.field, ...), custom_call_target="tpu_custom_call" | custom-call | tf_op jit(solution)/shard_map/pallas_call | solution.py:431
  22.4 13.5 %all_to_all.30.recv = f32[16,24,128]{2,1,0:T(8,128)S(1)} all-to-all(f32[16,24,128]{2,1,0:T(8,128)S(1)} %get-tuple-element.28), channel_id=1, replica_groups=mesh['groups'=2,'px'=8,'py'=2] {'px','py'}, dimensions={0} | all-to-all | bytes 393216 | tf_op jit(solution)/shard_map/all_to_all | solution.py:1054
  35.9 0.8 shard_map.186
  36.6 12.6 %all_to_all.31.recv = f32[16,32,128]{2,1,0:T(8,128)S(1)} all-to-all(f32[16,32,128]{2,1,0:T(8,128)S(1)} %shard_map.186), channel_id=1, replica_groups=mesh['groups'=2,'px'=8,'py'=2] {'px','py'}, dimensions={0} | all-to-all | bytes 524288 | tf_op jit(solution)/shard_map/all_to_all | solution.py:1056
  49.3 5.2 %shard_map.187 = (f32[16,9,2,128]{3,2,1,0:T(2,128)S(1)}, f32[288,496]{1,0:T(8,128)S(1)}) custom-call(f32[16,32,128]{2,1,0:T(8,128)S(1)} %all_to_all.31.recv, bf16[320,432]{1,0:T(8,128)(2,1)S(1)} %get-tuple-element.25.fwd1, bf16[288,496]{1,0:T(8,128)(2,1)S(1)} %get-tuple-element.26.fwd2, bf16[320,432]{1,0:T(8,128)(2,1)S(1)} %get-tuple-element.29.back2, ...), custom_call_target="tpu_custom_call" | custom-call | tf_op jit(solution)/shard_map/pallas_call | solution.py:431
  54.5 11.0 %all_to_all.32.recv = f32[16,9,2,128]{3,2,1,0:T(2,128)S(1)} all-to-all(f32[16,9,2,128]{3,2,1,0:T(2,128)S(1)} %get-tuple-element.31), channel_id=1, replica_groups=mesh['groups'=2,'px'=8,'py'=2] {'px','py'}, dimensions={0} | all-to-all | bytes 294912 | tf_op jit(solution)/shard_map/all_to_all | solution.py:1074
  65.5 1.0 %shard_map.188 = f32[16,3,4,128]{3,2,1,0:T(4,128)S(1)} custom-call(f32[16,9,2,128]{3,2,1,0:T(2,128)S(1)} %all_to_all.32.recv, bf16[512,96]{1,0:T(8,128)(2,1)S(1)} %copy-done.3, bf16[256,128]{1,0:T(8,128)(2,1)S(1)} %copy-done.8), custom_call_target="tpu_custom_call" | custom-call | tf_op jit(solution)/shard_map/pallas_call | solution.py:431
  66.5 10.0 %all_to_all.33.recv = f32[16,3,4,128]{3,2,1,0:T(4,128)S(1)} all-to-all(f32[16,3,4,128]{3,2,1,0:T(4,128)S(1)} %shard_map.188), channel_id=1, replica_groups=mesh['groups'=2,'px'=8,'py'=2] {'px','py'}, dimensions={0} | all-to-all | bytes 196608 | tf_op jit(solution)/shard_map/all_to_all | solution.py:1081
  76.5 3.9 %shard_map.189 = f32[8,72,128]{2,1,0:T(8,128)S(1)} custom-call(f32[16,3,4,128]{3,2,1,0:T(4,128)S(1)} %all_to_all.33.recv, f32[8,64,128]{2,1,0:T(8,128)S(1)} %all-to-all-done.recv.field, f32[160,1024]{1,0:T(8,128)S(1)} %get-tuple-element.32.hidden, f32[48,1024]{1,0:T(8,128)S(1)} %get-tuple-element.33.weights, bf16[864,1024]{1,0:T(8,128)(2,1)S(1)} %get-tuple-element.34.u_taps, ...), custom_call_target="tpu_custom_call" | custom-call | tf_op jit(solution)/shard_map/pallas_call | solution.py:431
  80.4 12.6 %all_to_all.34.recv = f32[8,72,128]{2,1,0:T(8,128)S(1)} all-to-all(f32[8,72,128]{2,1,0:T(8,128)S(1)} %shard_map.189), channel_id=1, replica_groups=mesh['groups'=2,'px'=8,'py'=2] {'px'}, dimensions={0} | all-to-all | bytes 589824 | tf_op jit(solution)/shard_map/all_to_all | solution.py:1099
  93.1 1.2 %collective-permute-done.1.other = f32[64,128]{1,0:T(8,128)S(1)} collective-permute-done((f32[64,128]{1,0:T(8,128)S(1)}, f32[64,128]{1,0:T(8,128)S(1)}, u32[]{:S(2)}, u32[]{:S(2)}) %collective-permute-start.1) | collective-permute-done | bytes 32800 | tf_op jit(solution)/shard_map/ppermute | solution.py:1103
  94.3 0.9 shard_map.191
  (27 shorter events, 0.2 us)
Async XLA Ops:
  0.6 2.4 %collective-permute-start = (f32[3,1,64,128]{3,2,1,0:T(8,128)}, f32[3,1,64,128]{3,2,1,0:T(8,128)S(1)}, u32[]{:S(2)}, u32[]{:S(2)}) collective-permute-start(f32[3,1,64,128]{3,2,1,0:T(8,128)} %field.1), channel_id=1, source_target_pairs={{0,1},{1,0},{2,3},{3,2},{4,5},{5,4},{6,7},{7,6},{8,9},{9,8},{10,11... | collective-permute-start | bytes 294920 | tf_op jit(solution)/shard_map/ppermute | solution.py:1004
  1.1 0.9 copy-start.5
  2.0 0.9 copy-start.6
  2.9 32.9 %copy-start.7 = (bf16[384,128]{1,0:T(8,128)(2,1)S(1)}, bf16[384,128]{1,0:T(8,128)(2,1)}, u32[]{:S(2)}) copy-start(bf16[384,128]{1,0:T(8,128)(2,1)} %constant.20.clone.table_out) | copy-start | bytes 294916
  2.9 32.9 %copy-start.9 = (bf16[256,128]{1,0:T(8,128)(2,1)S(1)}, bf16[256,128]{1,0:T(8,128)(2,1)}, u32[]{:S(2)}) copy-start(bf16[256,128]{1,0:T(8,128)(2,1)} %constant.19.clone.table_in) | copy-start | bytes 196612
  3.7 45.6 %copy-start.2 = (bf16[2,128,128]{2,1,0:T(8,128)(2,1)S(1)}, bf16[2,128,128]{2,1,0:T(8,128)(2,1)}, u32[]{:S(2)}) copy-start(bf16[2,128,128]{2,1,0:T(8,128)(2,1)} %constant.21.clone.from_z) | copy-start | bytes 196612
  3.7 16.5 %all-to-all-start = ((f32[8,64,128]{2,1,0:T(8,128)}), f32[8,64,128]{2,1,0:T(8,128)S(1)}, u32[]{:S(2)}, u32[]{:S(2)}) async-start(f32[8,64,128]{2,1,0:T(8,128)} %shard_map.183), calls=%async_computation | async-start | bytes 524288 | tf_op jit(solution)/shard_map/all_to_all | solution.py:1009
  10.7 0.9 copy-start.4
  11.6 0.8 copy-start.10
  12.4 0.8 copy-start.11
  13.2 0.7 copy-start.13
  13.9 0.7 copy-start.14
  22.3 43.2 %copy-start.3 = (bf16[512,96]{1,0:T(8,128)(2,1)S(1)}, bf16[512,96]{1,0:T(8,128)(2,1)}, u32[]{:S(2)}) copy-start(bf16[512,96]{1,0:T(8,128)(2,1)} %constant.22.clone.table_in) | copy-start | bytes 294916
  22.3 43.2 %copy-start.8 = (bf16[256,128]{1,0:T(8,128)(2,1)S(1)}, bf16[256,128]{1,0:T(8,128)(2,1)}, u32[]{:S(2)}) copy-start(bf16[256,128]{1,0:T(8,128)(2,1)} %constant.23.clone.table_out) | copy-start | bytes 196612
  35.8 40.6 %copy-start = (bf16[3,288,496]{2,1,0:T(8,128)(2,1)S(1)}, bf16[3,288,496]{2,1,0:T(8,128)(2,1)}, u32[]{:S(2)}) copy-start(bf16[3,288,496]{2,1,0:T(8,128)(2,1)} %constant.25.clone.mask) | copy-start | bytes 2571268
  35.8 40.6 %copy-start.1 = (bf16[1536,256]{1,0:T(8,128)(2,1)S(1)}, bf16[1536,256]{1,0:T(8,128)(2,1)}, u32[]{:S(2)}) copy-start(bf16[1536,256]{1,0:T(8,128)(2,1)} %constant.26.clone.lift) | copy-start | bytes 2359300
  35.8 40.6 %copy-start.12 = (bf16[32,288]{1,0:T(8,128)(2,1)S(1)}, bf16[32,288]{1,0:T(8,128)(2,1)}, u32[]{:S(2)}) copy-start(bf16[32,288]{1,0:T(8,128)(2,1)} %constant.24.clone.spread_t) | copy-start | bytes 55300
  93.0 1.3 %collective-permute-start.1 = (f32[64,128]{1,0:T(8,128)S(1)}, f32[64,128]{1,0:T(8,128)S(1)}, u32[]{:S(2)}, u32[]{:S(2)}) collective-permute-start(f32[64,128]{1,0:T(8,128)S(1)} %get-tuple-element.39.edge), channel_id=1, source_target_pairs={{0,1},{1,0},{2,3},{3,2},{4,5},{5,4},{6,7},{7,6},{8,9},{9,8},{10,11... | collective-permute-start | bytes 98312 | tf_op jit(solution)/shard_map/ppermute | solution.py:1103

commit v5 on v4

--- a/solution.py
+++ b/solution.py
@@ -297,6 +297,7 @@
 LOG = COEFFS * SLAB
 STACK = 9 * 48
 UNIT = 36
+BROAD = HID + 16
 DEEP = 3 * HID + 16
 PLACE = (0, 2, 1)
 FLAT = PLANES * DEPTH
@@ -314,8 +315,14 @@
     return np.stack(rows)
 
 
-def stacked_table(table):
-    return np.concatenate(halves(table))
+def wide_table(table):
+    high, low = halves(table)
+    return np.concatenate([high, low, high], axis=1)
+
+
+def tall_table(table):
+    high, low = halves(table)
+    return np.concatenate([high, high, low])
 
 
 def halves(table):
@@ -330,8 +337,6 @@
 
 @functools.cache
 def constants():
-    basis_x = real_basis(PLANES)
-    mode_x = np.stack([basis_x[(k // 2) + (PLANES // 2) * (k % 2)] for k in range(PLANES)])
     basis_z = real_basis(DEPTH)
     order = []
     for group in range(4):
@@ -382,13 +387,12 @@
     lift = lift.reshape(3 * 512, 256)
     half = jnp.bfloat16
     return dict(
-        mode_x=mode_x,
-        to_z=np.stack(halves(mode_z.T)),
-        from_z=np.stack(halves(mode_z)),
-        both_in=stacked_table(both_in),
-        both_out=stacked_table(both_out),
-        one_in=stacked_table(one_in),
-        one_out=stacked_table(one_out),
+        to_z=tall_table(mode_z.T),
+        from_z=tall_table(mode_z),
+        both_in=wide_table(both_in),
+        both_out=wide_table(both_out),
+        one_in=wide_table(one_in),
+        one_out=wide_table(one_out),
         spread_t=np.ascontiguousarray(spread.T).astype(half),
         mask=mask.astype(half),
         lift=lift.astype(half),
@@ -408,6 +412,15 @@
     rows = left.shape[0] // 2
     main = dot(left[...], right[0], dims)
     return main[:rows] + (main[rows:] + dot(left[0:rows, :], right[1], dims))
+
+
+def dot_wide(left, right):
+    return dot(left[...], jnp.concatenate([right[0], right[0], right[1]], axis=0))
+
+
+def widened(value):
+    high, low = split(value)
+    return jnp.concatenate([high, low, high], axis=1)
 
 
 def stacked(value):
@@ -560,39 +573,49 @@
     return jnp.where(row == 0, 1.0, 0.0).astype(jnp.bfloat16)
 
 
-def stack_planes(value, first, sign, high, low):
+def stack_planes(value, cut, high, low):
     parts = split(value)
-    for i in range(value.shape[1] // DEPTH):
-        for a in range(3):
-            rows = slice(PLACE[a] * HID, PLACE[a] * HID + HID)
-            to = plane(first + i + sign * (a - 1))
-            high[rows, to] = parts[0][:, i * DEPTH : (i + 1) * DEPTH]
-            low[rows, to] = parts[1][:, i * DEPTH : (i + 1) * DEPTH]
+    high[0:HID, cut] = parts[0]
+    low[0:HID, cut] = parts[1]
 
 
 def finish_planes(high, low):
-    high[3 * HID :, :] = unit_row()
-    low[3 * HID :, :] = jnp.zeros((16, FLAT), jnp.bfloat16)
-
-
-def stack_logits(whole, x, l_taps):
+    high[HID:, :] = unit_row()
+    low[HID:, :] = jnp.zeros((16, FLAT), jnp.bfloat16)
+
+
+def shifted(taps, first_row, rows, first, count, shift):
+    return beside(
+        [taps[first_row : first_row + rows, plane(first + i + shift)] for i in range(count)]
+    )
+
+
+def nine(taps, half, first, count, sign):
+    return jnp.concatenate(
+        [shifted(taps, 144 * half, 144, first, count, sign * (a - 1)) for a in range(3)], axis=0
+    )
+
+
+def three(taps, first, count, sign):
+    return jnp.concatenate(
+        [shifted(taps, 0, HID, first, count, sign * shift) for shift in (-1, 1, 0)]
+        + [shifted(taps, HID, 16, first, count, 0)],
+        axis=0,
+    )
+
+
+def stack_logits(whole, x, taps):
     for e in range(3):
-        parts = split(turn(whole, e - 1))
-        for a in range(3):
-            for half in range(2):
-                first = half * STACK + (a * 3 + e) * 48
-                l_taps[first : first + 48, plane(x + a - 1)] = parts[half]
+        for half, part_of in enumerate(split(turn(whole, e - 1))):
+            taps[144 * half + 48 * e : 144 * half + 48 * e + 48, plane(x)] = part_of
 
 
 def stack_field(field, taps):
     for x in range(PLANES):
         whole = field[x, 0:48, :]
         for e in range(3):
-            parts = split(turn(whole, 1 - e))
-            for a in range(3):
-                rows = slice((a * 3 + e) * 48, (a * 3 + e) * 48 + 48)
-                taps[rows, plane(x - a + 1)] = parts[0]
-                taps[STACK + rows.start : STACK + rows.stop, plane(x - a + 1)] = parts[1]
+            for half, part_of in enumerate(split(turn(whole, 1 - e))):
+                taps[144 * half + 48 * e : 144 * half + 48 * e + 48, plane(x)] = part_of
 
 
 def network(field, fwd1, fwd2, hidden, weights, u_taps, h_hi, h_lo, work):
@@ -600,12 +623,13 @@
     finish_planes(h_hi, h_lo)
     for pair in range(4):
         cut = slice(pair * 256, pair * 256 + 256)
-        value = jnp.tanh(dot_stacked(fwd1, (u_taps[0:STACK, cut], u_taps[STACK:, cut])))
+        taps = (nine(u_taps, 0, 2 * pair, 2, 1), nine(u_taps, 1, 2 * pair, 2, 1))
+        value = jnp.tanh(dot_stacked(fwd1, taps))
         hidden[:, cut] = value
-        stack_planes(value, 2 * pair, -1, h_hi, h_lo)
+        stack_planes(value, cut, h_hi, h_lo)
     for pair in range(4):
         cut = slice(pair * 256, pair * 256 + 256)
-        work[:, cut] = dot_stacked(fwd2, (h_hi[:, cut], h_lo[:, cut]))
+        work[:, cut] = dot_stacked(fwd2, (three(h_hi, 2 * pair, 2, 1), three(h_lo, 2 * pair, 2, 1)))
     for x in range(PLANES):
         total = work[LOG : 2 * LOG, plane(x)]
         total = total + turn(work[0:LOG, plane(x)], 1) + turn(work[2 * LOG : 3 * LOG, plane(x)], -1)
@@ -638,15 +662,34 @@
     return [center[m] - KAPPA * total[m] for m in range(3)]
 
 
-def mixed(values, table):
-    outs = []
-    for row in table:
-        total = None
-        for weight, value in zip(row, values):
-            term = value * float(weight)
-            total = term if total is None else total + term
-        outs.append(total)
-    return outs
+ROOT = math.sqrt(0.5)
+
+
+def to_modes(x):
+    s = [x[i] + x[i + 4] for i in range(4)]
+    d = [x[i] - x[i + 4] for i in range(4)]
+    even, odd = s[0] + s[2], s[1] + s[3]
+    up, down = ROOT * (d[1] + d[3]), ROOT * (d[1] - d[3])
+    scale = 0.5 * ROOT
+    return [
+        scale * (even + odd),
+        scale * (even - odd),
+        0.5 * (d[0] + down),
+        0.5 * (up + d[2]),
+        0.5 * (s[0] - s[2]),
+        0.5 * (s[1] - s[3]),
+        0.5 * (d[0] - down),
+        0.5 * (up - d[2]),
+    ]
+
+
+def from_modes(v):
+    even, odd = 0.5 * ROOT * (v[0] + v[1]), 0.5 * ROOT * (v[0] - v[1])
+    cos, sin = 0.5 * v[4], 0.5 * v[5]
+    e = [even + cos, odd + sin, even - cos, odd - sin]
+    across, along = 0.5 * ROOT * (v[2] - v[6]), 0.5 * ROOT * (v[3] + v[7])
+    o = [0.5 * (v[2] + v[6]), along + across, 0.5 * (v[3] - v[7]), along - across]
+    return [e[i] + o[i] for i in range(4)] + [e[i] - o[i] for i in range(4)]
 
 
 def lane_groups(size):
@@ -681,18 +724,18 @@
 
 
 def first_kernel_body(
-    mode_x, recv, fwd1, fwd2, to_z, out, hidden, weights, u_taps, h_hi, h_lo, work, modes
+    recv, fwd1, fwd2, to_z, out, hidden, weights, u_taps, h_hi, h_lo, work, modes
 ):
     network(recv, fwd1, fwd2, hidden, weights, u_taps, h_hi, h_lo, work)
-    table = (to_z[0], to_z[1])
+    table = to_z[...]
     moved_field = [jnp.concatenate(advected(recv, weights, x), axis=0) for x in range(PLANES)]
     for f in range(2):
         planes = moved_field if f == 0 else [recv[x, 40:64, :] for x in range(PLANES)]
-        for k, value in enumerate(mixed(planes, mode_x)):
+        for k, value in enumerate(to_modes(planes)):
             modes[f, k] = value
     for f in range(2):
         flat = modes[f].reshape(PLANES * 24, DEPTH)
-        modes[f] = dot_stacked(stacked(flat), table).reshape(PLANES, 24, DEPTH)
+        modes[f] = dot(widened(flat), table).reshape(PLANES, 24, DEPTH)
     scatter_modes(lambda f, k: modes[f, k], 24, out)
 
 
@@ -753,9 +796,9 @@
 
 def both_kernel(recv, table_in, table_out, out):
     data = beside([recv[:, 8 * m : 8 * m + 8, :].reshape(ROWS, DEPTH) for m in range(3)])
-    modes = dot_stacked(table_in, split(data))
+    modes = dot_wide(table_in, split(data))
     fixed = beside(leray([part(modes, m) for m in range(3)]))
-    back = dot_stacked(table_out, split(fixed))
+    back = dot_wide(table_out, split(fixed))
     for m in range(3):
         whole = part(back, m)
         out[:, 8 * m : 8 * m + 8, :] = whole[:ROWS].reshape(16, SLAB, DEPTH)
@@ -772,17 +815,17 @@
                 first = 4 * device + 2 * i
                 data[m, first : first + 2, :] = recv[device, 2 * m + i]
             data[m, 64 + 2 * device : 66 + 2 * device, :] = recv[device, 6 + m]
-    modes = dot_stacked(table_in, split(beside([data[m] for m in range(3)])))
+    modes = dot_wide(table_in, split(beside([data[m] for m in range(3)])))
     low, high = modes[:ROWS], modes[ROWS:]
     fixed = beside(leray([part(low, m) + turn(part(high, m), DEPTH // 2) for m in range(3)]))
-    back = dot_stacked(table_out, split(fixed))
+    back = dot_wide(table_out, split(fixed))
     for m in range(3):
         whole = two_halves(part(back, m)[:64], part(back, m)[64:])
         for device in range(16):
             out[device, m] = whole[4 * device : 4 * device + 4]
 
 
-def pullback(field, grad, hidden, weights, back2, back1, l_taps, p_hi, p_lo, work, slope):
+def pullback(field, grad, hidden, weights, back2, back1, l_taps, p_hi, p_lo, work, slope, middle, late):
     slope[...] = jnp.zeros_like(slope)
     row = lax.broadcasted_iota(jnp.int32, (SLAB, DEPTH), 0)
     stay = [None] * PLANES
@@ -840,38 +883,38 @@
             slope[x, m * REACH + RIM : m * REACH + RIM + SLAB, :] = value
     for pair in range(4):
         cut = slice(pair * 256, pair * 256 + 256)
-        value = dot_stacked(back2, (l_taps[0:STACK, cut], l_taps[STACK:, cut]))
+        taps = (nine(l_taps, 0, 2 * pair, 2, -1), nine(l_taps, 1, 2 * pair, 2, -1))
+        value = dot_stacked(back2, taps)
         value = value * (1.0 - hidden[:, cut] * hidden[:, cut])
-        stack_planes(value, 2 * pair, 1, p_hi, p_lo)
+        stack_planes(value, cut, p_hi, p_lo)
     finish_planes(p_hi, p_lo)
+    middle()
     for pair in range(4):
         cut = slice(pair * 256, pair * 256 + 256)
-        work[:, cut] = dot_stacked(back1, (p_hi[:, cut], p_lo[:, cut]))
+        work[:, cut] = dot_stacked(back1, (three(p_hi, 2 * pair, 2, -1), three(p_lo, 2 * pair, 2, -1)))
+    late()
     for x in range(PLANES):
         total = slope[x, 0:40, :] + work[48:88, plane(x)]
         slope[x, 0:40, :] = total + turn(work[0:40, plane(x)], -1) + turn(work[96:136, plane(x)], 1)
 
 
-def kernel_sums(u_taps, h_hi, h_lo, l_taps, p_hi, p_lo, sums):
-    for first, taps, high, low in ((0, l_taps, h_hi, h_lo), (144, u_taps, p_hi, p_lo)):
-        left = jnp.concatenate([taps[144:288, :], taps[STACK + 144 : STACK + 288, :]], axis=0)
-        main = dot(left, high[...], NT)
-        sums[first : first + 144, :] = main[:144] + (main[144:] + dot(left[:144], low[...], NT))
+def kernel_sums(taps, high, low, sign):
+    return dot_stacked(taps, (three(high, 0, PLANES, sign), three(low, 0, PLANES, sign)), NT)
 
 
 def second_kernel_body(
-    mode_x, recv, fwd1, fwd2, back2, back1, to_z, from_z,
+    recv, fwd1, fwd2, back2, back1, to_z, from_z,
     out, sums,
     field, hidden, grad, modes, rows6, weights, work, slope,
     u_taps, h_hi, h_lo, l_taps, p_hi, p_lo,
 ):
-    back_z = (from_z[0], from_z[1])
+    back_z = from_z[...]
     for k in range(PLANES):
         modes[k, 0:32, :] = gather_modes(recv, 0, k, 0, 32)
         modes[k, 32:40, :] = gather_modes(recv, 1, k, 24, 8)
-    flat = dot_stacked(stacked(modes[...].reshape(PLANES * 40, DEPTH)), back_z)
+    flat = dot(widened(modes[...].reshape(PLANES * 40, DEPTH)), back_z)
     modes[...] = flat.reshape(PLANES, 40, DEPTH)
-    for x, value in enumerate(mixed([modes[k] for k in range(PLANES)], mode_x.T)):
+    for x, value in enumerate(from_modes([modes[k] for k in range(PLANES)])):
         for m in range(3):
             first = m * REACH
             field[x, first : first + RIM, :] = value[24 + 2 * m : 26 + 2 * m]
@@ -881,18 +924,24 @@
         field[x, 37:48, :] = jnp.zeros((11, DEPTH), jnp.float32)
     for k in range(PLANES):
         grad[k] = gather_modes(recv, 1, k, 0, 24)
-    flat = dot_stacked(stacked(grad[...].reshape(PLANES * 24, DEPTH)), back_z)
+    flat = dot(widened(grad[...].reshape(PLANES * 24, DEPTH)), back_z)
     flat = flat.reshape(PLANES, 24, DEPTH)
-    for x, value in enumerate(mixed([flat[k] for k in range(PLANES)], mode_x.T)):
+    for x, value in enumerate(from_modes([flat[k] for k in range(PLANES)])):
         grad[x] = value
     network(field, fwd1, fwd2, hidden, weights, u_taps, h_hi, h_lo, work)
+
+    def middle():
+        sums[0:144, :] = kernel_sums(l_taps, h_hi, h_lo, 1)
+
+    def late():
+        sums[144:, :] = kernel_sums(u_taps, p_hi, p_lo, -1)
+
     pullback(
-        field, grad, hidden, weights, back2, back1, l_taps, p_hi, p_lo, work, slope
-    )
-    kernel_sums(u_taps, h_hi, h_lo, l_taps, p_hi, p_lo, sums)
-    for k, value in enumerate(mixed([slope[x, 0:40, :] for x in range(PLANES)], mode_x)):
+        field, grad, hidden, weights, back2, back1, l_taps, p_hi, p_lo, work, slope, middle, late
+    )
+    for k, value in enumerate(to_modes([slope[x, 0:40, :] for x in range(PLANES)])):
         modes[k] = value
-    flat = dot_stacked(stacked(modes[...].reshape(PLANES * 40, DEPTH)), (to_z[0], to_z[1]))
+    flat = dot(widened(modes[...].reshape(PLANES * 40, DEPTH)), to_z[...])
     modes[...] = flat.reshape(PLANES, 40, DEPTH)
     for h in range(2):
         for k in range(PLANES):
@@ -906,12 +955,12 @@
 
 
 def third_kernel_body(
-    mode_x, recv, field, hidden, weights, u_taps, h_hi, h_lo, back2, back1, from_z, old_sums,
+    recv, field, hidden, weights, u_taps, h_hi, h_lo, back2, back1, from_z, old_sums,
     spread_t, mask, lift,
     out,
     flat, grad, modes, l_taps, p_hi, p_lo, work, slope, sums, pieces,
 ):
-    back_z = (from_z[0], from_z[1])
+    back_z = from_z[...]
     flat[...] = jnp.zeros_like(flat)
     for device in range(16):
         for m in range(3):
@@ -919,17 +968,24 @@
     for h in range(2):
         for k in range(PLANES):
             modes[k] = gather_modes(flat, h, k, 0, 16)
-        moved_back = dot_stacked(stacked(modes[...].reshape(PLANES * 16, DEPTH)), back_z)
+        moved_back = dot(widened(modes[...].reshape(PLANES * 16, DEPTH)), back_z)
         modes[...] = moved_back.reshape(PLANES, 16, DEPTH)
-        for x, value in enumerate(mixed([modes[k] for k in range(PLANES)], mode_x.T)):
+        for x, value in enumerate(from_modes([modes[k] for k in range(PLANES)])):
             for m in range(3):
                 grad[x, m * SLAB + 4 * h : m * SLAB + 4 * h + 4, :] = value[m * 4 : m * 4 + 4, :]
-    pullback(field, grad, hidden, weights, back2, back1, l_taps, p_hi, p_lo, work, slope)
-    kernel_sums(u_taps, h_hi, h_lo, l_taps, p_hi, p_lo, sums)
-    sums[...] += old_sums[...]
+
+    def middle():
+        sums[0:144, :] = old_sums[0:144, :] + kernel_sums(l_taps, h_hi, h_lo, 1)
+        sums[144:, :] = old_sums[144:, :] + kernel_sums(u_taps, p_hi, p_lo, -1)
+
+    def late():
+        pack_grads(sums, spread_t, mask, lift, pieces)
+
+    pullback(
+        field, grad, hidden, weights, back2, back1, l_taps, p_hi, p_lo, work, slope, middle, late
+    )
     for x in range(PLANES):
         out[x, 0:36, :] = slope[x, 0:36, :]
-    pack_grads(sums, spread_t, mask, lift, pieces)
     for x in range(PLANES):
         out[x, 36:72, :] = pieces[0:36, :]
 
@@ -995,7 +1051,6 @@
 
 def slab_device(velocity, cotangent, first_kernel, first_bias, second_kernel, second_bias):
     c = constants()
-    mode_x = c["mode_x"]
     half = jnp.bfloat16
     f32 = lambda *dims: pltpu.VMEM(dims, jnp.float32)
     b16 = lambda *dims: pltpu.VMEM(dims, half)
@@ -1015,7 +1070,7 @@
             shape(2 * HID, STACK, kind=half),
             shape(2 * HID, STACK, kind=half),
             shape(288, DEEP, kind=half),
-            shape(2, DEPTH, DEPTH, kind=half),
+            shape(3 * DEPTH, DEPTH, kind=half),
         ],
         (
             jnp.transpose(first_kernel, (1, 2, 3, 4, 0)).reshape(27, 3, CHANNELS),
@@ -1036,16 +1091,16 @@
     )
 
     near = lambda rows: [b16(rows, FLAT), b16(rows, FLAT)]
-    stacks = near(2 * STACK)[:1] + near(DEEP) + near(2 * STACK)[:1] + near(DEEP)
+    stacks = near(288)[:1] + near(BROAD) + near(288)[:1] + near(BROAD)
     sent, hidden, weights, *kept = call(
-        functools.partial(first_kernel_body, mode_x),
+        first_kernel_body,
         [
             shape(16, 24, DEPTH),
             shape(HID, FLAT),
             shape(LOG, FLAT),
-            shape(2 * STACK, FLAT, kind=half),
-            shape(DEEP, FLAT, kind=half),
-            shape(DEEP, FLAT, kind=half),
+            shape(288, FLAT, kind=half),
+            shape(BROAD, FLAT, kind=half),
+            shape(BROAD, FLAT, kind=half),
         ],
         (recv, fwd1, fwd2, to_z),
         [f32(144, FLAT), f32(2, PLANES, 24, DEPTH)],
@@ -1056,7 +1111,7 @@
     moved_modes = lax.all_to_all(moved_modes, both, 0, 0)
 
     sent, sums = call(
-        functools.partial(second_kernel_body, mode_x),
+        second_kernel_body,
         [shape(16, 9, 2, DEPTH), shape(288, DEEP)],
         (moved_modes, fwd1, fwd2, back2, back1, to_z, c["from_z"]),
         [
@@ -1081,7 +1136,7 @@
     moved_modes = lax.all_to_all(moved_modes, both, 0, 0)
 
     sent = call(
-        functools.partial(third_kernel_body, mode_x),
+        third_kernel_body,
         shape(PLANES, 72, DEPTH),
         (
             moved_modes, recv, hidden, weights, *kept, back2, back1, c["from_z"], sums,

time: 95.8 us -> 93.9 us (0.980)
  local copies, waits for them, and re-layouts: 5.68 us -> 2.47 us
  waiting for transfers between devices: 2.76 us -> 5.95 us
  Pallas kernels: 18.8 us -> 17.5 us
    unnamed x30, local copies, waits for them, and re-layouts: 5.68 us -> 2.47 us
    all_to_all x1, waiting for transfers between devices: 1.57 us -> 4.76 us  [slab_device(): recv = lax.all_to_all(packed, 'px', 0, 0)]
    pallas_call x10, Pallas kernels: 18.8 us -> 17.5 us  [call(): pl.pallas_call(kernel, out_shape=outs, in_specs=[pl.BlockSpec(memory_spac...]
where the time goes in v5:
time: 93.9 us; the launch traced here: 93.3 us
  blocking collectives  59.1 us (63%)
  Pallas kernels  17.5 us (19%)
  starting transfers between devices  7.53 us (8%)
  waiting for transfers between devices  5.95 us (6%)
  local copies, waits for them, and re-layouts  2.47 us (3%)
    all_to_all x2, blocking collectives, slab_device(): moved_modes = lax.all_to_all(sent, both, 0, 0)  23.7 us
    all_to_all x2, blocking collectives, slab_device(): moved_modes = lax.all_to_all(moved_modes, both, 0, 0)  22.8 us
    pallas_call x10, Pallas kernels, call(): pl.pallas_call(kernel, out_shape=outs, in_specs=[pl.BlockSpec(memory_spac...  17.5 us
    all_to_all x1, blocking collectives, slab_device(): recv = lax.all_to_all(sent, 'px', 0, 0)  12.6 us
    all_to_all x1, starting transfers between devices, slab_device(): recv = lax.all_to_all(packed, 'px', 0, 0)  6.95 us
    all_to_all x1, waiting for transfers between devices, slab_device(): recv = lax.all_to_all(packed, 'px', 0, 0)  4.76 us
    unnamed x30, local copies, waits for them, and re-layouts  2.47 us
  transfers between devices with their start and end apart: 3, of which 2 were waited for; matrix products, arithmetic and copies ran while one was open for 0% of the time, Pallas kernels for 4%

profile of v5, /device:TPU:0, one launch (start us, length us, event | category | flops | bytes accessed | tf_op | source)
XLA Modules:
  0.0 93.3 jit_solution(9898610496135148704)
XLA Ops:
  0.6 0.5 collective-permute-start
  1.2 0.9 copy-done.6
  2.0 0.9 copy-done.7
  3.0 0.7 shard_map.183
  3.7 6.9 %all-to-all-start = ((f32[8,64,128]{2,1,0:T(8,128)}), f32[8,64,128]{2,1,0:T(8,128)S(1)}, u32[]{:S(2)}, u32[]{:S(2)}) async-start(f32[8,64,128]{2,1,0:T(8,128)} %shard_map.183), calls=%async_computation | async-start | bytes 524288 | tf_op jit(solution)/shard_map/all_to_all | solution.py:1064
  10.7 0.6 copy-done.13
  11.3 0.0 copy-done.14
  11.3 4.1 %shard_map.184 = (bf16[288,496]{1,0:T(8,128)(2,1)S(1)}, bf16[320,432]{1,0:T(8,128)(2,1)S(1)}, bf16[320,432]{1,0:T(8,128)(2,1)S(1)}, bf16[288,496]{1,0:T(8,128)(2,1)S(1)}, bf16[384,128]{1,0:T(8,128)(2,1)S(1)}) custom-call(f32[27,3,16]{2,1,0:T(4,128)S(1)} %bitcast.17, f32[54,3,16]{2,1,0:T(4,128)S(1)} %bitcast.16, f32[1,16]{1,0:T(1,128)S(1)} %bitcast.18, ...), custom_call_target="tpu_custom_call" | custom-call | flops 1 | bytes 1 | tf_op jit(solution)/shard_map/pallas_call | solution.py:444
  15.5 4.8 %all-to-all-done.recv.field = f32[8,64,128]{2,1,0:T(8,128)S(1)} async-done(((f32[8,64,128]{2,1,0:T(8,128)}), f32[8,64,128]{2,1,0:T(8,128)S(1)}, u32[]{:S(2)}, u32[]{:S(2)}) %all-to-all-start) | async-done | bytes 262176 | tf_op jit(solution)/shard_map/all_to_all | solution.py:1064
  20.2 2.0 %shard_map.185 = (f32[16,24,128]{2,1,0:T(8,128)S(1)}, f32[160,1024]{1,0:T(8,128)S(1)}, f32[48,1024]{1,0:T(8,128)S(1)}, bf16[288,1024]{1,0:T(8,128)(2,1)S(1)}, bf...) custom-call(f32[8,64,128]{2,1,0:T(8,128)S(1)} %all-to-all-done.recv.field, ...), custom_call_target="tpu_custom_call" | custom-call | tf_op jit(solution)/shard_map/pallas_call | solution.py:444
  22.2 0.0 copy-start.4
  22.2 12.6 %all_to_all.30.recv = f32[16,24,128]{2,1,0:T(8,128)S(1)} all-to-all(f32[16,24,128]{2,1,0:T(8,128)S(1)} %get-tuple-element.28), channel_id=1, replica_groups=mesh['groups'=2,'px'=8,'py'=2] {'px','py'}, dimensions={0} | all-to-all | bytes 393216 | tf_op jit(solution)/shard_map/all_to_all | solution.py:1109
  34.9 0.7 shard_map.186
  35.6 12.8 %all_to_all.31.recv = f32[16,32,128]{2,1,0:T(8,128)S(1)} all-to-all(f32[16,32,128]{2,1,0:T(8,128)S(1)} %shard_map.186), channel_id=1, replica_groups=mesh['groups'=2,'px'=8,'py'=2] {'px','py'}, dimensions={0} | all-to-all | bytes 524288 | tf_op jit(solution)/shard_map/all_to_all | solution.py:1111
  48.4 4.6 %shard_map.187 = (f32[16,9,2,128]{3,2,1,0:T(2,128)S(1)}, f32[288,496]{1,0:T(8,128)S(1)}) custom-call(f32[16,32,128]{2,1,0:T(8,128)S(1)} %all_to_all.31.recv, bf16[320,432]{1,0:T(8,128)(2,1)S(1)} %get-tuple-element.25.fwd1, bf16[288,496]{1,0:T(8,128)(2,1)S(1)} %get-tuple-element.26.fwd2, bf16[320,432]{1,0:T(8,128)(2,1)S(1)} %get-tuple-element.29.back2, ...), custom_call_target="tpu_custom_call" | custom-call | tf_op jit(solution)/shard_map/pallas_call | solution.py:444
  53.0 11.1 %all_to_all.32.recv = f32[16,9,2,128]{3,2,1,0:T(2,128)S(1)} all-to-all(f32[16,9,2,128]{3,2,1,0:T(2,128)S(1)} %get-tuple-element.31), channel_id=1, replica_groups=mesh['groups'=2,'px'=8,'py'=2] {'px','py'}, dimensions={0} | all-to-all | bytes 294912 | tf_op jit(solution)/shard_map/all_to_all | solution.py:1129
  64.1 0.8 shard_map.188
  65.0 10.0 %all_to_all.33.recv = f32[16,3,4,128]{3,2,1,0:T(4,128)S(1)} all-to-all(f32[16,3,4,128]{3,2,1,0:T(4,128)S(1)} %shard_map.188), channel_id=1, replica_groups=mesh['groups'=2,'px'=8,'py'=2] {'px','py'}, dimensions={0} | all-to-all | bytes 196608 | tf_op jit(solution)/shard_map/all_to_all | solution.py:1136
  75.0 3.5 %shard_map.189 = f32[8,72,128]{2,1,0:T(8,128)S(1)} custom-call(f32[16,3,4,128]{3,2,1,0:T(4,128)S(1)} %all_to_all.33.recv, f32[8,64,128]{2,1,0:T(8,128)S(1)} %all-to-all-done.recv.field, f32[160,1024]{1,0:T(8,128)S(1)} %get-tuple-element.32.hidden, f32[48,1024]{1,0:T(8,128)S(1)} %get-tuple-element.33.weights, bf16[288,1024]{1,0:T(8,128)(2,1)S(1)} %get-tuple-element.34.u_taps, ...), custom_call_target="tpu_custom_call" | custom-call | tf_op jit(solution)/shard_map/pallas_call | solution.py:444
  78.5 12.6 %all_to_all.34.recv = f32[8,72,128]{2,1,0:T(8,128)S(1)} all-to-all(f32[8,72,128]{2,1,0:T(8,128)S(1)} %shard_map.189), channel_id=1, replica_groups=mesh['groups'=2,'px'=8,'py'=2] {'px'}, dimensions={0} | all-to-all | bytes 589824 | tf_op jit(solution)/shard_map/all_to_all | solution.py:1154
  91.1 0.1 shard_map.190
  91.2 0.1 collective-permute-start.1
  91.3 1.2 %collective-permute-done.1.other = f32[64,128]{1,0:T(8,128)S(1)} collective-permute-done((f32[64,128]{1,0:T(8,128)S(1)}, f32[64,128]{1,0:T(8,128)S(1)}, u32[]{:S(2)}, u32[]{:S(2)}) %collective-permute-start.1) | collective-permute-done | bytes 32800 | tf_op jit(solution)/shard_map/ppermute | solution.py:1158
  92.5 0.9 shard_map.191
  (27 shorter events, 0.1 us)
Async XLA Ops:
  0.6 2.3 %collective-permute-start = (f32[3,1,64,128]{3,2,1,0:T(8,128)}, f32[3,1,64,128]{3,2,1,0:T(8,128)S(1)}, u32[]{:S(2)}, u32[]{:S(2)}) collective-permute-start(f32[3,1,64,128]{3,2,1,0:T(8,128)} %field.1), channel_id=1, source_target_pairs={{0,1},{1,0},{2,3},{3,2},{4,5},{5,4},{6,7},{7,6},{8,9},{9,8},{10,11... | collective-permute-start | bytes 294920 | tf_op jit(solution)/shard_map/ppermute | solution.py:1059
  1.1 0.9 copy-start.6
  2.0 0.9 copy-start.7
  3.7 7.0 %copy-start.5 = (f32[6,16,3,3,3]{1,4,3,2,0:T(4,128)S(1)}, f32[6,16,3,3,3]{1,4,3,2,0:T(4,128)}, u32[]{:S(2)}) copy-start(f32[6,16,3,3,3]{1,4,3,2,0:T(4,128)} %param.19) | copy-start | bytes 31108
  3.7 7.0 %copy-start.8 = (bf16[384,128]{1,0:T(8,128)(2,1)S(1)}, bf16[384,128]{1,0:T(8,128)(2,1)}, u32[]{:S(2)}) copy-start(bf16[384,128]{1,0:T(8,128)(2,1)} %constant.18.clone.z_in) | copy-start | bytes 294916
  3.7 7.0 %copy-start.11 = (f32[16,3,3,3,3]{0,4,3,2,1:T(4,128)S(1)}, f32[16,3,3,3,3]{0,4,3,2,1:T(4,128)}, u32[]{:S(2)}) copy-start(f32[16,3,3,3,3]{0,4,3,2,1:T(4,128)} %param.17) | copy-start | bytes 15556
  3.7 16.5 %all-to-all-start = ((f32[8,64,128]{2,1,0:T(8,128)}), f32[8,64,128]{2,1,0:T(8,128)S(1)}, u32[]{:S(2)}, u32[]{:S(2)}) async-start(f32[8,64,128]{2,1,0:T(8,128)} %shard_map.183), calls=%async_computation | async-start | bytes 524288 | tf_op jit(solution)/shard_map/all_to_all | solution.py:1064
  10.7 0.7 copy-start.13
  10.7 0.7 copy-start.14
  22.2 12.6 %copy-start.4 = (bf16[192,384]{1,0:T(8,128)(2,1)S(1)}, bf16[192,384]{1,0:T(8,128)(2,1)}, u32[]{:S(2)}) copy-start(bf16[192,384]{1,0:T(8,128)(2,1)} %constant.20.clone.table_out) | copy-start | bytes 442372
  22.2 12.6 %copy-start.10 = (bf16[128,384]{1,0:T(8,128)(2,1)S(1)}, bf16[128,384]{1,0:T(8,128)(2,1)}, u32[]{:S(2)}) copy-start(bf16[128,384]{1,0:T(8,128)(2,1)} %constant.19.clone.table_in) | copy-start | bytes 294916
  35.6 12.8 %copy-start.2 = (bf16[384,128]{1,0:T(8,128)(2,1)S(1)}, bf16[384,128]{1,0:T(8,128)(2,1)}, u32[]{:S(2)}) copy-start(bf16[384,128]{1,0:T(8,128)(2,1)} %constant.21.clone.from_z) | copy-start | bytes 294916
  48.4 15.8 %copy-start.3 = (bf16[256,288]{1,0:T(8,128)(2,1)S(1)}, bf16[256,288]{1,0:T(8,128)(2,1)}, u32[]{:S(2)}) copy-start(bf16[256,288]{1,0:T(8,128)(2,1)} %constant.22.clone.table_in) | copy-start | bytes 442372
  48.4 15.8 %copy-start.9 = (bf16[128,384]{1,0:T(8,128)(2,1)S(1)}, bf16[128,384]{1,0:T(8,128)(2,1)}, u32[]{:S(2)}) copy-start(bf16[128,384]{1,0:T(8,128)(2,1)} %constant.23.clone.table_out) | copy-start | bytes 294916
  48.4 26.6 %copy-start.1 = (bf16[1536,256]{1,0:T(8,128)(2,1)S(1)}, bf16[1536,256]{1,0:T(8,128)(2,1)}, u32[]{:S(2)}) copy-start(bf16[1536,256]{1,0:T(8,128)(2,1)} %constant.26.clone.lift) | copy-start | bytes 2359300
  53.0 22.0 %copy-start = (bf16[3,288,496]{2,1,0:T(8,128)(2,1)S(1)}, bf16[3,288,496]{2,1,0:T(8,128)(2,1)}, u32[]{:S(2)}) copy-start(bf16[3,288,496]{2,1,0:T(8,128)(2,1)} %constant.25.clone.mask) | copy-start | bytes 2571268
  65.0 10.0 %copy-start.12 = (bf16[32,288]{1,0:T(8,128)(2,1)S(1)}, bf16[32,288]{1,0:T(8,128)(2,1)}, u32[]{:S(2)}) copy-start(bf16[32,288]{1,0:T(8,128)(2,1)} %constant.24.clone.spread_t) | copy-start | bytes 55300
  91.2 1.3 %collective-permute-start.1 = (f32[64,128]{1,0:T(8,128)S(1)}, f32[64,128]{1,0:T(8,128)S(1)}, u32[]{:S(2)}, u32[]{:S(2)}) collective-permute-start(f32[64,128]{1,0:T(8,128)S(1)} %get-tuple-element.39.edge), channel_id=1, source_target_pairs={{0,1},{1,0},{2,3},{3,2},{4,5},{5,4},{6,7},{7,6},{8,9},{9,8},{10,11... | collective-permute-start | bytes 98312 | tf_op jit(solution)/shard_map/ppermute | solution.py:1158

commit v6 on v5

--- a/solution.py
+++ b/solution.py
@@ -393,7 +393,7 @@
         both_out=wide_table(both_out),
         one_in=wide_table(one_in),
         one_out=wide_table(one_out),
-        spread_t=np.ascontiguousarray(spread.T).astype(half),
+        spread_t=np.concatenate([spread.T, spread.T], axis=1).astype(half),
         mask=mask.astype(half),
         lift=lift.astype(half),
     )
@@ -549,14 +549,14 @@
         fwd2[start : start + LOG, 3 * HID :] = value.astype(jnp.bfloat16)
 
 
-def pack_kernel(field, cot, out, ext):
+def pack_kernel(fields, out, ext):
     ext[...] = jnp.zeros_like(ext)
     for m in range(3):
-        ext[m, 8:72, :] = field[m, 0]
+        ext[m, 8:72, :] = fields[m, 0]
     for q in range(PLANES):
         for m in range(3):
             out[q, m * REACH : (m + 1) * REACH, :] = ext[m, 8 * q + 6 : 8 * q + 18, :]
-            out[q, 40 + 8 * m : 48 + 8 * m, :] = cot[m, 0, 8 * q : 8 * q + 8, :]
+            out[q, 40 + 8 * m : 48 + 8 * m, :] = fields[3 + m, 0, 8 * q : 8 * q + 8, :]
         out[q, 36:37, :] = jnp.ones((1, DEPTH), jnp.float32)
         out[q, 37:40, :] = jnp.zeros((3, DEPTH), jnp.float32)
 
@@ -995,7 +995,8 @@
     empty = jnp.zeros((32, 512 - DEEP), jnp.float32)
     rows = []
     for b in range(3):
-        rows.append(dot(spread_t[...], whole[0] * mask[b]) + dot(spread_t[...], whole[1] * mask[b]))
+        both = jnp.concatenate([whole[0] * mask[b], whole[1] * mask[b]], axis=0)
+        rows.append(dot(spread_t[...], both))
         rows.append(empty)
     placed = dot(stacked(beside(rows)), lift[...])
     placed = placed[:32] + placed[32:]
@@ -1057,8 +1058,9 @@
     swap = [(0, 1), (1, 0)]
 
     other = lax.ppermute(velocity, "py", swap)
+    fields = jnp.concatenate([velocity, cotangent], axis=0)
     packed = call(
-        pack_kernel, shape(PLANES, 64, DEPTH), (velocity, cotangent), [f32(3, 80, DEPTH)], room=4
+        pack_kernel, shape(PLANES, 64, DEPTH), (fields,), [f32(3, 80, DEPTH)], room=4
     )
     packed = call(rim_kernel, shape(PLANES, 64, DEPTH), (packed, other), room=4)
     recv = lax.all_to_all(packed, "px", 0, 0)

time: 93.9 us -> 93.1 us (level)
  local copies, waits for them, and re-layouts: 2.47 us -> 0.69 us
  other arithmetic: 0 us -> 0.95 us
    unnamed x30 -> x26, local copies, waits for them, and re-layouts: 2.47 us -> 0.69 us
    concatenate x0 -> x1, other arithmetic: none -> 0.95 us  [slab_device(): fields = jnp.concatenate([velocity, cotangent], axis=0)]
  transfers between devices with their start and end apart: 3 -> 3, of which waited for: 2 -> 3; matrix products, arithmetic and copies ran while one was open for 0% -> 1% of each run, Pallas kernels for 4% -> 5%
where the time goes in v6:
time: 93.1 us; the launch traced here: 92.5 us
  blocking collectives  59.1 us (63%)
  Pallas kernels  17.4 us (19%)
  starting transfers between devices  7.88 us (8%)
  waiting for transfers between devices  5.76 us (6%)
  other arithmetic  0.95 us (1%)
    all_to_all x2, blocking collectives, slab_device(): moved_modes = lax.all_to_all(sent, both, 0, 0)  23.7 us
    all_to_all x2, blocking collectives, slab_device(): moved_modes = lax.all_to_all(moved_modes, both, 0, 0)  22.8 us
    pallas_call x10, Pallas kernels, call(): pl.pallas_call(kernel, out_shape=outs, in_specs=[pl.BlockSpec(memory_spac...  17.4 us
    all_to_all x1, blocking collectives, slab_device(): recv = lax.all_to_all(sent, 'px', 0, 0)  12.6 us
    all_to_all x1, starting transfers between devices, slab_device(): recv = lax.all_to_all(packed, 'px', 0, 0)  7.29 us
    all_to_all x1, waiting for transfers between devices, slab_device(): recv = lax.all_to_all(packed, 'px', 0, 0)  4.41 us
  transfers between devices with their start and end apart: 3, of which 3 were waited for; matrix products, arithmetic and copies ran while one was open for 1% of the time, Pallas kernels for 5%

profile of v6, /device:TPU:0, one launch (start us, length us, event | category | flops | bytes accessed | tf_op | source)
XLA Modules:
  0.0 92.5 jit_solution(2448019368807764474)
XLA Ops:
  0.6 0.5 collective-permute-start
  1.1 1.0 %pad_maximum_fusion.fields = f32[6,1,64,128]{3,2,1,0:T(8,128)S(1)} fusion(f32[3,1,64,128]{3,2,1,0:T(8,128)} %param.16, f32[3,1,64,128]{3,2,1,0:T(8,128)} %param.15), kind=kLoop, calls=%fused_computation | loop fusion | flops 49152 | bytes 393216 | tf_op jit(solution)/shard_map/concatenate | solution.py:1061
  2.1 0.2 collective-permute-done.other
  2.3 0.7 shard_map.183
  3.0 7.3 %all-to-all-start = ((f32[8,64,128]{2,1,0:T(8,128)}), f32[8,64,128]{2,1,0:T(8,128)S(1)}, u32[]{:S(2)}, u32[]{:S(2)}) async-start(f32[8,64,128]{2,1,0:T(8,128)} %shard_map.183), calls=%async_computation | async-start | bytes 524288 | tf_op jit(solution)/shard_map/all_to_all | solution.py:1066
  10.4 0.6 copy-done.11
  11.0 0.0 copy-done.12
  11.0 4.1 %shard_map.184 = (bf16[288,496]{1,0:T(8,128)(2,1)S(1)}, bf16[320,432]{1,0:T(8,128)(2,1)S(1)}, bf16[320,432]{1,0:T(8,128)(2,1)S(1)}, bf16[288,496]{1,0:T(8,128)(2,1)S(1)}, bf16[384,128]{1,0:T(8,128)(2,1)S(1)}) custom-call(f32[27,3,16]{2,1,0:T(4,128)S(1)} %bitcast.17, f32[54,3,16]{2,1,0:T(4,128)S(1)} %bitcast.16, f32[1,16]{1,0:T(1,128)S(1)} %bitcast.18, ...), custom_call_target="tpu_custom_call" | custom-call | flops 1 | bytes 1 | tf_op jit(solution)/shard_map/pallas_call | solution.py:444
  15.1 4.4 %all-to-all-done.recv.field = f32[8,64,128]{2,1,0:T(8,128)S(1)} async-done(((f32[8,64,128]{2,1,0:T(8,128)}), f32[8,64,128]{2,1,0:T(8,128)S(1)}, u32[]{:S(2)}, u32[]{:S(2)}) %all-to-all-start) | async-done | bytes 262176 | tf_op jit(solution)/shard_map/all_to_all | solution.py:1066
  19.6 2.0 %shard_map.185 = (f32[16,24,128]{2,1,0:T(8,128)S(1)}, f32[160,1024]{1,0:T(8,128)S(1)}, f32[48,1024]{1,0:T(8,128)S(1)}, bf16[288,1024]{1,0:T(8,128)(2,1)S(1)}, bf...) custom-call(f32[8,64,128]{2,1,0:T(8,128)S(1)} %all-to-all-done.recv.field, ...), custom_call_target="tpu_custom_call" | custom-call | tf_op jit(solution)/shard_map/pallas_call | solution.py:444
  21.5 0.0 copy-start.4
  21.5 12.6 %all_to_all.30.recv = f32[16,24,128]{2,1,0:T(8,128)S(1)} all-to-all(f32[16,24,128]{2,1,0:T(8,128)S(1)} %get-tuple-element.28), channel_id=1, replica_groups=mesh['groups'=2,'px'=8,'py'=2] {'px','py'}, dimensions={0} | all-to-all | bytes 393216 | tf_op jit(solution)/shard_map/all_to_all | solution.py:1111
  34.2 0.7 shard_map.186
  34.9 12.8 %all_to_all.31.recv = f32[16,32,128]{2,1,0:T(8,128)S(1)} all-to-all(f32[16,32,128]{2,1,0:T(8,128)S(1)} %shard_map.186), channel_id=1, replica_groups=mesh['groups'=2,'px'=8,'py'=2] {'px','py'}, dimensions={0} | all-to-all | bytes 524288 | tf_op jit(solution)/shard_map/all_to_all | solution.py:1113
  47.7 4.6 %shard_map.187 = (f32[16,9,2,128]{3,2,1,0:T(2,128)S(1)}, f32[288,496]{1,0:T(8,128)S(1)}) custom-call(f32[16,32,128]{2,1,0:T(8,128)S(1)} %all_to_all.31.recv, bf16[320,432]{1,0:T(8,128)(2,1)S(1)} %get-tuple-element.25.fwd1, bf16[288,496]{1,0:T(8,128)(2,1)S(1)} %get-tuple-element.26.fwd2, bf16[320,432]{1,0:T(8,128)(2,1)S(1)} %get-tuple-element.29.back2, ...), custom_call_target="tpu_custom_call" | custom-call | tf_op jit(solution)/shard_map/pallas_call | solution.py:444
  52.3 11.1 %all_to_all.32.recv = f32[16,9,2,128]{3,2,1,0:T(2,128)S(1)} all-to-all(f32[16,9,2,128]{3,2,1,0:T(2,128)S(1)} %get-tuple-element.31), channel_id=1, replica_groups=mesh['groups'=2,'px'=8,'py'=2] {'px','py'}, dimensions={0} | all-to-all | bytes 294912 | tf_op jit(solution)/shard_map/all_to_all | solution.py:1131
  63.4 0.8 shard_map.188
  64.3 10.0 %all_to_all.33.recv = f32[16,3,4,128]{3,2,1,0:T(4,128)S(1)} all-to-all(f32[16,3,4,128]{3,2,1,0:T(4,128)S(1)} %shard_map.188), channel_id=1, replica_groups=mesh['groups'=2,'px'=8,'py'=2] {'px','py'}, dimensions={0} | all-to-all | bytes 196608 | tf_op jit(solution)/shard_map/all_to_all | solution.py:1138
  74.3 3.5 %shard_map.189 = f32[8,72,128]{2,1,0:T(8,128)S(1)} custom-call(f32[16,3,4,128]{3,2,1,0:T(4,128)S(1)} %all_to_all.33.recv, f32[8,64,128]{2,1,0:T(8,128)S(1)} %all-to-all-done.recv.field, f32[160,1024]{1,0:T(8,128)S(1)} %get-tuple-element.32.hidden, f32[48,1024]{1,0:T(8,128)S(1)} %get-tuple-element.33.weights, bf16[288,1024]{1,0:T(8,128)(2,1)S(1)} %get-tuple-element.34.u_taps, ...), custom_call_target="tpu_custom_call" | custom-call | tf_op jit(solution)/shard_map/pallas_call | solution.py:444
  77.8 12.6 %all_to_all.34.recv = f32[8,72,128]{2,1,0:T(8,128)S(1)} all-to-all(f32[8,72,128]{2,1,0:T(8,128)S(1)} %shard_map.189), channel_id=1, replica_groups=mesh['groups'=2,'px'=8,'py'=2] {'px'}, dimensions={0} | all-to-all | bytes 589824 | tf_op jit(solution)/shard_map/all_to_all | solution.py:1156
  90.4 0.1 shard_map.190
  90.4 0.1 collective-permute-start.1
  90.5 1.2 %collective-permute-done.1.other = f32[64,128]{1,0:T(8,128)S(1)} collective-permute-done((f32[64,128]{1,0:T(8,128)S(1)}, f32[64,128]{1,0:T(8,128)S(1)}, u32[]{:S(2)}, u32[]{:S(2)}) %collective-permute-start.1) | collective-permute-done | bytes 32800 | tf_op jit(solution)/shard_map/ppermute | solution.py:1160
  91.7 0.9 shard_map.191
  (24 shorter events, 0.1 us)
Async XLA Ops:
  0.6 1.7 %collective-permute-start = (f32[3,1,64,128]{3,2,1,0:T(8,128)}, f32[3,1,64,128]{3,2,1,0:T(8,128)S(1)}, u32[]{:S(2)}, u32[]{:S(2)}) collective-permute-start(f32[3,1,64,128]{3,2,1,0:T(8,128)} %param.15), channel_id=1, source_target_pairs={{0,1},{1,0},{2,3},{3,2},{4,5},{5,4},{6,7},{7,6},{8,9},{9,8},{10,11... | collective-permute-start | bytes 294920 | tf_op jit(solution)/shard_map/ppermute | solution.py:1060
  3.0 7.3 %copy-start.5 = (f32[6,16,3,3,3]{1,4,3,2,0:T(4,128)S(1)}, f32[6,16,3,3,3]{1,4,3,2,0:T(4,128)}, u32[]{:S(2)}) copy-start(f32[6,16,3,3,3]{1,4,3,2,0:T(4,128)} %param.19) | copy-start | bytes 31108
  3.0 7.3 %copy-start.6 = (bf16[384,128]{1,0:T(8,128)(2,1)S(1)}, bf16[384,128]{1,0:T(8,128)(2,1)}, u32[]{:S(2)}) copy-start(bf16[384,128]{1,0:T(8,128)(2,1)} %constant.18.clone.z_in) | copy-start | bytes 294916
  3.0 7.3 %copy-start.9 = (f32[16,3,3,3,3]{0,4,3,2,1:T(4,128)S(1)}, f32[16,3,3,3,3]{0,4,3,2,1:T(4,128)}, u32[]{:S(2)}) copy-start(f32[16,3,3,3,3]{0,4,3,2,1:T(4,128)} %param.17) | copy-start | bytes 15556
  3.0 16.5 %all-to-all-start = ((f32[8,64,128]{2,1,0:T(8,128)}), f32[8,64,128]{2,1,0:T(8,128)S(1)}, u32[]{:S(2)}, u32[]{:S(2)}) async-start(f32[8,64,128]{2,1,0:T(8,128)} %shard_map.183), calls=%async_computation | async-start | bytes 524288 | tf_op jit(solution)/shard_map/all_to_all | solution.py:1066
  10.3 0.7 copy-start.11
  10.3 0.7 copy-start.12
  21.5 12.6 %copy-start.4 = (bf16[192,384]{1,0:T(8,128)(2,1)S(1)}, bf16[192,384]{1,0:T(8,128)(2,1)}, u32[]{:S(2)}) copy-start(bf16[192,384]{1,0:T(8,128)(2,1)} %constant.20.clone.table_out) | copy-start | bytes 442372
  21.5 12.6 %copy-start.8 = (bf16[128,384]{1,0:T(8,128)(2,1)S(1)}, bf16[128,384]{1,0:T(8,128)(2,1)}, u32[]{:S(2)}) copy-start(bf16[128,384]{1,0:T(8,128)(2,1)} %constant.19.clone.table_in) | copy-start | bytes 294916
  34.9 12.8 %copy-start.2 = (bf16[384,128]{1,0:T(8,128)(2,1)S(1)}, bf16[384,128]{1,0:T(8,128)(2,1)}, u32[]{:S(2)}) copy-start(bf16[384,128]{1,0:T(8,128)(2,1)} %constant.21.clone.from_z) | copy-start | bytes 294916
  47.7 15.8 %copy-start.3 = (bf16[256,288]{1,0:T(8,128)(2,1)S(1)}, bf16[256,288]{1,0:T(8,128)(2,1)}, u32[]{:S(2)}) copy-start(bf16[256,288]{1,0:T(8,128)(2,1)} %constant.22.clone.table_in) | copy-start | bytes 442372
  47.7 15.8 %copy-start.7 = (bf16[128,384]{1,0:T(8,128)(2,1)S(1)}, bf16[128,384]{1,0:T(8,128)(2,1)}, u32[]{:S(2)}) copy-start(bf16[128,384]{1,0:T(8,128)(2,1)} %constant.23.clone.table_out) | copy-start | bytes 294916
  47.7 26.6 %copy-start.1 = (bf16[1536,256]{1,0:T(8,128)(2,1)S(1)}, bf16[1536,256]{1,0:T(8,128)(2,1)}, u32[]{:S(2)}) copy-start(bf16[1536,256]{1,0:T(8,128)(2,1)} %constant.26.clone.lift) | copy-start | bytes 2359300
  52.3 22.0 %copy-start = (bf16[3,288,496]{2,1,0:T(8,128)(2,1)S(1)}, bf16[3,288,496]{2,1,0:T(8,128)(2,1)}, u32[]{:S(2)}) copy-start(bf16[3,288,496]{2,1,0:T(8,128)(2,1)} %constant.25.clone.mask) | copy-start | bytes 2571268
  64.3 10.0 %copy-start.10 = (bf16[32,576]{1,0:T(8,128)(2,1)S(1)}, bf16[32,576]{1,0:T(8,128)(2,1)}, u32[]{:S(2)}) copy-start(bf16[32,576]{1,0:T(8,128)(2,1)} %constant.24.clone.spread_t) | copy-start | bytes 110596
  90.4 1.3 %collective-permute-start.1 = (f32[64,128]{1,0:T(8,128)S(1)}, f32[64,128]{1,0:T(8,128)S(1)}, u32[]{:S(2)}, u32[]{:S(2)}) collective-permute-start(f32[64,128]{1,0:T(8,128)S(1)} %get-tuple-element.39.edge), channel_id=1, source_target_pairs={{0,1},{1,0},{2,3},{3,2},{4,5},{5,4},{6,7},{7,6},{8,9},{9,8},{10,11... | collective-permute-start | bytes 98312 | tf_op jit(solution)/shard_map/ppermute | solution.py:1160

commit v7 on v6

--- a/solution.py
+++ b/solution.py
@@ -383,7 +383,7 @@
     for b in range(3):
         for a in range(3):
             lift[b, PLACE[a] * HID + np.arange(HID), 16 * (3 * b + a) + np.arange(HID) // WIDE] = 1.0
-    lift[0, 3 * HID, 128 + 64] = 1.0
+    lift[0, 3 * HID, 128 + 96] = 1.0
     lift = lift.reshape(3 * 512, 256)
     half = jnp.bfloat16
     return dict(
@@ -556,16 +556,17 @@
     for q in range(PLANES):
         for m in range(3):
             out[q, m * REACH : (m + 1) * REACH, :] = ext[m, 8 * q + 6 : 8 * q + 18, :]
-            out[q, 40 + 8 * m : 48 + 8 * m, :] = fields[3 + m, 0, 8 * q : 8 * q + 8, :]
-        out[q, 36:37, :] = jnp.ones((1, DEPTH), jnp.float32)
-        out[q, 37:40, :] = jnp.zeros((3, DEPTH), jnp.float32)
+            out[q, 36 + 8 * m : 44 + 8 * m, :] = fields[3 + m, 0, 8 * q : 8 * q + 8, :]
+        out[q, 60:64, :] = jnp.zeros((4, DEPTH), jnp.float32)
 
 
 def rim_kernel(packed, other, out):
-    out[...] = packed[...]
+    for q in range(PLANES):
+        for i in range(15):
+            out[q, i] = packed[q, 4 * i : 4 * i + 4, :]
     for m in range(3):
-        out[0, m * REACH : m * REACH + 2, :] = other[m, 0, 62:64, :]
-        out[PLANES - 1, m * REACH + 10 : m * REACH + 12, :] = other[m, 0, 0:2, :]
+        out[0, 3 * m, 0:2, :] = other[m, 0, 62:64, :]
+        out[PLANES - 1, 3 * m + 2, 2:4, :] = other[m, 0, 0:2, :]
 
 
 def unit_row():
@@ -636,21 +637,27 @@
         weights[:, plane(x)] = jax.nn.sigmoid(total)
 
 
-def around(field, x, direction, sign):
+def own_rows(field):
+    return [
+        [field[x, m * REACH + RIM : m * REACH + RIM + SLAB, :] for m in range(3)] for x in range(PLANES)
+    ]
+
+
+def around(field, own, x, direction, sign):
     if direction == 0:
-        return [field[(x + sign) % PLANES, m * REACH + RIM : m * REACH + RIM + SLAB, :] for m in range(3)]
+        return own[(x + sign) % PLANES]
     if direction == 1:
         first = RIM + sign
         return [field[x, m * REACH + first : m * REACH + first + SLAB, :] for m in range(3)]
-    return [turn(field[x, m * REACH + RIM : m * REACH + RIM + SLAB, :], -sign) for m in range(3)]
-
-
-def advected(field, weights, x):
-    center = around(field, x, 0, 0)
+    return [turn(value, -sign) for value in own[x]]
+
+
+def advected(field, cells, weights, x):
+    center = cells[x]
     total = [jnp.zeros((SLAB, DEPTH), jnp.float32)] * 3
     for d in range(3):
-        ahead = around(field, x, d, 1)
-        behind = around(field, x, d, -1)
+        ahead = around(field, cells, x, d, 1)
+        behind = around(field, cells, x, d, -1)
         plus = 0.5 * (center[d] + ahead[d])
         minus = 0.5 * (behind[d] + center[d])
         rate_up = weights[2 * d * SLAB : (2 * d + 1) * SLAB, plane(x)]
@@ -724,13 +731,21 @@
 
 
 def first_kernel_body(
-    recv, fwd1, fwd2, to_z, out, hidden, weights, u_taps, h_hi, h_lo, work, modes
+    recv, fwd1, fwd2, to_z, out, field, hidden, weights, u_taps, h_hi, h_lo, work, modes, cot
 ):
-    network(recv, fwd1, fwd2, hidden, weights, u_taps, h_hi, h_lo, work)
+    for x in range(PLANES):
+        for i in range(9):
+            field[x, 4 * i : 4 * i + 4, :] = recv[x, i]
+        field[x, 36:37, :] = jnp.ones((1, DEPTH), jnp.float32)
+        field[x, 37:48, :] = jnp.zeros((11, DEPTH), jnp.float32)
+        for i in range(6):
+            cot[x, 4 * i : 4 * i + 4, :] = recv[x, 9 + i]
+    network(field, fwd1, fwd2, hidden, weights, u_taps, h_hi, h_lo, work)
     table = to_z[...]
-    moved_field = [jnp.concatenate(advected(recv, weights, x), axis=0) for x in range(PLANES)]
+    cells = own_rows(field)
+    moved_field = [jnp.concatenate(advected(field, cells, weights, x), axis=0) for x in range(PLANES)]
     for f in range(2):
-        planes = moved_field if f == 0 else [recv[x, 40:64, :] for x in range(PLANES)]
+        planes = moved_field if f == 0 else [cot[x] for x in range(PLANES)]
         for k, value in enumerate(to_modes(planes)):
             modes[f, k] = value
     for f in range(2):
@@ -829,15 +844,16 @@
     slope[...] = jnp.zeros_like(slope)
     row = lax.broadcasted_iota(jnp.int32, (SLAB, DEPTH), 0)
     stay = [None] * PLANES
+    cells = own_rows(field)
     pushed = {}
     for x in range(PLANES):
-        center = around(field, x, 0, 0)
+        center = cells[x]
         source = [-KAPPA * grad[x, m * SLAB : (m + 1) * SLAB, :] for m in range(3)]
         own = [grad[x, m * SLAB : (m + 1) * SLAB, :] for m in range(3)]
         logits = []
         for d in range(3):
-            ahead = around(field, x, d, 1)
-            behind = around(field, x, d, -1)
+            ahead = around(field, cells, x, d, 1)
+            behind = around(field, cells, x, d, -1)
             plus = 0.5 * (center[d] + ahead[d])
             minus = 0.5 * (behind[d] + center[d])
             rate_up = weights[2 * d * SLAB : (2 * d + 1) * SLAB, plane(x)]
@@ -985,9 +1001,11 @@
         field, grad, hidden, weights, back2, back1, l_taps, p_hi, p_lo, work, slope, middle, late
     )
     for x in range(PLANES):
-        out[x, 0:36, :] = slope[x, 0:36, :]
+        for i in range(9):
+            out[x, i] = slope[x, 4 * i : 4 * i + 4, :]
     for x in range(PLANES):
-        out[x, 36:72, :] = pieces[0:36, :]
+        for i in range(8):
+            out[x, 9 + i] = pieces[4 * i : 4 * i + 4, :]
 
 
 def pack_grads(sums, spread_t, mask, lift, pieces):
@@ -1001,10 +1019,13 @@
     placed = dot(stacked(beside(rows)), lift[...])
     placed = placed[:32] + placed[32:]
     pieces[0:28, :] = placed[0:28, 0:128]
-    total = placed[0:8, 128:]
-    for i in range(1, 4):
-        total = total + turn(placed[8 * i : 8 * i + 8, 128:], 16 * i)
-    pieces[28:36, :] = total
+    rest = placed[:, 128:]
+    lane = lax.broadcasted_iota(jnp.int32, rest.shape, 1)
+    low, high = jnp.where(lane < 64, rest, 0.0), jnp.where(lane < 64, 0.0, rest)
+    total = turn(high[4:8], 16) + turn(high[8:12], 17)
+    for i in range(7):
+        total = total + turn(low[4 * i : 4 * i + 4], 16 * i)
+    pieces[28:32, :] = total
 
 
 def fold_kernel(recv, main, edge, ext):
@@ -1012,16 +1033,18 @@
     total = None
     for q in range(PLANES):
         for m in range(3):
-            ext[m, 8 * q + 6 : 8 * q + 18, :] += recv[q, m * REACH : (m + 1) * REACH, :]
-        block = recv[q, 36:72, :]
+            for i in range(3):
+                first = 8 * q + 6 + 4 * i
+                ext[m, first : first + 4, :] += recv[q, 3 * m + i]
+        block = recv[q, 9:17]
         total = block if total is None else total + block
     for m in range(3):
         main[m, 0] = ext[m, 8:72, :]
         edge[m * 8 : m * 8 + 2, :] = ext[m, 72:74, :]
         edge[m * 8 + 2 : m * 8 + 4, :] = ext[m, 6:8, :]
         edge[m * 8 + 4 : m * 8 + 8, :] = jnp.zeros((4, DEPTH), jnp.float32)
-    edge[24:60, :] = total
-    edge[60:64, :] = jnp.zeros((4, DEPTH), jnp.float32)
+    for i in range(8):
+        edge[24 + 4 * i : 28 + 4 * i, :] = total[i]
 
 
 def last_kernel(main, edge, other, out, first, end1, second, end2, turned):
@@ -1029,7 +1052,7 @@
         out[m, 0] = main[m, 0]
         out[m, 0, 0:2, :] += other[m * 8 : m * 8 + 2, :]
         out[m, 0, 62:64, :] += other[m * 8 + 2 : m * 8 + 4, :]
-    grads = edge[24:64, :] + other[24:64, :]
+    grads = edge[24:56, :] + other[24:56, :]
     for slot in range(8):
         turned[slot] = turn(grads, -16 * slot)
     for b in range(3):
@@ -1038,7 +1061,7 @@
                 for i in range(9):
                     row = e * 6 + i if i < 6 else 18 + e * 3 + i - 6
                     slot = 3 * b + a
-                    slot, inner = (slot, row) if slot < 8 else (row // 8, 28 + row % 8)
+                    slot, inner = (slot, row) if slot < 8 else (row // 4, 28 + row % 4)
                     line = turned[slot, inner, 0:16]
                     if i < 6:
                         second[i * 9 + a * 3 + b, e, :] = line
@@ -1046,8 +1069,8 @@
                         first[(i - 6) * 9 + a * 3 + b, e, :] = line
     end1[...] = turned[1, 27:28, 0:16]
     for o in range(COEFFS):
-        slot, inner = (4, 34 + o) if o < 2 else (5, 26 + o)
-        end2[0:1, o : o + 1] = turned[slot, inner : inner + 1, 0:1]
+        inner, place = 28 + (6 + o) % 4, (6 + o) // 4 - 1
+        end2[0:1, o : o + 1] = turned[7, inner : inner + 1, place : place + 1]
 
 
 def slab_device(velocity, cotangent, first_kernel, first_bias, second_kernel, second_bias):
@@ -1062,7 +1085,7 @@
     packed = call(
         pack_kernel, shape(PLANES, 64, DEPTH), (fields,), [f32(3, 80, DEPTH)], room=4
     )
-    packed = call(rim_kernel, shape(PLANES, 64, DEPTH), (packed, other), room=4)
+    packed = call(rim_kernel, shape(PLANES, 15, 4, DEPTH), (packed, other), room=4)
     recv = lax.all_to_all(packed, "px", 0, 0)
 
     fwd2, fwd1, back2, back1, to_z = call(
@@ -1094,10 +1117,11 @@
 
     near = lambda rows: [b16(rows, FLAT), b16(rows, FLAT)]
     stacks = near(288)[:1] + near(BROAD) + near(288)[:1] + near(BROAD)
-    sent, hidden, weights, *kept = call(
+    sent, field, hidden, weights, *kept = call(
         first_kernel_body,
         [
             shape(16, 24, DEPTH),
+            shape(PLANES, 48, DEPTH),
             shape(HID, FLAT),
             shape(LOG, FLAT),
             shape(288, FLAT, kind=half),
@@ -1105,7 +1129,7 @@
             shape(BROAD, FLAT, kind=half),
         ],
         (recv, fwd1, fwd2, to_z),
-        [f32(144, FLAT), f32(2, PLANES, 24, DEPTH)],
+        [f32(144, FLAT), f32(2, PLANES, 24, DEPTH), f32(PLANES, 24, DEPTH)],
     )
     both = ("px", "py")
     moved_modes = lax.all_to_all(sent, both, 0, 0)
@@ -1139,9 +1163,9 @@
 
     sent = call(
         third_kernel_body,
-        shape(PLANES, 72, DEPTH),
+        shape(PLANES, 17, 4, DEPTH),
         (
-            moved_modes, recv, hidden, weights, *kept, back2, back1, c["from_z"], sums,
+            moved_modes, field, hidden, weights, *kept, back2, back1, c["from_z"], sums,
             c["spread_t"], c["mask"], c["lift"],
         ),
         [f32(16, 16, DEPTH), f32(PLANES, 24, DEPTH), f32(PLANES, 16, DEPTH)]
@@ -1150,12 +1174,12 @@
             f32(144, FLAT),
             f32(PLANES, 48, DEPTH),
             f32(288, DEEP),
-            f32(36, DEPTH),
+            f32(32, DEPTH),
         ],
     )
     recv = lax.all_to_all(sent, "px", 0, 0)
     main, edge = call(
-        fold_kernel, [shape(3, 1, 64, DEPTH), shape(64, DEPTH)], (recv,), [f32(3, 80, DEPTH)]
+        fold_kernel, [shape(3, 1, 64, DEPTH), shape(56, DEPTH)], (recv,), [f32(3, 80, DEPTH)]
     )
     other = lax.ppermute(edge, "py", swap)
     grad_velocity, first, end1, second, end2 = call(
@@ -1168,7 +1192,7 @@
             shape(1, COEFFS),
         ],
         (main, edge, other),
-        [f32(8, 40, DEPTH)],
+        [f32(8, 32, DEPTH)],
     )
     return (
         grad_velocity,

time: 93.1 us -> 92.5 us (level)
  no operation moved by 1% of the time
where the time goes in v7:
time: 92.5 us; the launch traced here: 92 us
  blocking collectives  58.7 us (63%)
  Pallas kernels  17.5 us (19%)
  starting transfers between devices  7.88 us (9%)
  waiting for transfers between devices  5.51 us (6%)
  other arithmetic  0.95 us (1%)
    all_to_all x2, blocking collectives, slab_device(): moved_modes = lax.all_to_all(sent, both, 0, 0)  23.6 us
    all_to_all x2, blocking collectives, slab_device(): moved_modes = lax.all_to_all(moved_modes, both, 0, 0)  22.8 us
    pallas_call x10, Pallas kernels, call(): pl.pallas_call(kernel, out_shape=outs, in_specs=[pl.BlockSpec(memory_spac...  17.5 us
    all_to_all x1, blocking collectives, slab_device(): recv = lax.all_to_all(sent, 'px', 0, 0)  12.3 us
    all_to_all x1, starting transfers between devices, slab_device(): recv = lax.all_to_all(packed, 'px', 0, 0)  7.29 us
    all_to_all x1, waiting for transfers between devices, slab_device(): recv = lax.all_to_all(packed, 'px', 0, 0)  4.17 us
  transfers between devices with their start and end apart: 3, of which 3 were waited for; matrix products, arithmetic and copies ran while one was open for 1% of the time, Pallas kernels for 5%

profile of v7, /device:TPU:0, one launch (start us, length us, event | category | flops | bytes accessed | tf_op | source)
XLA Modules:
  0.0 92.0 jit_solution(3892313564498857873)
XLA Ops:
  0.6 0.5 collective-permute-start
  1.1 1.0 %pad_maximum_fusion.fields = f32[6,1,64,128]{3,2,1,0:T(8,128)S(1)} fusion(f32[3,1,64,128]{3,2,1,0:T(8,128)} %param.16, f32[3,1,64,128]{3,2,1,0:T(8,128)} %param.15), kind=kLoop, calls=%fused_computation | loop fusion | flops 49152 | bytes 393216 | tf_op jit(solution)/shard_map/concatenate | solution.py:1084
  2.1 0.2 collective-permute-done.other
  2.3 0.7 shard_map.183
  3.0 7.3 %all-to-all-start = ((f32[8,15,4,128]{3,2,1,0:T(4,128)}), f32[8,15,4,128]{3,2,1,0:T(4,128)S(1)}, u32[]{:S(2)}, u32[]{:S(2)}) async-start(f32[8,15,4,128]{3,2,1,0:T(4,128)} %shard_map.183), calls=%async_computation | async-start | bytes 491520 | tf_op jit(solution)/shard_map/all_to_all | solution.py:1089
  10.4 0.6 copy-done.11
  11.0 0.0 copy-done.12
  11.0 4.1 %shard_map.184 = (bf16[288,496]{1,0:T(8,128)(2,1)S(1)}, bf16[320,432]{1,0:T(8,128)(2,1)S(1)}, bf16[320,432]{1,0:T(8,128)(2,1)S(1)}, bf16[288,496]{1,0:T(8,128)(2,1)S(1)}, bf16[384,128]{1,0:T(8,128)(2,1)S(1)}) custom-call(f32[27,3,16]{2,1,0:T(4,128)S(1)} %bitcast.17, f32[54,3,16]{2,1,0:T(4,128)S(1)} %bitcast.16, f32[1,16]{1,0:T(1,128)S(1)} %bitcast.18, ...), custom_call_target="tpu_custom_call" | custom-call | flops 1 | bytes 1 | tf_op jit(solution)/shard_map/pallas_call | solution.py:444
  15.1 4.2 %all-to-all-done.recv = f32[8,15,4,128]{3,2,1,0:T(4,128)S(1)} async-done(((f32[8,15,4,128]{3,2,1,0:T(4,128)}), f32[8,15,4,128]{3,2,1,0:T(4,128)S(1)}, u32[]{:S(2)}, u32[]{:S(2)}) %all-to-all-start) | async-done | bytes 245792 | tf_op jit(solution)/shard_map/all_to_all | solution.py:1089
  19.3 2.0 %shard_map.185 = (f32[16,24,128]{2,1,0:T(8,128)S(1)}, f32[8,48,128]{2,1,0:T(8,128)S(1)}, f32[160,1024]{1,0:T(8,128)S(1)}, f32[48,1024]{1,0:T(8,128)S(1)}, bf16[2...) custom-call(f32[8,15,4,128]{3,2,1,0:T(4,128)S(1)} %all-to-all-done.recv, ...), custom_call_target="tpu_custom_call" | custom-call | tf_op jit(solution)/shard_map/pallas_call | solution.py:444
  21.3 0.0 copy-start.8
  21.3 12.5 %all_to_all.30.recv = f32[16,24,128]{2,1,0:T(8,128)S(1)} all-to-all(f32[16,24,128]{2,1,0:T(8,128)S(1)} %get-tuple-element.29), channel_id=1, replica_groups=mesh['groups'=2,'px'=8,'py'=2] {'px','py'}, dimensions={0} | all-to-all | bytes 393216 | tf_op jit(solution)/shard_map/all_to_all | solution.py:1135
  33.8 0.7 shard_map.186
  34.5 12.8 %all_to_all.31.recv = f32[16,32,128]{2,1,0:T(8,128)S(1)} all-to-all(f32[16,32,128]{2,1,0:T(8,128)S(1)} %shard_map.186), channel_id=1, replica_groups=mesh['groups'=2,'px'=8,'py'=2] {'px','py'}, dimensions={0} | all-to-all | bytes 524288 | tf_op jit(solution)/shard_map/all_to_all | solution.py:1137
  47.3 4.6 %shard_map.187 = (f32[16,9,2,128]{3,2,1,0:T(2,128)S(1)}, f32[288,496]{1,0:T(8,128)S(1)}) custom-call(f32[16,32,128]{2,1,0:T(8,128)S(1)} %all_to_all.31.recv, bf16[320,432]{1,0:T(8,128)(2,1)S(1)} %get-tuple-element.26.fwd1, bf16[288,496]{1,0:T(8,128)(2,1)S(1)} %get-tuple-element.27.fwd2, bf16[320,432]{1,0:T(8,128)(2,1)S(1)} %get-tuple-element.30.back2, ...), custom_call_target="tpu_custom_call" | custom-call | tf_op jit(solution)/shard_map/pallas_call | solution.py:444
  52.0 11.1 %all_to_all.32.recv = f32[16,9,2,128]{3,2,1,0:T(2,128)S(1)} all-to-all(f32[16,9,2,128]{3,2,1,0:T(2,128)S(1)} %get-tuple-element.32), channel_id=1, replica_groups=mesh['groups'=2,'px'=8,'py'=2] {'px','py'}, dimensions={0} | all-to-all | bytes 294912 | tf_op jit(solution)/shard_map/all_to_all | solution.py:1155
  63.1 0.8 shard_map.188
  64.0 10.0 %all_to_all.33.recv = f32[16,3,4,128]{3,2,1,0:T(4,128)S(1)} all-to-all(f32[16,3,4,128]{3,2,1,0:T(4,128)S(1)} %shard_map.188), channel_id=1, replica_groups=mesh['groups'=2,'px'=8,'py'=2] {'px','py'}, dimensions={0} | all-to-all | bytes 196608 | tf_op jit(solution)/shard_map/all_to_all | solution.py:1162
  74.0 3.5 %shard_map.189 = f32[8,17,4,128]{3,2,1,0:T(4,128)S(1)} custom-call(f32[16,3,4,128]{3,2,1,0:T(4,128)S(1)} %all_to_all.33.recv, f32[8,48,128]{2,1,0:T(8,128)S(1)} %get-tuple-element.33.field, f32[160,1024]{1,0:T(8,128)S(1)} %get-tuple-element.34.hidden, f32[48,1024]{1,0:T(8,128)S(1)} %get-tuple-element.35.weights, ...), custom_call_target="tpu_custom_call" | custom-call | tf_op jit(solution)/shard_map/pallas_call | solution.py:444
  77.5 12.3 %all_to_all.34.recv = f32[8,17,4,128]{3,2,1,0:T(4,128)S(1)} all-to-all(f32[8,17,4,128]{3,2,1,0:T(4,128)S(1)} %shard_map.189), channel_id=1, replica_groups=mesh['groups'=2,'px'=8,'py'=2] {'px'}, dimensions={0} | all-to-all | bytes 557056 | tf_op jit(solution)/shard_map/all_to_all | solution.py:1180
  89.8 0.1 shard_map.190
  89.9 0.1 collective-permute-start.1
  89.9 1.2 %collective-permute-done.1.other = f32[56,128]{1,0:T(8,128)S(1)} collective-permute-done((f32[56,128]{1,0:T(8,128)S(1)}, f32[56,128]{1,0:T(8,128)S(1)}, u32[]{:S(2)}, u32[]{:S(2)}) %collective-permute-start.1) | collective-permute-done | bytes 28704 | tf_op jit(solution)/shard_map/ppermute | solution.py:1184
  91.1 0.9 shard_map.191
  (24 shorter events, 0.1 us)
Async XLA Ops:
  0.6 1.7 %collective-permute-start = (f32[3,1,64,128]{3,2,1,0:T(8,128)}, f32[3,1,64,128]{3,2,1,0:T(8,128)S(1)}, u32[]{:S(2)}, u32[]{:S(2)}) collective-permute-start(f32[3,1,64,128]{3,2,1,0:T(8,128)} %param.15), channel_id=1, source_target_pairs={{0,1},{1,0},{2,3},{3,2},{4,5},{5,4},{6,7},{7,6},{8,9},{9,8},{10,11... | collective-permute-start | bytes 294920 | tf_op jit(solution)/shard_map/ppermute | solution.py:1083
  3.0 7.3 %copy-start.5 = (f32[6,16,3,3,3]{1,4,3,2,0:T(4,128)S(1)}, f32[6,16,3,3,3]{1,4,3,2,0:T(4,128)}, u32[]{:S(2)}) copy-start(f32[6,16,3,3,3]{1,4,3,2,0:T(4,128)} %param.19) | copy-start | bytes 31108
  3.0 7.3 %copy-start.6 = (bf16[384,128]{1,0:T(8,128)(2,1)S(1)}, bf16[384,128]{1,0:T(8,128)(2,1)}, u32[]{:S(2)}) copy-start(bf16[384,128]{1,0:T(8,128)(2,1)} %constant.18.clone.z_in) | copy-start | bytes 294916
  3.0 7.3 %copy-start.9 = (f32[16,3,3,3,3]{0,4,3,2,1:T(4,128)S(1)}, f32[16,3,3,3,3]{0,4,3,2,1:T(4,128)}, u32[]{:S(2)}) copy-start(f32[16,3,3,3,3]{0,4,3,2,1:T(4,128)} %param.17) | copy-start | bytes 15556
  3.0 16.3 %all-to-all-start = ((f32[8,15,4,128]{3,2,1,0:T(4,128)}), f32[8,15,4,128]{3,2,1,0:T(4,128)S(1)}, u32[]{:S(2)}, u32[]{:S(2)}) async-start(f32[8,15,4,128]{3,2,1,0:T(4,128)} %shard_map.183), calls=%async_computation | async-start | bytes 491520 | tf_op jit(solution)/shard_map/all_to_all | solution.py:1089
  10.3 0.7 copy-start.11
  10.3 0.7 copy-start.12
  21.3 12.5 %copy-start.4 = (bf16[192,384]{1,0:T(8,128)(2,1)S(1)}, bf16[192,384]{1,0:T(8,128)(2,1)}, u32[]{:S(2)}) copy-start(bf16[192,384]{1,0:T(8,128)(2,1)} %constant.20.clone.table_out) | copy-start | bytes 442372
  21.3 12.5 %copy-start.8 = (bf16[128,384]{1,0:T(8,128)(2,1)S(1)}, bf16[128,384]{1,0:T(8,128)(2,1)}, u32[]{:S(2)}) copy-start(bf16[128,384]{1,0:T(8,128)(2,1)} %constant.19.clone.table_in) | copy-start | bytes 294916
  34.5 12.8 %copy-start.2 = (bf16[384,128]{1,0:T(8,128)(2,1)S(1)}, bf16[384,128]{1,0:T(8,128)(2,1)}, u32[]{:S(2)}) copy-start(bf16[384,128]{1,0:T(8,128)(2,1)} %constant.21.clone.from_z) | copy-start | bytes 294916
  47.3 15.8 %copy-start.3 = (bf16[256,288]{1,0:T(8,128)(2,1)S(1)}, bf16[256,288]{1,0:T(8,128)(2,1)}, u32[]{:S(2)}) copy-start(bf16[256,288]{1,0:T(8,128)(2,1)} %constant.22.clone.table_in) | copy-start | bytes 442372
  47.3 15.8 %copy-start.7 = (bf16[128,384]{1,0:T(8,128)(2,1)S(1)}, bf16[128,384]{1,0:T(8,128)(2,1)}, u32[]{:S(2)}) copy-start(bf16[128,384]{1,0:T(8,128)(2,1)} %constant.23.clone.table_out) | copy-start | bytes 294916
  47.3 26.6 %copy-start.1 = (bf16[1536,256]{1,0:T(8,128)(2,1)S(1)}, bf16[1536,256]{1,0:T(8,128)(2,1)}, u32[]{:S(2)}) copy-start(bf16[1536,256]{1,0:T(8,128)(2,1)} %constant.26.clone.lift) | copy-start | bytes 2359300
  52.0 22.0 %copy-start = (bf16[3,288,496]{2,1,0:T(8,128)(2,1)S(1)}, bf16[3,288,496]{2,1,0:T(8,128)(2,1)}, u32[]{:S(2)}) copy-start(bf16[3,288,496]{2,1,0:T(8,128)(2,1)} %constant.25.clone.mask) | copy-start | bytes 2571268
  63.9 10.0 %copy-start.10 = (bf16[32,576]{1,0:T(8,128)(2,1)S(1)}, bf16[32,576]{1,0:T(8,128)(2,1)}, u32[]{:S(2)}) copy-start(bf16[32,576]{1,0:T(8,128)(2,1)} %constant.24.clone.spread_t) | copy-start | bytes 110596
  89.9 1.3 %collective-permute-start.1 = (f32[56,128]{1,0:T(8,128)S(1)}, f32[56,128]{1,0:T(8,128)S(1)}, u32[]{:S(2)}, u32[]{:S(2)}) collective-permute-start(f32[56,128]{1,0:T(8,128)S(1)} %get-tuple-element.41.edge), channel_id=1, source_target_pairs={{0,1},{1,0},{2,3},{3,2},{4,5},{5,4},{6,7},{7,6},{8,9},{9,8},{10,11... | collective-permute-start | bytes 86024 | tf_op jit(solution)/shard_map/ppermute | solution.py:1184

commit v8 on v7

--- a/solution.py
+++ b/solution.py
@@ -938,13 +938,13 @@
             field[x, first + RIM + SLAB : first + REACH, :] = value[32 + 2 * m : 34 + 2 * m]
         field[x, 36:37, :] = jnp.ones((1, DEPTH), jnp.float32)
         field[x, 37:48, :] = jnp.zeros((11, DEPTH), jnp.float32)
+    network(field, fwd1, fwd2, hidden, weights, u_taps, h_hi, h_lo, work)
     for k in range(PLANES):
         grad[k] = gather_modes(recv, 1, k, 0, 24)
     flat = dot(widened(grad[...].reshape(PLANES * 24, DEPTH)), back_z)
     flat = flat.reshape(PLANES, 24, DEPTH)
     for x, value in enumerate(from_modes([flat[k] for k in range(PLANES)])):
         grad[x] = value
-    network(field, fwd1, fwd2, hidden, weights, u_taps, h_hi, h_lo, work)
 
     def middle():
         sums[0:144, :] = kernel_sums(l_taps, h_hi, h_lo, 1)

time: 92.5 us -> 92.6 us (level)
  no operation moved by 1% of the time
where the time goes in v8:
time: 92.6 us; the launch traced here: 92.1 us
  blocking collectives  58.7 us (63%)
  Pallas kernels  17.5 us (19%)
  starting transfers between devices  7.88 us (9%)
  waiting for transfers between devices  5.51 us (6%)
  other arithmetic  0.95 us (1%)
    all_to_all x2, blocking collectives, slab_device(): moved_modes = lax.all_to_all(sent, both, 0, 0)  23.6 us
    all_to_all x2, blocking collectives, slab_device(): moved_modes = lax.all_to_all(moved_modes, both, 0, 0)  22.8 us
    pallas_call x10, Pallas kernels, call(): pl.pallas_call(kernel, out_shape=outs, in_specs=[pl.BlockSpec(memory_spac...  17.5 us
    all_to_all x1, blocking collectives, slab_device(): recv = lax.all_to_all(sent, 'px', 0, 0)  12.3 us
    all_to_all x1, starting transfers between devices, slab_device(): recv = lax.all_to_all(packed, 'px', 0, 0)  7.29 us
    all_to_all x1, waiting for transfers between devices, slab_device(): recv = lax.all_to_all(packed, 'px', 0, 0)  4.17 us
  transfers between devices with their start and end apart: 3, of which 3 were waited for; matrix products, arithmetic and copies ran while one was open for 1% of the time, Pallas kernels for 5%

profile of v8, /device:TPU:0, one launch (start us, length us, event | category | flops | bytes accessed | tf_op | source)
XLA Modules:
  0.0 92.1 jit_solution(4440929936761693995)
XLA Ops:
  0.6 0.5 collective-permute-start
  1.1 1.0 %pad_maximum_fusion.fields = f32[6,1,64,128]{3,2,1,0:T(8,128)S(1)} fusion(f32[3,1,64,128]{3,2,1,0:T(8,128)} %param.16, f32[3,1,64,128]{3,2,1,0:T(8,128)} %param.15), kind=kLoop, calls=%fused_computation | loop fusion | flops 49152 | bytes 393216 | tf_op jit(solution)/shard_map/concatenate | solution.py:1084
  2.1 0.2 collective-permute-done.other
  2.3 0.7 shard_map.183
  3.0 7.3 %all-to-all-start = ((f32[8,15,4,128]{3,2,1,0:T(4,128)}), f32[8,15,4,128]{3,2,1,0:T(4,128)S(1)}, u32[]{:S(2)}, u32[]{:S(2)}) async-start(f32[8,15,4,128]{3,2,1,0:T(4,128)} %shard_map.183), calls=%async_computation | async-start | bytes 491520 | tf_op jit(solution)/shard_map/all_to_all | solution.py:1089
  10.4 0.6 copy-done.11
  11.0 0.0 copy-done.12
  11.0 4.1 %shard_map.184 = (bf16[288,496]{1,0:T(8,128)(2,1)S(1)}, bf16[320,432]{1,0:T(8,128)(2,1)S(1)}, bf16[320,432]{1,0:T(8,128)(2,1)S(1)}, bf16[288,496]{1,0:T(8,128)(2,1)S(1)}, bf16[384,128]{1,0:T(8,128)(2,1)S(1)}) custom-call(f32[27,3,16]{2,1,0:T(4,128)S(1)} %bitcast.17, f32[54,3,16]{2,1,0:T(4,128)S(1)} %bitcast.16, f32[1,16]{1,0:T(1,128)S(1)} %bitcast.18, ...), custom_call_target="tpu_custom_call" | custom-call | flops 1 | bytes 1 | tf_op jit(solution)/shard_map/pallas_call | solution.py:444
  15.1 4.2 %all-to-all-done.recv = f32[8,15,4,128]{3,2,1,0:T(4,128)S(1)} async-done(((f32[8,15,4,128]{3,2,1,0:T(4,128)}), f32[8,15,4,128]{3,2,1,0:T(4,128)S(1)}, u32[]{:S(2)}, u32[]{:S(2)}) %all-to-all-start) | async-done | bytes 245792 | tf_op jit(solution)/shard_map/all_to_all | solution.py:1089
  19.3 2.0 %shard_map.185 = (f32[16,24,128]{2,1,0:T(8,128)S(1)}, f32[8,48,128]{2,1,0:T(8,128)S(1)}, f32[160,1024]{1,0:T(8,128)S(1)}, f32[48,1024]{1,0:T(8,128)S(1)}, bf16[2...) custom-call(f32[8,15,4,128]{3,2,1,0:T(4,128)S(1)} %all-to-all-done.recv, ...), custom_call_target="tpu_custom_call" | custom-call | tf_op jit(solution)/shard_map/pallas_call | solution.py:444
  21.3 0.0 copy-start.4
  21.3 12.5 %all_to_all.30.recv = f32[16,24,128]{2,1,0:T(8,128)S(1)} all-to-all(f32[16,24,128]{2,1,0:T(8,128)S(1)} %get-tuple-element.29), channel_id=1, replica_groups=mesh['groups'=2,'px'=8,'py'=2] {'px','py'}, dimensions={0} | all-to-all | bytes 393216 | tf_op jit(solution)/shard_map/all_to_all | solution.py:1135
  33.8 0.7 shard_map.186
  34.5 12.8 %all_to_all.31.recv = f32[16,32,128]{2,1,0:T(8,128)S(1)} all-to-all(f32[16,32,128]{2,1,0:T(8,128)S(1)} %shard_map.186), channel_id=1, replica_groups=mesh['groups'=2,'px'=8,'py'=2] {'px','py'}, dimensions={0} | all-to-all | bytes 524288 | tf_op jit(solution)/shard_map/all_to_all | solution.py:1137
  47.3 4.7 %shard_map.187 = (f32[16,9,2,128]{3,2,1,0:T(2,128)S(1)}, f32[288,496]{1,0:T(8,128)S(1)}) custom-call(f32[16,32,128]{2,1,0:T(8,128)S(1)} %all_to_all.31.recv, bf16[320,432]{1,0:T(8,128)(2,1)S(1)} %get-tuple-element.26.fwd1, bf16[288,496]{1,0:T(8,128)(2,1)S(1)} %get-tuple-element.27.fwd2, bf16[320,432]{1,0:T(8,128)(2,1)S(1)} %get-tuple-element.30.back2, ...), custom_call_target="tpu_custom_call" | custom-call | tf_op jit(solution)/shard_map/pallas_call | solution.py:444
  52.1 11.1 %all_to_all.32.recv = f32[16,9,2,128]{3,2,1,0:T(2,128)S(1)} all-to-all(f32[16,9,2,128]{3,2,1,0:T(2,128)S(1)} %get-tuple-element.32), channel_id=1, replica_groups=mesh['groups'=2,'px'=8,'py'=2] {'px','py'}, dimensions={0} | all-to-all | bytes 294912 | tf_op jit(solution)/shard_map/all_to_all | solution.py:1155
  63.2 0.8 shard_map.188
  64.0 10.0 %all_to_all.33.recv = f32[16,3,4,128]{3,2,1,0:T(4,128)S(1)} all-to-all(f32[16,3,4,128]{3,2,1,0:T(4,128)S(1)} %shard_map.188), channel_id=1, replica_groups=mesh['groups'=2,'px'=8,'py'=2] {'px','py'}, dimensions={0} | all-to-all | bytes 196608 | tf_op jit(solution)/shard_map/all_to_all | solution.py:1162
  74.0 3.5 %shard_map.189 = f32[8,17,4,128]{3,2,1,0:T(4,128)S(1)} custom-call(f32[16,3,4,128]{3,2,1,0:T(4,128)S(1)} %all_to_all.33.recv, f32[8,48,128]{2,1,0:T(8,128)S(1)} %get-tuple-element.33.field, f32[160,1024]{1,0:T(8,128)S(1)} %get-tuple-element.34.hidden, f32[48,1024]{1,0:T(8,128)S(1)} %get-tuple-element.35.weights, ...), custom_call_target="tpu_custom_call" | custom-call | tf_op jit(solution)/shard_map/pallas_call | solution.py:444
  77.5 12.3 %all_to_all.34.recv = f32[8,17,4,128]{3,2,1,0:T(4,128)S(1)} all-to-all(f32[8,17,4,128]{3,2,1,0:T(4,128)S(1)} %shard_map.189), channel_id=1, replica_groups=mesh['groups'=2,'px'=8,'py'=2] {'px'}, dimensions={0} | all-to-all | bytes 557056 | tf_op jit(solution)/shard_map/all_to_all | solution.py:1180
  89.9 0.1 shard_map.190
  90.0 0.1 collective-permute-start.1
  90.0 1.2 %collective-permute-done.1.other = f32[56,128]{1,0:T(8,128)S(1)} collective-permute-done((f32[56,128]{1,0:T(8,128)S(1)}, f32[56,128]{1,0:T(8,128)S(1)}, u32[]{:S(2)}, u32[]{:S(2)}) %collective-permute-start.1) | collective-permute-done | bytes 28704 | tf_op jit(solution)/shard_map/ppermute | solution.py:1184
  91.2 0.9 shard_map.191
  (24 shorter events, 0.1 us)
Async XLA Ops:
  0.6 1.7 %collective-permute-start = (f32[3,1,64,128]{3,2,1,0:T(8,128)}, f32[3,1,64,128]{3,2,1,0:T(8,128)S(1)}, u32[]{:S(2)}, u32[]{:S(2)}) collective-permute-start(f32[3,1,64,128]{3,2,1,0:T(8,128)} %param.15), channel_id=1, source_target_pairs={{0,1},{1,0},{2,3},{3,2},{4,5},{5,4},{6,7},{7,6},{8,9},{9,8},{10,11... | collective-permute-start | bytes 294920 | tf_op jit(solution)/shard_map/ppermute | solution.py:1083
  3.0 7.3 %copy-start.5 = (f32[6,16,3,3,3]{1,4,3,2,0:T(4,128)S(1)}, f32[6,16,3,3,3]{1,4,3,2,0:T(4,128)}, u32[]{:S(2)}) copy-start(f32[6,16,3,3,3]{1,4,3,2,0:T(4,128)} %param.19) | copy-start | bytes 31108
  3.0 7.3 %copy-start.6 = (bf16[384,128]{1,0:T(8,128)(2,1)S(1)}, bf16[384,128]{1,0:T(8,128)(2,1)}, u32[]{:S(2)}) copy-start(bf16[384,128]{1,0:T(8,128)(2,1)} %constant.18.clone.z_in) | copy-start | bytes 294916
  3.0 7.3 %copy-start.9 = (f32[16,3,3,3,3]{0,4,3,2,1:T(4,128)S(1)}, f32[16,3,3,3,3]{0,4,3,2,1:T(4,128)}, u32[]{:S(2)}) copy-start(f32[16,3,3,3,3]{0,4,3,2,1:T(4,128)} %param.17) | copy-start | bytes 15556
  3.0 16.3 %all-to-all-start = ((f32[8,15,4,128]{3,2,1,0:T(4,128)}), f32[8,15,4,128]{3,2,1,0:T(4,128)S(1)}, u32[]{:S(2)}, u32[]{:S(2)}) async-start(f32[8,15,4,128]{3,2,1,0:T(4,128)} %shard_map.183), calls=%async_computation | async-start | bytes 491520 | tf_op jit(solution)/shard_map/all_to_all | solution.py:1089
  10.3 0.7 copy-start.11
  10.3 0.7 copy-start.12
  21.3 12.5 %copy-start.4 = (bf16[192,384]{1,0:T(8,128)(2,1)S(1)}, bf16[192,384]{1,0:T(8,128)(2,1)}, u32[]{:S(2)}) copy-start(bf16[192,384]{1,0:T(8,128)(2,1)} %constant.20.clone.table_out) | copy-start | bytes 442372
  21.3 12.5 %copy-start.8 = (bf16[128,384]{1,0:T(8,128)(2,1)S(1)}, bf16[128,384]{1,0:T(8,128)(2,1)}, u32[]{:S(2)}) copy-start(bf16[128,384]{1,0:T(8,128)(2,1)} %constant.19.clone.table_in) | copy-start | bytes 294916
  34.5 12.8 %copy-start.2 = (bf16[384,128]{1,0:T(8,128)(2,1)S(1)}, bf16[384,128]{1,0:T(8,128)(2,1)}, u32[]{:S(2)}) copy-start(bf16[384,128]{1,0:T(8,128)(2,1)} %constant.21.clone.from_z) | copy-start | bytes 294916
  47.3 15.9 %copy-start.3 = (bf16[256,288]{1,0:T(8,128)(2,1)S(1)}, bf16[256,288]{1,0:T(8,128)(2,1)}, u32[]{:S(2)}) copy-start(bf16[256,288]{1,0:T(8,128)(2,1)} %constant.22.clone.table_in) | copy-start | bytes 442372
  47.3 15.9 %copy-start.7 = (bf16[128,384]{1,0:T(8,128)(2,1)S(1)}, bf16[128,384]{1,0:T(8,128)(2,1)}, u32[]{:S(2)}) copy-start(bf16[128,384]{1,0:T(8,128)(2,1)} %constant.23.clone.table_out) | copy-start | bytes 294916
  47.3 26.7 %copy-start.1 = (bf16[1536,256]{1,0:T(8,128)(2,1)S(1)}, bf16[1536,256]{1,0:T(8,128)(2,1)}, u32[]{:S(2)}) copy-start(bf16[1536,256]{1,0:T(8,128)(2,1)} %constant.26.clone.lift) | copy-start | bytes 2359300
  52.1 22.0 %copy-start = (bf16[3,288,496]{2,1,0:T(8,128)(2,1)S(1)}, bf16[3,288,496]{2,1,0:T(8,128)(2,1)}, u32[]{:S(2)}) copy-start(bf16[3,288,496]{2,1,0:T(8,128)(2,1)} %constant.25.clone.mask) | copy-start | bytes 2571268
  64.0 10.0 %copy-start.10 = (bf16[32,576]{1,0:T(8,128)(2,1)S(1)}, bf16[32,576]{1,0:T(8,128)(2,1)}, u32[]{:S(2)}) copy-start(bf16[32,576]{1,0:T(8,128)(2,1)} %constant.24.clone.spread_t) | copy-start | bytes 110596
  90.0 1.3 %collective-permute-start.1 = (f32[56,128]{1,0:T(8,128)S(1)}, f32[56,128]{1,0:T(8,128)S(1)}, u32[]{:S(2)}, u32[]{:S(2)}) collective-permute-start(f32[56,128]{1,0:T(8,128)S(1)} %get-tuple-element.41.edge), channel_id=1, source_target_pairs={{0,1},{1,0},{2,3},{3,2},{4,5},{5,4},{6,7},{7,6},{8,9},{9,8},{10,11... | collective-permute-start | bytes 86024 | tf_op jit(solution)/shard_map/ppermute | solution.py:1184
